TPU v7x, 128 devices: a whole 4x4x4 slice. The times are simulated.
128 devices in a mesh: row: 8 (over x, core), col: 16 (over z, y).
Axes of the slice: x: 4, y: 4, z: 4, core: 2. Of those that a mesh axis runs over, the one named last changes fastest.
Arguments:
- tile_weight: bfloat16 [128, 128, 2, 128, 128], P(('row', 'col')), may hold values from 0.049804688 to 1
- tile_angle: bfloat16 [128, 128, 2, 128, 128], P(('row', 'col')), may hold values from -3.140625 to 3.140625
- tile_list: int32 [128, 128, 2, 2], P(('row', 'col')), may hold values from 0 to 255, as said below
- tile_count: int32 [128, 128], P(('row', 'col')), may hold values from 0 to 2, as said below
- init_basis: float32 [2, 32, 32768], P(None, None, ('row', 'col')), may hold values from -6 to 6
Outputs:
- basis: float32 [2, 32, 32768], P(None, None, ('row', 'col'))
Inputs may be any that keep to these rules, and one draw needn't show every extreme that they name: `tile_list`: let piece(b) = b // 2 for a block b, and number devices s = a * 16 + e' along row+col. For device s = a * 16 + b' and destination d = f * 16 + e, slot [s, d, k] holds I with piece(I) = a * 16 + e and J with piece(J) = f * 16 + b'. The slots of one s, d hold distinct tiles; for d = s they hold the diagonal tiles (I, I) of the first 2 blocks of the device's piece. tile_count[s, s] = 2, and one destination has 2 live slots from every device.
All inputs are finite; a program needn't handle non-finite values.
Results may differ from a plain program's by a relative error of at most 0.0053.
Values may be sent and summed in bfloat16 or wider, within the bound.
No kernel may reach another device: no remote copies, remote signals or barrier semaphores. Data moves between devices by JAX's collectives and lax.ppermute only.
A program may use at most 256 MiB of HBM per device.

v0:
```python
import jax
import jax.numpy as jnp
from jax import lax
from jax.sharding import PartitionSpec as P

ITERS = 3


def complex_tiles(weight, angle):
    weight_f = weight.astype(jnp.float32)
    angle_f = angle.astype(jnp.float32)
    return (
        (weight_f * jnp.cos(angle_f)).astype(jnp.bfloat16),
        (weight_f * jnp.sin(angle_f)).astype(jnp.bfloat16),
    )


def highest_dot(left, right):
    return jnp.dot(left, right, precision=lax.Precision.HIGHEST, preferred_element_type=jnp.float32)


def gram_terms(image_real, image_imag):
    gram_real = highest_dot(image_real, image_real.T) + highest_dot(image_imag, image_imag.T)
    gram_imag = highest_dot(image_real, image_imag.T) - highest_dot(image_imag, image_real.T)
    return (gram_real, gram_imag)


def orthonormal(gram_real, gram_imag, image_real, image_imag):
    width = gram_real.shape[0]
    indices = jnp.arange(width)
    ridge = 0.01 * jnp.trace(gram_real) / width + 1e-06
    gram_real = gram_real + ridge * jnp.eye(width, dtype=jnp.float32)
    lower_real = jnp.zeros((width, width), jnp.float32)
    lower_imag = jnp.zeros((width, width), jnp.float32)
    for column in range(width):
        prod_real = highest_dot(lower_real, lower_real[column]) + highest_dot(
            lower_imag, lower_imag[column]
        )
        prod_imag = highest_dot(lower_imag, lower_real[column]) - highest_dot(
            lower_real, lower_imag[column]
        )
        pivot = jnp.sqrt(gram_real[column, column] - prod_real[column])
        below = indices > column
        col_real = (gram_real[:, column] - prod_real) / pivot
        col_imag = (gram_imag[:, column] - prod_imag) / pivot
        lower_real = lower_real.at[:, column].set(
            jnp.where(below, col_real, jnp.where(indices == column, pivot, 0.0))
        )
        lower_imag = lower_imag.at[:, column].set(jnp.where(below, col_imag, 0.0))
    inv_real = jnp.zeros((width, width), jnp.float32)
    inv_imag = jnp.zeros((width, width), jnp.float32)
    for column in range(width):
        unit = (indices == column).astype(jnp.float32)
        sum_real = highest_dot(lower_real[column], inv_real) - highest_dot(
            lower_imag[column], inv_imag
        )
        sum_imag = highest_dot(lower_real[column], inv_imag) + highest_dot(
            lower_imag[column], inv_real
        )
        diag_value = lower_real[column, column]
        inv_real = inv_real.at[column].set((unit - sum_real) / diag_value)
        inv_imag = inv_imag.at[column].set(-sum_imag / diag_value)
    new_real = highest_dot(inv_real, image_real) + highest_dot(inv_imag, image_imag)
    new_imag = highest_dot(inv_real, image_imag) - highest_dot(inv_imag, image_real)
    return jnp.stack([new_real, new_imag], 0)


def one_hot(position, count, values):
    return (position[:, None] == jnp.arange(count)[None, :]).astype(jnp.float32) * values[:, None]


def place_rows(hot_table, sums):
    return jnp.einsum("ng,ni->gi", hot_table, sums, precision=lax.Precision.HIGHEST)


def to_blocks(gathered, tile):
    parts, width, length = gathered.shape
    return jnp.transpose(gathered.reshape(parts, width, length // tile, tile), (2, 0, 1, 3))


def forward_terms(real_part, imag_part, taken, hot_table):
    first = jnp.einsum("nskj,nij->nski", taken, real_part, preferred_element_type=jnp.float32)
    second = jnp.einsum("nskj,nij->nski", taken, imag_part, preferred_element_type=jnp.float32)
    terms = jnp.stack([first[:, 0] - second[:, 1], first[:, 1] + second[:, 0]], 1)
    return jnp.einsum("ng,nski->skgi", hot_table, terms, precision=lax.Precision.HIGHEST)


def mirror_terms(real_part, imag_part, taken, hot_table):
    first = jnp.einsum("chqr,crg->chqg", taken, real_part, preferred_element_type=jnp.float32)
    second = jnp.einsum("chqr,crg->chqg", taken, imag_part, preferred_element_type=jnp.float32)
    terms = jnp.stack([first[:, 0] + second[:, 1], first[:, 1] - second[:, 0]], 1)
    return jnp.einsum("ng,nski->skgi", hot_table, terms, precision=lax.Precision.HIGHEST)


def shards(tile_weight, tile_angle, tile_list, tile_count, init_basis):
    rows_axis = lax.axis_size("row")
    cols_axis = lax.axis_size("col")
    row_place = lax.axis_index("row")
    devices = rows_axis * cols_axis
    tile = tile_weight.shape[-1]
    pair_cap = tile_weight.shape[2]
    width = init_basis.shape[2]
    columns = init_basis.shape[1]
    per_device = width // tile
    group_rows = cols_axis * per_device
    slot_count = devices * pair_cap
    images_all = width * devices
    weights = tile_weight.reshape(slot_count, tile, tile)
    angles = tile_angle.reshape(slot_count, tile, tile)
    listing = tile_list.reshape(slot_count, 2)
    row_global = listing[:, 0]
    col_global = listing[:, 1]
    alive = (jnp.arange(pair_cap)[None, :] < tile_count.reshape(devices, 1)).reshape(slot_count)
    halves = jnp.where(alive, 0.5, 0.0).astype(jnp.float32)
    row_local = row_global - row_place * group_rows
    col_local = col_global // per_device // cols_axis * per_device + col_global % per_device
    real_part, imag_part = complex_tiles(weights, angles)
    row_hot = one_hot(row_local, group_rows, halves)
    degree_part = place_rows(row_hot, jnp.sum(weights, axis=2, dtype=jnp.float32))
    mirror_col = row_global // per_device // cols_axis * per_device + row_global % per_device
    mirror_row = col_global // per_device % cols_axis * per_device + col_global % per_device
    index_pairs = jnp.where(alive[:, None], jnp.stack([mirror_col, mirror_row], -1), -1)
    index_pairs = index_pairs.reshape(devices, pair_cap, 2)
    sent_weight, sent_angle = (
        lax.all_to_all(
            tile_weight.reshape(devices, pair_cap, tile, tile),
            ("row", "col"),
            split_axis=0,
            concat_axis=0,
            tiled=True,
        ),
        lax.all_to_all(
            tile_angle.reshape(devices, pair_cap, tile, tile),
            ("row", "col"),
            split_axis=0,
            concat_axis=0,
            tiled=True,
        ),
    )
    sent_index = lax.all_to_all(
        index_pairs, ("row", "col"), split_axis=0, concat_axis=0, tiled=True
    )
    recv_weight = sent_weight.reshape(slot_count, tile, tile)
    recv_angle = sent_angle.reshape(slot_count, tile, tile)
    recv_index = sent_index.reshape(slot_count, 2)
    recv_halves = jnp.where(recv_index[:, 0] >= 0, 0.5, 0.0).astype(jnp.float32)
    recv_take = jnp.maximum(recv_index[:, 0], 0)
    recv_put = jnp.maximum(recv_index[:, 1], 0)
    recv_real, recv_imag = complex_tiles(recv_weight, recv_angle)
    recv_hot = one_hot(recv_put, group_rows, recv_halves)
    degree_part = degree_part + place_rows(
        recv_hot, jnp.sum(recv_weight, axis=1, dtype=jnp.float32)
    )
    degree = lax.psum_scatter(
        degree_part.reshape(group_rows * tile), "col", scatter_dimension=0, tiled=True
    )
    scale = lax.rsqrt(degree)
    basis = init_basis
    for rounds in range(ITERS):
        scaled = (basis * scale).astype(jnp.bfloat16)
        col_blocks = to_blocks(lax.all_gather(scaled, "row", axis=2, tiled=True), tile)
        partial_value = forward_terms(real_part, imag_part, col_blocks[col_local], row_hot)
        partial_value = partial_value + mirror_terms(
            recv_real, recv_imag, col_blocks[recv_take], recv_hot
        )
        image = lax.psum_scatter(
            partial_value.reshape(2, columns, group_rows * tile),
            "col",
            scatter_dimension=2,
            tiled=True,
        )
        image = image * scale
        gram_real, gram_imag = gram_terms(image[0], image[1])
        gram_real, gram_imag = lax.psum((gram_real, gram_imag), ("row", "col"))
        basis = orthonormal(gram_real / images_all, gram_imag / images_all, image[0], image[1])
    return basis


def solution(mesh):
    placed = (
        P(("row", "col"), None, None, None, None),
        P(("row", "col"), None, None, None, None),
        P(("row", "col"), None, None, None),
        P(("row", "col"), None),
        P(None, None, ("row", "col")),
    )
    return jax.shard_map(
        shards, mesh=mesh, in_specs=placed, out_specs=P(None, None, ("row", "col")), check_vma=False
    )
```

profile of v0, /device:TPU:1, one launch (start us, length us, event | category | flops | bytes accessed | tf_op | source)
XLA Modules:
  0.0 1730.1 jit_solution(9580391009465592624)
XLA Ops:
  9.0 21.7 %all_to_all.15 = s32[128,2,2]{1,2,0:T(2,128)S(1)} all-to-all(s32[128,2,2]{1,2,0:T(2,128)S(1)} %copy.53), channel_id=1, replica_groups=mesh['row'=8,'col'=16] {'row','col'}, dimensions={0} | all-to-all | bytes 4096 | tf_op jit(solution)/shard_map/all_to_all | solution.py:140
  30.8 102.3 %all_to_all.16 = bf16[128,2,128,128]{3,2,1,0:T(8,128)(2,1)} all-to-all(bf16[128,2,128,128]{3,2,1,0:T(8,128)(2,1)} %bitcast.8314), channel_id=1, replica_groups=mesh['row'=8,'col'=16] {'row','col'}, dimensions={0} | all-to-all | bytes 16777216 | tf_op jit(solution)/shard_map/all_to_all | solution.py:132
  142.3 65.4 %fusion = (bf16[1,128,2,128,128]{4,3,2,1,0:T(8,128)(2,1)}, bf16[1,128,2,128,128]{4,3,2,1,0:T(8,128)(2,1)}, f32[128,2,128]{2,1,0:T(2,128)S(1)}) fusion(bf16[1,128,2,128,128]{4,3,2,1,0:T(8,128)(2,1)} %param.774, bf16[1,128,2,128,128]{4,3,2,1,0:T(8,128)(2,1)} %param.773), kind=kLoop, calls=%fused_computation.16 | loop fusion | flops 29327360 | bytes 33685504 | tf_op jit(solution)/shard_map/convert_element_type | solution.py:13
  208.2 34.8 %all-to-all-done.1 = bf16[128,2,128,128]{3,2,1,0:T(8,128)(2,1)} async-done(((bf16[128,2,128,128]{3,2,1,0:T(8,128)(2,1)}), bf16[128,2,128,128]{3,2,1,0:T(8,128)(2,1)}, u32[]{:S(2)}, u32[]{:S(2)}) %all-to-all-start.1) | async-done | bytes 8388640 | tf_op jit(solution)/shard_map/all_to_all | solution.py:125
  242.9 64.7 %fusion.2 = (bf16[128,2,128,128]{3,2,1,0:T(8,128)(2,1)}, bf16[128,2,128,128]{3,2,1,0:T(8,128)(2,1)}, f32[128,2,128]{2,1,0:T(2,128)S(1)}) fusion(bf16[128,2,128,128]{3,2,1,0:T(8,128)(2,1)} %all_to_all.16, bf16[128,2,128,128]{3,2,1,0:T(8,128)(2,1)} %all-to-all-done.1), kind=kLoop, calls=%fused_computation.18 | loop fusion | flops 29327360 | bytes 33685504 | tf_op jit(solution)/shard_map/convert_element_type | solution.py:13
  307.8 57.9 %all-reduce.12 = f32[4096]{0:T(1024)S(1)} all-reduce(f32[4096]{0:T(1024)S(1)} %fusion.40), channel_id=2, replica_groups=mesh['row'=8,'col'=16] {'col'}, use_global_device_ids=true, to_apply=%region_3.4.clone | all-reduce | flops 4096 | bytes 32768
  365.8 29.5 %all_gather.9 = bf16[2,32,2048]{2,1,0:T(8,128)(2,1)S(1)} all-gather(bf16[2,32,256]{2,1,0:T(8,128)(2,1)S(1)} %multiply_convert_fusion), channel_id=1, replica_groups=mesh['row'=8,'col'=16] {'row'}, dimensions={2}, use_global_device_ids=true | all-gather | bytes 294912 | tf_op jit(solution)/shard_map/all_gather | solution.py:161
  398.5 10.3 fusion.2343
  413.3 11.2 slice_add_fusion.4
  429.0 18.3 %fusion.12 = f32[2,32,128,32]{2,3,1,0:T(8,128)S(1)} fusion(f32[256,2,32,128]{3,2,1,0:T(8,128)S(1)} %pad_maximum_fusion.1, f32[256]{0:T(256)S(1)} %bitcast.8323, s32[256]{0:T(256)S(1)} %bitcast.8327), kind=kOutput, calls=%fused_computation.34 | convolution fusion | flops 805322752 | bytes 9439232 | tf_op jit(solution)/shard_map/ng,nski->skgi/dot_general | solution.py:92
  450.5 13.8 fusion.2341
  464.3 12.4 fusion.2340
  489.9 10.0 fusion.31
  522.1 45.4 %reduce-scatter.4.cloned.1.call-done = f32[2,32,256]{2,1,0:T(8,128)} async-done(((f32[2,32,4096]{2,1,0:T(8,128)}), f32[2,32,256]{2,1,0:T(8,128)}) %reduce-scatter.4.cloned.1.call-update) | async-done | bytes 65552 | tf_op jit(solution)/shard_map/reduce_scatter | solution.py:166
  569.0 66.0 %all-reduce.15 = (f32[32,32]{1,0:T(8,128)S(1)}, f32[32,32]{1,0:T(8,128)S(1)}) all-reduce(f32[32,32]{1,0:T(8,128)S(1)} %convolution_add_fusion.5, f32[32,32]{1,0:T(8,128)S(1)} %convolution_subtract_fusion.5), channel_id=1, replica_groups=mesh['row'=8,'col'=16] {'row','col'}, use_global_device_ids=true, to_apply=%region_5.6 | all-reduce | flops 2048 | bytes 16384 | tf_op jit(solution)/shard_map/psum | solution.py:174
  831.8 14.2 all_gather.10
  849.2 10.3 fusion.2347
  871.6 13.8 fusion.2345
  885.4 12.4 fusion.2344
  897.8 10.2 slice_add_fusion.2
  921.0 10.0 slice_subtract_fusion.3
  934.2 10.0 fusion.28
  945.5 67.5 %reduce-scatter.6.cloned.1.call-done = f32[2,32,256]{2,1,0:T(8,128)} async-done(((f32[2,32,4096]{2,1,0:T(8,128)}), f32[2,32,256]{2,1,0:T(8,128)}) %reduce-scatter.6.cloned.1.call-update) | async-done | bytes 65552 | tf_op jit(solution)/shard_map/reduce_scatter | solution.py:166
  1014.6 65.9 %all-reduce.14 = (f32[32,32]{1,0:T(8,128)S(1)}, f32[32,32]{1,0:T(8,128)S(1)}) all-reduce(f32[32,32]{1,0:T(8,128)S(1)} %convolution_add_fusion.4, f32[32,32]{1,0:T(8,128)S(1)} %convolution_subtract_fusion.4), channel_id=1, replica_groups=mesh['row'=8,'col'=16] {'row','col'}, use_global_device_ids=true, to_apply=%region_39.40 | all-reduce | flops 2048 | bytes 16384 | tf_op jit(solution)/shard_map/psum | solution.py:174
  1277.6 13.8 all_gather.11
  1294.5 10.3 fusion.2351
  1316.8 13.9 fusion.2349
  1330.7 12.4 fusion.2348
  1343.1 10.4 slice_add_fusion
  1366.4 10.0 slice_subtract_fusion.1
  1390.6 67.8 %reduce-scatter.8.cloned.1.call-done = f32[2,32,256]{2,1,0:T(8,128)} async-done(((f32[2,32,4096]{2,1,0:T(8,128)}), f32[2,32,256]{2,1,0:T(8,128)}) %reduce-scatter.8.cloned.1.call-update) | async-done | bytes 65552 | tf_op jit(solution)/shard_map/reduce_scatter | solution.py:166
  1459.9 66.0 %all-reduce.13 = (f32[32,32]{1,0:T(8,128)S(1)}, f32[32,32]{1,0:T(8,128)S(1)}) all-reduce(f32[32,32]{1,0:T(8,128)S(1)} %convolution_add_fusion.3, f32[32,32]{1,0:T(8,128)S(1)} %convolution_subtract_fusion.3), channel_id=1, replica_groups=mesh['row'=8,'col'=16] {'row','col'}, use_global_device_ids=true, to_apply=%region_43.44 | all-reduce | flops 2048 | bytes 16384 | tf_op jit(solution)/shard_map/psum | solution.py:174
  (1698 shorter events, 606.4 us)
Async XLA Ops:
  133.0 7.8 copy-start.7
  133.0 8.0 copy-start.8
  133.0 109.9 %all-to-all-start.1 = ((bf16[128,2,128,128]{3,2,1,0:T(8,128)(2,1)}), bf16[128,2,128,128]{3,2,1,0:T(8,128)(2,1)}, u32[]{:S(2)}, u32[]{:S(2)}) async-start(bf16[128,2,128,128]{3,2,1,0:T(8,128)(2,1)} %bitcast.8315), calls=%async_computation.1 | async-start | bytes 16777216 | tf_op jit(solution)/shard_map/all_to_all | solution.py:125
  140.8 426.7 %reduce-scatter.4.cloned.1.call-start = ((), (), s32[]{:S(2)}) async-start(), calls=%async_computation.6 | async-start | bytes 1114112 | tf_op jit(solution)/shard_map/reduce_scatter | solution.py:166
  208.2 157.7 %copy-start.6 = (f32[2,32,256]{2,1,0:T(8,128)S(1)}, f32[2,32,256]{2,1,0:T(8,128)}, u32[]{:S(2)}) copy-start(f32[2,32,256]{2,1,0:T(8,128)} %param.777) | copy-start | bytes 196612
  398.5 10.3 slice-start
  398.5 10.3 slice-start.1
  398.5 10.3 copy-start.1
  450.5 13.9 copy-start.4
  501.2 511.9 %reduce-scatter.6.cloned.1.call-start = ((), (), s32[]{:S(2)}) async-start(), calls=%async_computation.7 | async-start | bytes 1114112 | tf_op jit(solution)/shard_map/reduce_scatter | solution.py:166
  849.2 10.3 copy-start.2
  871.6 13.8 copy-start.5
  945.5 512.9 %reduce-scatter.8.cloned.1.call-start = ((), (), s32[]{:S(2)}) async-start(), calls=%async_computation.8 | async-start | bytes 1114112 | tf_op jit(solution)/shard_map/reduce_scatter | solution.py:166
  1294.5 10.3 copy-start
  1316.8 13.9 copy-start.3
Sparse Core Ops, SparseCore 0:
  501.3 66.1 reduce-scatter.3
  945.6 67.3 reduce-scatter.5
  1390.7 67.5 reduce-scatter.7
where the time goes:
time: 1740 us; the launch traced here: 1730 us
  matrix products  480 us (28%)
  blocking collectives  437 us (25%)
  other arithmetic  297 us (17%)
  waiting for transfers between devices  215 us (12%)
  local copies, waits for them, and re-layouts  152 us (9%)
  between operations  141 us (8%)
    dot_general x775, matrix products, highest_dot(): jnp.dot(left, right, precision=lax.Precision.HIGHEST, preferred_element_t...  279 us
    psum x3, blocking collectives, shards(): gram_real, gram_imag = lax.psum((gram_real, gram_imag), ('row', 'col'))  198 us
    reduce_scatter x3, waiting for transfers between devices, shards(): lax.psum_scatter(partial_value.reshape(2, columns, group_rows * tile), 'c...  181 us
    convert_element_type x2, other arithmetic, complex_tiles(): (weight_f * jnp.cos(angle_f)).astype(jnp.bfloat16)  130 us
    all_to_all x1, blocking collectives, shards(): lax.all_to_all(tile_angle.reshape(devices, pair_cap, tile, tile), ('row',...  102 us
    another operation x124, other arithmetic  78.9 us
    slice x99, local copies, waits for them, and re-layouts, orthonormal(): pivot = jnp.sqrt(gram_real[column, column] - prod_real[column])  63.3 us
    unnamed x1, blocking collectives  57.9 us
  transfers between devices with their start and end apart: 4, of which 4 were waited for; matrix products, arithmetic and copies ran while one was open for 5% of the time, Pallas kernels for 0%

commit v1 on v0

v1 whole, which is shorter than its diff:
```python
import functools

import jax
import jax.numpy as jnp
from jax import lax
from jax.experimental import pallas as pl
from jax.experimental.pallas import tpu as pltpu
from jax.sharding import PartitionSpec as P

ITERS = 3
IMAGES = 32768
TILE = 128
WIDTH = 32
SLOTS = 256
ROW_BLOCKS = 32
COL_BLOCKS = 16
CHUNK = 16
TRIG_CHUNK = 8
HALF_SIN = (0.5, -0.020833322778344154, 0.00026040783268399537, -1.5475804957532091e-06, 5.088141019626846e-09)
HALF_COS = (0.9999999403953552, -0.1249997615814209, 0.0026039734948426485, -2.164632678613998e-05, 9.044046578310372e-08)
HIGHEST = lax.Precision.HIGHEST
MIB = 1 << 20


def horner(u, coefs):
    value = coefs[-1]
    for coef in coefs[-2::-1]:
        value = value * u + coef
    return value


def lanes(shape):
    return lax.broadcasted_iota(jnp.int32, shape, 1)


def pair_swap(x):
    even = (lanes(x.shape) // WIDTH) % 2 == 0
    return jnp.where(even, -pltpu.roll(x, TILE - WIDTH, 1), pltpu.roll(x, WIDTH, 1))


def degree_kernel(rows_of, cols_of, live, w_ref, row_ref, col_ref, row_acc, col_acc):
    step = pl.program_id(0)

    @pl.when(step == 0)
    def _():
        row_acc[...] = jnp.zeros_like(row_acc)
        col_acc[...] = jnp.zeros_like(col_acc)

    for u in range(CHUNK):
        slot = step * CHUNK + u

        @pl.when(live[slot] > 0)
        def _():
            w = w_ref[u].astype(jnp.float32)
            row_acc[rows_of[slot]] += w
            col_acc[cols_of[slot]] += jnp.sum(w.reshape(TILE // 8, 8, TILE), axis=0)

    @pl.when(step == SLOTS // CHUNK - 1)
    def _():
        for p in range(ROW_BLOCKS // 2):
            sums = [jnp.sum(row_acc[2 * p + k].T, axis=0, keepdims=True) for k in range(2)]
            row_ref[p] = 0.5 * jnp.concatenate(sums * 4, axis=0)
        for p in range(COL_BLOCKS // 2):
            sums = [jnp.sum(col_acc[2 * p + k], axis=0, keepdims=True) for k in range(2)]
            col_ref[p] = 0.5 * jnp.concatenate(sums * 4, axis=0)


def degrees(rows_of, cols_of, live, weights):
    return pl.pallas_call(
        degree_kernel,
        grid_spec=pltpu.PrefetchScalarGridSpec(
            num_scalar_prefetch=3,
            grid=(SLOTS // CHUNK,),
            in_specs=[pl.BlockSpec((CHUNK, TILE, TILE), lambda c, *_: (c, 0, 0))],
            out_specs=[
                pl.BlockSpec((ROW_BLOCKS // 2, 8, TILE), lambda c, *_: (0, 0, 0)),
                pl.BlockSpec((COL_BLOCKS // 2, 8, TILE), lambda c, *_: (0, 0, 0)),
            ],
            scratch_shapes=[
                pltpu.VMEM((ROW_BLOCKS, TILE, TILE), jnp.float32),
                pltpu.VMEM((COL_BLOCKS, 8, TILE), jnp.float32),
            ],
        ),
        out_shape=[
            jax.ShapeDtypeStruct((ROW_BLOCKS // 2, 8, TILE), jnp.float32),
            jax.ShapeDtypeStruct((COL_BLOCKS // 2, 8, TILE), jnp.float32),
        ],
        compiler_params=pltpu.CompilerParams(vmem_limit_bytes=16 * MIB),
        cost_estimate=pl.CostEstimate(flops=0, bytes_accessed=18 * MIB, transcendentals=0),
        name="degrees",
    )(rows_of, cols_of, live, weights)


def tiles_kernel(order, count, *refs):
    w_refs, a_refs = refs[:TRIG_CHUNK], refs[TRIG_CHUNK : 2 * TRIG_CHUNK]
    plain_ref, turned_ref = refs[2 * TRIG_CHUNK :]
    step = pl.program_id(0)

    @pl.when(step * TRIG_CHUNK < pl.cdiv(count[0], CHUNK) * CHUNK)
    def _():
        for u in range(TRIG_CHUNK):
            half = jnp.where(step * TRIG_CHUNK + u < count[0], 0.5, 0.0).astype(jnp.float32)
            theta = a_refs[u][0].astype(jnp.float32)
            w = w_refs[u][0].astype(jnp.float32) * half
            square = theta * theta
            sine = theta * horner(square, HALF_SIN)
            cosine = horner(square, HALF_COS)
            part = (w + w) * sine
            real = w - part * sine
            imag = part * cosine
            plain_ref[u, :, :TILE] = real.astype(jnp.bfloat16)
            plain_ref[u, :, TILE:] = imag.astype(jnp.bfloat16)
            turned_ref[u, :, :TILE] = real.T.astype(jnp.bfloat16)
            turned_ref[u, :, TILE:] = imag.T.astype(jnp.bfloat16)


def complex_tiles(order, count, weights, angles):
    steps = SLOTS // TRIG_CHUNK

    def last(count):
        return pl.cdiv(count[0], CHUNK) * (CHUNK // TRIG_CHUNK) - 1

    def taken(u):
        return pl.BlockSpec(
            (1, TILE, TILE),
            lambda c, order, count: (order[jnp.minimum(c, last(count)) * TRIG_CHUNK + u], 0, 0),
        )

    out = pl.BlockSpec(
        (TRIG_CHUNK, TILE, 2 * TILE), lambda c, order, count: (jnp.minimum(c, last(count)), 0, 0)
    )
    return pl.pallas_call(
        tiles_kernel,
        grid_spec=pltpu.PrefetchScalarGridSpec(
            num_scalar_prefetch=2,
            grid=(steps,),
            in_specs=[taken(u) for u in range(TRIG_CHUNK)] * 2,
            out_specs=[out, out],
        ),
        out_shape=[jax.ShapeDtypeStruct((SLOTS, TILE, 2 * TILE), jnp.bfloat16)] * 2,
        compiler_params=pltpu.CompilerParams(vmem_limit_bytes=24 * MIB),
        cost_estimate=pl.CostEstimate(flops=0, bytes_accessed=60 * MIB, transcendentals=0),
        name="complex_tiles",
    )(order, count, *([weights] * TRIG_CHUNK), *([angles] * TRIG_CHUNK))


def product_kernel(sign, sizes, takes, puts, count, tiles_ref, *refs):
    x_refs = refs[: len(sizes)]
    out_ref, x_mat, acc = refs[len(sizes) :]
    step = pl.program_id(0)

    @pl.when(step == 0)
    def _():
        acc[...] = jnp.zeros_like(acc)
        low = lanes((TILE, TILE)) < 2 * WIDTH
        base = 0
        for x_ref, size in zip(x_refs, sizes):
            for p in range(size):
                value = x_ref[p, :TILE].astype(jnp.float32)
                high = value.astype(jnp.bfloat16).astype(jnp.float32)
                rest = value - high
                for k in range(2):
                    if k == 0:
                        top = jnp.where(low, high, pltpu.roll(rest, 2 * WIDTH, 1))
                    else:
                        top = jnp.where(low, pltpu.roll(high, 2 * WIDTH, 1), rest)
                    x_mat[base + 2 * p + k, :TILE] = top.astype(jnp.bfloat16)
                    x_mat[base + 2 * p + k, TILE:] = (sign * pair_swap(top)).astype(jnp.bfloat16)
            base += 2 * size

    @pl.when(step * CHUNK < count[0])
    def _():
        for u in range(CHUNK):
            slot = step * CHUNK + u
            acc[puts[slot]] += jnp.dot(
                tiles_ref[u], x_mat[takes[slot]], preferred_element_type=jnp.float32
            )

    @pl.when(step == SLOTS // CHUNK - 1)
    def _():
        low = lanes((TILE, TILE)) < 2 * WIDTH
        for p in range(out_ref.shape[0]):
            first, second = acc[2 * p], acc[2 * p + 1]
            out_ref[p] = jnp.where(
                low,
                first + pltpu.roll(first, 2 * WIDTH, 1),
                second + pltpu.roll(second, 2 * WIDTH, 1),
            )


def products(sign, takes, puts, count, tiles, sources, out_pieces, name):
    sizes = tuple(s.shape[0] for s in sources)

    def whole(s):
        return pl.BlockSpec(s.shape, lambda c, *_: (0, 0, 0))

    def chunk(c, takes, puts, count):
        return (jnp.minimum(c, pl.cdiv(count[0], CHUNK) - 1), 0, 0)

    return pl.pallas_call(
        functools.partial(product_kernel, sign, sizes),
        grid_spec=pltpu.PrefetchScalarGridSpec(
            num_scalar_prefetch=3,
            grid=(SLOTS // CHUNK,),
            in_specs=[pl.BlockSpec((CHUNK, TILE, 2 * TILE), chunk)] + [whole(s) for s in sources],
            out_specs=pl.BlockSpec((out_pieces, TILE, TILE), lambda c, *_: (0, 0, 0)),
            scratch_shapes=[
                pltpu.VMEM((2 * sum(sizes), 2 * TILE, TILE), jnp.bfloat16),
                pltpu.VMEM((2 * out_pieces, TILE, TILE), jnp.float32),
            ],
        ),
        out_shape=jax.ShapeDtypeStruct((out_pieces, TILE, TILE), jnp.float32),
        compiler_params=pltpu.CompilerParams(vmem_limit_bytes=24 * MIB),
        cost_estimate=pl.CostEstimate(flops=0, bytes_accessed=36 * MIB, transcendentals=0),
        name=name,
    )(takes, puts, count, tiles, *sources)


def gather_kernel(turned, n_parts, *refs):
    wide_ref, part_refs = refs[0], refs[1 : 1 + n_parts]
    scale_ref = refs[1 + n_parts]
    rest = refs[2 + n_parts :]
    total = wide_ref[0]
    for p in range(1, wide_ref.shape[0]):
        total = total + wide_ref[p]
    for ref in part_refs:
        total = total + ref[0]
    image = total * scale_ref[...]
    if turned:
        image = nt_dot(image, rest[0][...])
        rest = rest[1:]
    image_ref, gram_ref = rest
    image_ref[...] = image
    gram = lax.dot_general(image.T, image.T, (((1,), (1,)), ((), ())), precision=HIGHEST, preferred_element_type=jnp.float32)
    pairs = gram[: 2 * WIDTH] + pltpu.roll(gram[2 * WIDTH :], 2 * WIDTH, 1)
    upper, lower = pairs[:WIDTH], pairs[WIDTH:]
    even = lanes(upper.shape) < WIDTH
    other = jnp.where(even, pltpu.roll(lower, TILE - WIDTH, 1), -pltpu.roll(lower, WIDTH, 1))
    both = upper + other
    low = lanes((WIDTH // 2, TILE)) < 2 * WIDTH
    gram_ref[...] = jnp.where(
        low, both[: WIDTH // 2], pltpu.roll(both[WIDTH // 2 :], 2 * WIDTH, 1)
    )


def nt_dot(left, right):
    return lax.dot_general(
        left, right, (((1,), (1,)), ((), ())), precision=HIGHEST, preferred_element_type=jnp.float32
    )


def new_image(wide, parts, scale, turn):
    operands = [wide, *parts, scale] + ([] if turn is None else [turn])
    return pl.pallas_call(
        functools.partial(gather_kernel, turn is not None, len(parts)),
        out_shape=[
            jax.ShapeDtypeStruct((TILE, TILE), jnp.float32),
            jax.ShapeDtypeStruct((WIDTH // 2, TILE), jnp.float32),
        ],
        compiler_params=pltpu.CompilerParams(vmem_limit_bytes=16 * MIB),
        cost_estimate=pl.CostEstimate(flops=0, bytes_accessed=6 * MIB, transcendentals=0),
        name="new_image",
    )(*operands)


def turn_kernel(gram_ref, turn_ref):
    packed = gram_ref[...] * (1.0 / IMAGES)
    lane = lanes((WIDTH, TILE))
    place = lax.broadcasted_iota(jnp.int32, (WIDTH, TILE), 0)
    value = jnp.concatenate([packed, pltpu.roll(packed, 2 * WIDTH, 1)], axis=0)
    value = jnp.where(lane < 2 * WIDTH, value, 0.0)
    diagonal = lane == place
    trace = jnp.sum(jnp.where(diagonal, value, 0.0))
    ridge = 0.01 * trace / WIDTH + 1e-6
    value = value + jnp.where(diagonal, ridge, 0.0)
    value = value + jnp.where(lane == place + 2 * WIDTH, 1.0, 0.0)
    for column in range(WIDTH):
        row = value[column : column + 1]
        inverse = 1.0 / row[:, column : column + 1]
        below = lax.broadcasted_iota(jnp.int32, (WIDTH, 1), 0) > column
        real = jnp.where(below, value[:, column : column + 1] * inverse, 0.0)
        imag = jnp.where(below, value[:, WIDTH + column : WIDTH + column + 1] * inverse, 0.0)
        value = value - (real * row + imag * pair_swap(row))
    pivot = jnp.sum(jnp.where(diagonal, value, 0.0), axis=1, keepdims=True)
    value = value * lax.rsqrt(pivot)
    high = lane >= 2 * WIDTH
    second = jnp.where(high, value, 0.0)
    first = pltpu.roll(second, 2 * WIDTH, 1)
    turn_ref[0:WIDTH] = first
    turn_ref[WIDTH : 2 * WIDTH] = pair_swap(first)
    turn_ref[2 * WIDTH : 3 * WIDTH] = second
    turn_ref[3 * WIDTH :] = pair_swap(second)


def turn_of(gram):
    return pl.pallas_call(
        turn_kernel,
        out_shape=jax.ShapeDtypeStruct((TILE, TILE), jnp.float32),
        cost_estimate=pl.CostEstimate(flops=0, bytes_accessed=12 * MIB, transcendentals=0),
        name="turn",
    )(gram)


def basis_kernel(image_ref, turn_ref, out_ref):
    out_ref[...] = nt_dot(image_ref[...], turn_ref[...]).T


def last_basis(image, turn):
    return pl.pallas_call(
        basis_kernel,
        out_shape=jax.ShapeDtypeStruct((TILE, TILE), jnp.float32),
        name="basis",
    )(image, turn)


def along_x(value, step):
    return lax.ppermute(value, "row", [(i, (i + 2 * step) % 8) for i in range(8)])


def other_core(value):
    return lax.ppermute(value, "row", [(i, i ^ 1) for i in range(8)])


def along_col(value, z_step, y_step):
    return lax.ppermute(
        value,
        "col",
        [(i, (i // 4 + z_step) % 4 * 4 + (i % 4 + y_step) % 4) for i in range(16)],
    )


def to_column(value):
    return lax.all_to_all(value, "col", split_axis=0, concat_axis=0, tiled=True)


def gather_row(value):
    mine = jnp.stack([value] + [along_x(value, d) for d in (1, 2, 3)], 0)
    return mine, other_core(mine)


def reduce_row(value):
    half = value.shape[0] // 2
    mine = value[:half] + other_core(value[half:])
    return [mine[0:1]] + [along_x(mine[d : d + 1], d) for d in (1, 2, 3)]


def sum_row(value):
    value = value + other_core(value)
    return value + along_x(value, 1) + along_x(value, 2) + along_x(value, 3)


def sum_all(value):
    value = sum_row(value)
    value = value + along_col(value, 1, 0) + along_col(value, 2, 0) + along_col(value, 3, 0)
    return value + along_col(value, 0, 1) + along_col(value, 0, 2) + along_col(value, 0, 3)


def shards(tile_weight, tile_angle, tile_list, tile_count, init_basis):
    place = lax.axis_index("row")
    x_place, core = place // 2, place % 2
    weights = tile_weight.reshape(SLOTS, TILE, TILE)
    angles = tile_angle.reshape(SLOTS, TILE, TILE)
    listing = tile_list.reshape(SLOTS, 2)
    row_of = listing[:, 0] % ROW_BLOCKS
    col_global = listing[:, 1]
    piece = col_global // ROW_BLOCKS
    core_away = (piece % 2) ^ core
    col_from = (core_away * 4 + (x_place - piece // 2) % 4) * 2 + col_global % 2
    col_to = (core_away * 4 + (piece // 2 - x_place) % 4) * 2 + col_global % 2
    live = (jnp.arange(2)[None, :] < tile_count.reshape(SLOTS // 2, 1)).reshape(SLOTS).astype(jnp.int32)
    slots = jnp.arange(SLOTS, dtype=jnp.int32)
    earlier = slots[None, :] < slots[:, None]
    count = jnp.sum(live)
    live_before = jnp.sum(jnp.where(earlier, live[None, :], 0), axis=1)
    at = jnp.where(live > 0, live_before, count + slots - live_before)
    code = slots + SLOTS * (col_from + COL_BLOCKS * (col_to + COL_BLOCKS * row_of))
    code = jnp.sum(jnp.where(at[None, :] == slots[:, None], code[None, :], 0), axis=1)
    order = code % SLOTS
    takes_col = code // SLOTS % COL_BLOCKS
    puts_col = code // (SLOTS * COL_BLOCKS) % COL_BLOCKS
    rows = code // (SLOTS * COL_BLOCKS * COL_BLOCKS)
    count = count.reshape(1)

    row_part, col_part = degrees(row_of, col_to, live, weights)
    row_part = to_column(row_part)
    col_parts = reduce_row(col_part)
    degree = jnp.sum(row_part, axis=0) + sum(c[0] for c in col_parts)
    scale = lax.rsqrt(degree[:2])
    scale = jnp.broadcast_to(scale.T[:, :, None], (TILE, 2, 2 * WIDTH)).reshape(TILE, TILE)
    plain, turned = complex_tiles(order, count, weights, angles)

    basis = jnp.transpose(init_basis.reshape(2, WIDTH, 2, TILE), (3, 2, 0, 1)).reshape(TILE, TILE)
    sent = (basis * scale).astype(jnp.bfloat16)
    turn, gram = None, None
    for rounds in range(ITERS):
        near, far = gather_row(sent)
        body = sent if gram is None else jnp.concatenate([sent, gram], 0)
        column = to_column(jnp.broadcast_to(body[None], (16,) + body.shape))
        forward = products(1.0, takes_col, rows, count, plain, [near, far], 16, "forward")
        mirror = products(-1.0, rows, puts_col, count, turned, [column], 8, "mirror")
        wide = to_column(forward)
        parts = reduce_row(mirror)
        if gram is not None:
            turn = turn_of(sum_row(jnp.sum(column[:, TILE:], axis=0)))
        image, gram = new_image(wide, parts, scale, turn)
        sent = image * scale
    basis = last_basis(image, turn_of(sum_all(gram)))
    return jnp.transpose(basis.reshape(2, 2, WIDTH, TILE), (1, 2, 0, 3)).reshape(2, WIDTH, 2 * TILE)


def solution(mesh):
    placed = (
        P(("row", "col"), None, None, None, None),
        P(("row", "col"), None, None, None, None),
        P(("row", "col"), None, None, None),
        P(("row", "col"), None),
        P(None, None, ("row", "col")),
    )
    return jax.shard_map(
        shards, mesh=mesh, in_specs=placed, out_specs=P(None, None, ("row", "col")), check_vma=False
    )
```

time: 1740 us -> 299 us (0.17)
  matrix products: 480 us -> 0 us
  blocking collectives: 437 us -> 0 us
  other arithmetic: 297 us -> 4.46 us
  waiting for transfers between devices: 215 us -> 20.5 us
  between operations: 141 us -> 0.56 us
  starting transfers between devices: 7.84 us -> 117 us
  local copies, waits for them, and re-layouts: 152 us -> 53.3 us
  Pallas kernels: 0 us -> 97.7 us
    dot_general x795 -> x0, matrix products: 480 us -> none  [the longest x775 279 us: highest_dot(): jnp.dot(left, right, precision=lax.Precision.HIGHEST, preferred_element_t...]
    psum x3 -> x0, blocking collectives: 198 us -> none  [shards(): gram_real, gram_imag = lax.psum((gram_real, gram_imag), ('row', 'col'))]
    reduce_scatter x3 -> x0, waiting for transfers between devices: 181 us -> none  [shards(): lax.psum_scatter(partial_value.reshape(2, columns, group_rows * tile), 'c...]
    convert_element_type x5 -> x3, other arithmetic: 130 us -> 0.76 us  [the longest x1 0.74 us: shards(): (jnp.arange(2)[None, :] < tile_count.reshape(SLOTS // 2, 1)).reshape(SLOTS)]
    all_to_all x2 -> x0, blocking collectives: 124 us -> none  [the longest x1 102 us: shards(): lax.all_to_all(tile_angle.reshape(devices, pair_cap, tile, tile), ('row',...]
    slice x318 -> x9, local copies, waits for them, and re-layouts: 114 us -> 0.13 us  [the longest x4 0.06 us: reduce_row(): return [mine[0:1]] + [along_x(mine[d:d + 1], d) for d in (1, 2, 3)]]
    another operation x131 -> x3, other arithmetic: 99.9 us -> 0.06 us  [gather_row(): mine = jnp.stack([value] + [along_x(value, d) for d in (1, 2, 3)], 0)]
    pallas_call x0 -> x15, Pallas kernels: none -> 97.7 us  [the longest x6 51.8 us: products(): pl.pallas_call(functools.partial(product_kernel, sign, sizes), grid_spec=...]
  transfers between devices with their start and end apart: 4 -> 53, of which waited for: 4 -> 21; matrix products, arithmetic and copies ran while one was open for 5% -> 1% of each run, Pallas kernels for 0% -> 28%
where the time goes in v1:
time: 299 us; the launch traced here: 294 us
  starting transfers between devices  117 us (39%)
  Pallas kernels  97.7 us (33%)
  local copies, waits for them, and re-layouts  53.3 us (18%)
  waiting for transfers between devices  20.5 us (7%)
  other arithmetic  4.46 us (1%)
    pallas_call x6, Pallas kernels, products(): pl.pallas_call(functools.partial(product_kernel, sign, sizes), grid_spec=...  51.8 us
    all_to_all x7, starting transfers between devices, to_column(): return lax.all_to_all(value, 'col', split_axis=0, concat_axis=0, tiled=True)  50.7 us
    unnamed x29, local copies, waits for them, and re-layouts  47.9 us
    ppermute x30, starting transfers between devices, along_x(): lax.ppermute(value, 'row', [(i, (i + 2 * step) % 8) for i in range(8)])  37.1 us
    pallas_call x3, Pallas kernels, turn_of(): pl.pallas_call(turn_kernel, out_shape=jax.ShapeDtypeStruct((TILE, TILE),...  19.1 us
    ppermute x10, starting transfers between devices, other_core(): return lax.ppermute(value, 'row', [(i, i ^ 1) for i in range(8)])  19 us
    pallas_call x1, Pallas kernels, complex_tiles(): pl.pallas_call(tiles_kernel, grid_spec=pltpu.PrefetchScalarGridSpec(num_s...  16.6 us
    ppermute x30, waiting for transfers between devices, along_x(): lax.ppermute(value, 'row', [(i, (i + 2 * step) % 8) for i in range(8)])  11.1 us
  transfers between devices with their start and end apart: 53, of which 21 were waited for; matrix products, arithmetic and copies ran while one was open for 1% of the time, Pallas kernels for 28%

profile of v1, /device:TPU:1, one launch (start us, length us, event | category | flops | bytes accessed | tf_op | source)
XLA Modules:
  0.0 293.8 jit_solution(9467215398237240092)
XLA Ops:
  1.9 3.4 %copy-done = bf16[1,128,2,128,128]{4,3,2,1,0:T(8,128)(2,1)S(1)} copy-done((bf16[1,128,2,128,128]{4,3,2,1,0:T(8,128)(2,1)S(1)}, bf16[1,128,2,128,128]{4,3,2,1,0:T(8,128)(2,1)}, u32[]{:S(2)}) %copy-start) | copy-done | bytes 8388632
  5.3 5.8 %degrees.1 = (f32[16,8,128]{2,1,0:T(8,128)}, f32[8,8,128]{2,1,0:T(8,128)S(1)}) custom-call(s32[256]{0:T(256)S(1)} %get-tuple-element.48.rows_of, s32[256]{0:T(256)S(1)} %get-tuple-element.26.cols_of, s32[256]{0:T(256)S(1)} %reshape.239.live, bf16[256,128,128]{2,1,0:T(8,128)(2,1)S(1)} %bitcast.39), custom_call_target="tpu_custom_call" | custom-call | bytes 18874368 | tf_op jit(solution)/shard_map/degrees/pallas_call | solution.py:69
  12.7 7.8 %all-to-all-start = ((f32[16,8,128]{2,1,0:T(8,128)}), f32[16,8,128]{2,1,0:T(8,128)S(1)}, u32[]{:S(2)}, u32[]{:S(2)}) async-start(f32[16,8,128]{2,1,0:T(8,128)} %get-tuple-element.16), calls=%async_computation | async-start | bytes 131072 | tf_op jit(solution)/shard_map/all_to_all | solution.py:333
  29.0 3.0 %collective-permute-start.5 = (bf16[128,128]{1,0:T(8,128)(2,1)S(1)}, bf16[128,128]{1,0:T(8,128)(2,1)S(1)}, u32[]{:S(2)}, u32[]{:S(2)}) collective-permute-start(bf16[128,128]{1,0:T(8,128)(2,1)S(1)} %multiply_convert_fusion), channel_id=1, source_target_pairs={{0,64},{16,80},{32,96},{48,112},{64,0},{80,16},{96,32},{112,48},{1... | collective-permute-start | bytes 98312 | tf_op jit(solution)/shard_map/ppermute | solution.py:317
  33.2 6.4 %all-to-all-start.2 = ((bf16[16,128,128]{2,1,0:T(8,128)(2,1)}), bf16[16,128,128]{2,1,0:T(8,128)(2,1)S(1)}, u32[]{:S(2)}, u32[]{:S(2)}) async-start(bf16[16,128,128]{2,1,0:T(8,128)(2,1)} %broadcast_in_dim.30), calls=%async_computation.2 | async-start | bytes 1048576 | tf_op jit(solution)/shard_map/all_to_all | solution.py:333
  39.7 3.2 %collective-permute-start.7 = (bf16[4,128,128]{2,1,0:T(8,128)(2,1)S(1)}, bf16[4,128,128]{2,1,0:T(8,128)(2,1)S(1)}, u32[]{:S(2)}, u32[]{:S(2)}) collective-permute-start(bf16[4,128,128]{2,1,0:T(8,128)(2,1)S(1)} %pad_maximum_fusion.2.refs_0_), channel_id=1, source_target_pairs={{0,16},{16,0},{32,48},{48,32},{64,80},{80,64},{96,112},{112,96},{1... | collective-permute-start | bytes 393224 | tf_op jit(solution)/shard_map/ppermute | solution.py:321
  43.0 3.4 %copy-done.1 = bf16[1,128,2,128,128]{4,3,2,1,0:T(8,128)(2,1)S(1)} copy-done((bf16[1,128,2,128,128]{4,3,2,1,0:T(8,128)(2,1)S(1)}, bf16[1,128,2,128,128]{4,3,2,1,0:T(8,128)(2,1)}, u32[]{:S(2)}) %copy-start.1) | copy-done | bytes 8388632
  46.4 3.4 %copy-done.2 = bf16[1,128,2,128,128]{4,3,2,1,0:T(8,128)(2,1)S(1)} copy-done((bf16[1,128,2,128,128]{4,3,2,1,0:T(8,128)(2,1)S(1)}, bf16[1,128,2,128,128]{4,3,2,1,0:T(8,128)(2,1)}, u32[]{:S(2)}) %copy-start.2) | copy-done | bytes 8388632
  49.7 16.6 %complex_tiles.1 = (bf16[256,128,256]{2,1,0:T(8,128)(2,1)}, bf16[256,128,256]{2,1,0:T(8,128)(2,1)}) custom-call(s32[256]{0:T(256)S(1)} %get-tuple-element.46.order, s32[1]{0:T(128)} %bitcast.3.count, bf16[256,128,128]{2,1,0:T(8,128)(2,1)S(1)} %bitcast.40, bf16[256,128,128]{2,1,0:T(8,128)(2,1)S(1)} %bitcast.41, bf16[256,128,128]{2,1,0:T(8,128)(2,1)S(1)} %bitcast.42, ...), custom_call_target="tpu_custom_call" | custom-call | bytes 62914560 | tf_op jit(solution)/shard_map/complex_tiles/pallas_call | solution.py:132
  66.3 5.8 %copy-done.6 = bf16[256,128,256]{2,1,0:T(8,128)(2,1)S(1)} copy-done((bf16[256,128,256]{2,1,0:T(8,128)(2,1)S(1)}, bf16[256,128,256]{2,1,0:T(8,128)(2,1)}, u32[]{:S(2)}) %copy-start.6) | copy-done | bytes 16777240
  72.1 8.5 %forward.3 = f32[16,128,128]{2,1,0:T(8,128)} custom-call(s32[256]{0:T(256)S(1)} %get-tuple-element.47.takes, s32[256]{0:T(256)S(1)} %get-tuple-element.45.puts.takes, s32[1]{0:T(128)} %bitcast.3.count, bf16[256,128,256]{2,1,0:T(8,128)(2,1)S(1)} %copy-done.6, bf16[4,128,128]{2,1,0:T(8,128)(2,1)S(1)} %pad_maximum_fusion.2.refs_0_, ...), custom_call_target="tpu_custom_call" | custom-call | bytes 37748736 | tf_op jit(solution)/shard_map/forward/pallas_call | solution.py:200
  80.6 8.9 %all-to-all-start.1 = ((f32[16,128,128]{2,1,0:T(8,128)}), f32[16,128,128]{2,1,0:T(8,128)S(1)}, u32[]{:S(2)}, u32[]{:S(2)}) async-start(f32[16,128,128]{2,1,0:T(8,128)} %forward.3), calls=%async_computation.1 | async-start | bytes 2097152 | tf_op jit(solution)/shard_map/all_to_all | solution.py:333
  89.4 5.8 %copy-done.3 = bf16[256,128,256]{2,1,0:T(8,128)(2,1)S(1)} copy-done((bf16[256,128,256]{2,1,0:T(8,128)(2,1)S(1)}, bf16[256,128,256]{2,1,0:T(8,128)(2,1)}, u32[]{:S(2)}) %copy-start.3) | copy-done | bytes 16777240
  95.2 8.8 %mirror.3 = f32[8,128,128]{2,1,0:T(8,128)S(1)} custom-call(s32[256]{0:T(256)S(1)} %get-tuple-element.45.puts.takes, s32[256]{0:T(256)S(1)} %get-tuple-element.44.puts, s32[1]{0:T(128)} %bitcast.3.count, bf16[256,128,256]{2,1,0:T(8,128)(2,1)S(1)} %copy-done.3, bf16[16,128,128]{2,1,0:T(8,128)(2,1)S(1)} %all-to-all-done.2.refs_0_), custom_call_target="tpu_custom_call" | custom-call | bytes 37748736 | tf_op jit(solution)/shard_map/mirror/pallas_call | solution.py:200
  116.7 6.5 %all-to-all-start.4 = ((f32[16,144,128]{2,1,0:T(8,128)}), f32[16,144,128]{2,1,0:T(8,128)S(1)}, u32[]{:S(2)}, u32[]{:S(2)}) async-start(f32[16,144,128]{2,1,0:T(8,128)} %broadcast_in_dim.54), calls=%async_computation.4 | async-start | bytes 2359296 | tf_op jit(solution)/shard_map/all_to_all | solution.py:333
  129.1 3.9 %collective-permute-start.15 = (f32[4,128,128]{2,1,0:T(8,128)S(1)}, f32[4,128,128]{2,1,0:T(8,128)S(1)}, u32[]{:S(2)}, u32[]{:S(2)}) collective-permute-start(f32[4,128,128]{2,1,0:T(8,128)S(1)} %pad_maximum_fusion.refs_0_), channel_id=1, source_target_pairs={{0,16},{16,0},{32,48},{48,32},{64,80},{80,64},{96,112},{112,96},{1... | collective-permute-start | bytes 786440 | tf_op jit(solution)/shard_map/ppermute | solution.py:321
  134.1 5.8 %copy-done.7 = bf16[256,128,256]{2,1,0:T(8,128)(2,1)S(1)} copy-done((bf16[256,128,256]{2,1,0:T(8,128)(2,1)S(1)}, bf16[256,128,256]{2,1,0:T(8,128)(2,1)}, u32[]{:S(2)}) %copy-start.7) | copy-done | bytes 16777240
  139.9 8.4 %forward.4 = f32[16,128,128]{2,1,0:T(8,128)} custom-call(s32[256]{0:T(256)S(1)} %get-tuple-element.47.takes, s32[256]{0:T(256)S(1)} %get-tuple-element.45.puts.takes, s32[1]{0:T(128)} %bitcast.3.count, bf16[256,128,256]{2,1,0:T(8,128)(2,1)S(1)} %copy-done.7, f32[4,128,128]{2,1,0:T(8,128)S(1)} %pad_maximum_fusion.refs_0_, ...), custom_call_target="tpu_custom_call" | custom-call | bytes 37748736 | tf_op jit(solution)/shard_map/forward/pallas_call | solution.py:200
  148.3 6.9 %all-to-all-start.3 = ((f32[16,128,128]{2,1,0:T(8,128)}), f32[16,128,128]{2,1,0:T(8,128)S(1)}, u32[]{:S(2)}, u32[]{:S(2)}) async-start(f32[16,128,128]{2,1,0:T(8,128)} %forward.4), calls=%async_computation.3 | async-start | bytes 2097152 | tf_op jit(solution)/shard_map/all_to_all | solution.py:333
  155.2 5.8 %copy-done.4 = bf16[256,128,256]{2,1,0:T(8,128)(2,1)S(1)} copy-done((bf16[256,128,256]{2,1,0:T(8,128)(2,1)S(1)}, bf16[256,128,256]{2,1,0:T(8,128)(2,1)}, u32[]{:S(2)}) %copy-start.4) | copy-done | bytes 16777240
  161.0 8.8 %mirror.4 = f32[8,128,128]{2,1,0:T(8,128)S(1)} custom-call(s32[256]{0:T(256)S(1)} %get-tuple-element.45.puts.takes, s32[256]{0:T(256)S(1)} %get-tuple-element.44.puts, s32[1]{0:T(128)} %bitcast.3.count, bf16[256,128,256]{2,1,0:T(8,128)(2,1)S(1)} %copy-done.4, f32[16,144,128]{2,1,0:T(8,128)S(1)} %all-to-all-done.4.refs_0_), custom_call_target="tpu_custom_call" | custom-call | bytes 37748736 | tf_op jit(solution)/shard_map/mirror/pallas_call | solution.py:200
  180.3 6.4 %turn.3.refs_6_ = f32[128,128]{1,0:T(8,128)} custom-call(f32[16,128]{1,0:T(8,128)} %add_add_fusion.4.gram_ref), custom_call_target="tpu_custom_call" | custom-call | bytes 12582912 | tf_op jit(solution)/shard_map/turn/pallas_call | solution.py:296
  189.7 7.2 %all-to-all-start.6 = ((f32[16,144,128]{2,1,0:T(8,128)}), f32[16,144,128]{2,1,0:T(8,128)S(1)}, u32[]{:S(2)}, u32[]{:S(2)}) async-start(f32[16,144,128]{2,1,0:T(8,128)} %broadcast_in_dim.55), calls=%async_computation.6 | async-start | bytes 2359296 | tf_op jit(solution)/shard_map/all_to_all | solution.py:333
  202.6 3.7 %collective-permute-start.27 = (f32[4,128,128]{2,1,0:T(8,128)S(1)}, f32[4,128,128]{2,1,0:T(8,128)S(1)}, u32[]{:S(2)}, u32[]{:S(2)}) collective-permute-start(f32[4,128,128]{2,1,0:T(8,128)S(1)} %pad_maximum_fusion.1.refs_0_), channel_id=1, source_target_pairs={{0,16},{16,0},{32,48},{48,32},{64,80},{80,64},{96,112},{112,96},{1... | collective-permute-start | bytes 786440 | tf_op jit(solution)/shard_map/ppermute | solution.py:321
  207.5 5.8 %copy-done.8 = bf16[256,128,256]{2,1,0:T(8,128)(2,1)S(1)} copy-done((bf16[256,128,256]{2,1,0:T(8,128)(2,1)S(1)}, bf16[256,128,256]{2,1,0:T(8,128)(2,1)}, u32[]{:S(2)}) %copy-start.8) | copy-done | bytes 16777240
  213.2 8.5 %forward.5 = f32[16,128,128]{2,1,0:T(8,128)} custom-call(s32[256]{0:T(256)S(1)} %get-tuple-element.47.takes, s32[256]{0:T(256)S(1)} %get-tuple-element.45.puts.takes, s32[1]{0:T(128)} %bitcast.3.count, bf16[256,128,256]{2,1,0:T(8,128)(2,1)S(1)} %copy-done.8, f32[4,128,128]{2,1,0:T(8,128)S(1)} %pad_maximum_fusion.1.refs_0_, ...), custom_call_target="tpu_custom_call" | custom-call | bytes 37748736 | tf_op jit(solution)/shard_map/forward/pallas_call | solution.py:200
  221.7 7.0 %all-to-all-start.5 = ((f32[16,128,128]{2,1,0:T(8,128)}), f32[16,128,128]{2,1,0:T(8,128)S(1)}, u32[]{:S(2)}, u32[]{:S(2)}) async-start(f32[16,128,128]{2,1,0:T(8,128)} %forward.5), calls=%async_computation.5 | async-start | bytes 2097152 | tf_op jit(solution)/shard_map/all_to_all | solution.py:333
  228.7 5.8 %copy-done.5 = bf16[256,128,256]{2,1,0:T(8,128)(2,1)S(1)} copy-done((bf16[256,128,256]{2,1,0:T(8,128)(2,1)S(1)}, bf16[256,128,256]{2,1,0:T(8,128)(2,1)}, u32[]{:S(2)}) %copy-start.5) | copy-done | bytes 16777240
  234.5 8.8 %mirror.5 = f32[8,128,128]{2,1,0:T(8,128)S(1)} custom-call(s32[256]{0:T(256)S(1)} %get-tuple-element.45.puts.takes, s32[256]{0:T(256)S(1)} %get-tuple-element.44.puts, s32[1]{0:T(128)} %bitcast.3.count, bf16[256,128,256]{2,1,0:T(8,128)(2,1)S(1)} %copy-done.5, f32[16,144,128]{2,1,0:T(8,128)S(1)} %all-to-all-done.6.refs_0_), custom_call_target="tpu_custom_call" | custom-call | bytes 37748736 | tf_op jit(solution)/shard_map/mirror/pallas_call | solution.py:200
  254.0 6.4 %turn.4.refs_6_ = f32[128,128]{1,0:T(8,128)} custom-call(f32[16,128]{1,0:T(8,128)} %add_add_fusion.3.gram_ref), custom_call_target="tpu_custom_call" | custom-call | bytes 12582912 | tf_op jit(solution)/shard_map/turn/pallas_call | solution.py:296
  278.2 2.8 collective-permute-start.44
  284.1 6.4 %turn.5.turn_ref = f32[128,128]{1,0:T(8,128)} custom-call(f32[16,128]{1,0:T(8,128)} %add_add_fusion.gram_ref), custom_call_target="tpu_custom_call" | custom-call | bytes 12582912 | tf_op jit(solution)/shard_map/turn/pallas_call | solution.py:296
  (173 shorter events, 87.9 us)
Async XLA Ops:
  11.1 10.9 %collective-permute-start = (f32[4,8,128]{2,1,0:T(8,128)S(1)}, f32[4,8,128]{2,1,0:T(8,128)S(1)}, u32[]{:S(2)}, u32[]{:S(2)}) collective-permute-start(f32[4,8,128]{2,1,0:T(8,128)S(1)} %slice.90), channel_id=1, source_target_pairs={{0,16},{16,0},{32,48},{48,32},{64,80},{80,64},{96,112},{112,96},{1... | collective-permute-start | bytes 49160 | tf_op jit(solution)/shard_map/ppermute | solution.py:321
  12.7 14.6 %all-to-all-start = ((f32[16,8,128]{2,1,0:T(8,128)}), f32[16,8,128]{2,1,0:T(8,128)S(1)}, u32[]{:S(2)}, u32[]{:S(2)}) async-start(f32[16,8,128]{2,1,0:T(8,128)} %get-tuple-element.16), calls=%async_computation | async-start | bytes 131072 | tf_op jit(solution)/shard_map/all_to_all | solution.py:333
  22.0 5.3 %collective-permute-start.1 = (f32[1,8,128]{2,1,0:T(8,128)S(1)}, f32[1,8,128]{2,1,0:T(8,128)S(1)}, u32[]{:S(2)}, u32[]{:S(2)}) collective-permute-start(f32[1,8,128]{2,1,0:T(8,128)S(1)} %get-tuple-element.39), channel_id=1, source_target_pairs={{0,32},{16,48},{32,64},{48,80},{64,96},{80,112},{96,0},{112,16},{1... | collective-permute-start | bytes 12296 | tf_op jit(solution)/shard_map/ppermute | solution.py:317
  28.6 11.1 %collective-permute-start.4 = (bf16[128,128]{1,0:T(8,128)(2,1)S(1)}, bf16[128,128]{1,0:T(8,128)(2,1)S(1)}, u32[]{:S(2)}, u32[]{:S(2)}) collective-permute-start(bf16[128,128]{1,0:T(8,128)(2,1)S(1)} %multiply_convert_fusion), channel_id=1, source_target_pairs={{0,32},{16,48},{32,64},{48,80},{64,96},{80,112},{96,0},{112,16},{1... | collective-permute-start | bytes 98312 | tf_op jit(solution)/shard_map/ppermute | solution.py:317
  29.0 10.7 %collective-permute-start.5 = (bf16[128,128]{1,0:T(8,128)(2,1)S(1)}, bf16[128,128]{1,0:T(8,128)(2,1)S(1)}, u32[]{:S(2)}, u32[]{:S(2)}) collective-permute-start(bf16[128,128]{1,0:T(8,128)(2,1)S(1)} %multiply_convert_fusion), channel_id=1, source_target_pairs={{0,64},{16,80},{32,96},{48,112},{64,0},{80,16},{96,32},{112,48},{1... | collective-permute-start | bytes 98312 | tf_op jit(solution)/shard_map/ppermute | solution.py:317
  32.0 7.7 %collective-permute-start.6 = (bf16[128,128]{1,0:T(8,128)(2,1)S(1)}, bf16[128,128]{1,0:T(8,128)(2,1)S(1)}, u32[]{:S(2)}, u32[]{:S(2)}) collective-permute-start(bf16[128,128]{1,0:T(8,128)(2,1)S(1)} %multiply_convert_fusion), channel_id=1, source_target_pairs={{0,96},{16,112},{32,0},{48,16},{64,32},{80,48},{96,64},{112,80},{1... | collective-permute-start | bytes 98312 | tf_op jit(solution)/shard_map/ppermute | solution.py:317
  33.2 47.4 %all-to-all-start.2 = ((bf16[16,128,128]{2,1,0:T(8,128)(2,1)}), bf16[16,128,128]{2,1,0:T(8,128)(2,1)S(1)}, u32[]{:S(2)}, u32[]{:S(2)}) async-start(bf16[16,128,128]{2,1,0:T(8,128)(2,1)} %broadcast_in_dim.30), calls=%async_computation.2 | async-start | bytes 1048576 | tf_op jit(solution)/shard_map/all_to_all | solution.py:333
  39.7 26.6 %collective-permute-start.7 = (bf16[4,128,128]{2,1,0:T(8,128)(2,1)S(1)}, bf16[4,128,128]{2,1,0:T(8,128)(2,1)S(1)}, u32[]{:S(2)}, u32[]{:S(2)}) collective-permute-start(bf16[4,128,128]{2,1,0:T(8,128)(2,1)S(1)} %pad_maximum_fusion.2.refs_0_), channel_id=1, source_target_pairs={{0,16},{16,0},{32,48},{48,32},{64,80},{80,64},{96,112},{112,96},{1... | collective-permute-start | bytes 393224 | tf_op jit(solution)/shard_map/ppermute | solution.py:321
  80.6 34.4 %all-to-all-start.1 = ((f32[16,128,128]{2,1,0:T(8,128)}), f32[16,128,128]{2,1,0:T(8,128)S(1)}, u32[]{:S(2)}, u32[]{:S(2)}) async-start(f32[16,128,128]{2,1,0:T(8,128)} %forward.3), calls=%async_computation.1 | async-start | bytes 2097152 | tf_op jit(solution)/shard_map/all_to_all | solution.py:333
  116.7 31.6 %all-to-all-start.4 = ((f32[16,144,128]{2,1,0:T(8,128)}), f32[16,144,128]{2,1,0:T(8,128)S(1)}, u32[]{:S(2)}, u32[]{:S(2)}) async-start(f32[16,144,128]{2,1,0:T(8,128)} %broadcast_in_dim.54), calls=%async_computation.4 | async-start | bytes 2359296 | tf_op jit(solution)/shard_map/all_to_all | solution.py:333
  123.2 5.3 %collective-permute-start.12 = (f32[128,128]{1,0:T(8,128)S(1)}, f32[128,128]{1,0:T(8,128)S(1)}, u32[]{:S(2)}, u32[]{:S(2)}) collective-permute-start(f32[128,128]{1,0:T(8,128)S(1)} %mul.74), channel_id=1, source_target_pairs={{0,32},{16,48},{32,64},{48,80},{64,96},{80,112},{96,0},{112,16},{1... | collective-permute-start | bytes 196616 | tf_op jit(solution)/shard_map/ppermute | solution.py:317
  123.5 5.0 %collective-permute-start.13 = (f32[128,128]{1,0:T(8,128)S(1)}, f32[128,128]{1,0:T(8,128)S(1)}, u32[]{:S(2)}, u32[]{:S(2)}) collective-permute-start(f32[128,128]{1,0:T(8,128)S(1)} %mul.74), channel_id=1, source_target_pairs={{0,64},{16,80},{32,96},{48,112},{64,0},{80,16},{96,32},{112,48},{1... | collective-permute-start | bytes 196616 | tf_op jit(solution)/shard_map/ppermute | solution.py:317
  129.1 5.0 %collective-permute-start.15 = (f32[4,128,128]{2,1,0:T(8,128)S(1)}, f32[4,128,128]{2,1,0:T(8,128)S(1)}, u32[]{:S(2)}, u32[]{:S(2)}) collective-permute-start(f32[4,128,128]{2,1,0:T(8,128)S(1)} %pad_maximum_fusion.refs_0_), channel_id=1, source_target_pairs={{0,16},{16,0},{32,48},{48,32},{64,80},{80,64},{96,112},{112,96},{1... | collective-permute-start | bytes 786440 | tf_op jit(solution)/shard_map/ppermute | solution.py:321
  148.3 38.4 %all-to-all-start.3 = ((f32[16,128,128]{2,1,0:T(8,128)}), f32[16,128,128]{2,1,0:T(8,128)S(1)}, u32[]{:S(2)}, u32[]{:S(2)}) async-start(f32[16,128,128]{2,1,0:T(8,128)} %forward.4), calls=%async_computation.3 | async-start | bytes 2097152 | tf_op jit(solution)/shard_map/all_to_all | solution.py:333
  169.9 5.8 %collective-permute-start.16 = (f32[4,128,128]{2,1,0:T(8,128)S(1)}, f32[4,128,128]{2,1,0:T(8,128)S(1)}, u32[]{:S(2)}, u32[]{:S(2)}) collective-permute-start(f32[4,128,128]{2,1,0:T(8,128)S(1)} %slice.129), channel_id=1, source_target_pairs={{0,16},{16,0},{32,48},{48,32},{64,80},{80,64},{96,112},{112,96},{1... | collective-permute-start | bytes 786440 | tf_op jit(solution)/shard_map/ppermute | solution.py:321
  172.4 5.4 %collective-permute-start.21 = (f32[16,128]{1,0:T(8,128)S(1)}, f32[16,128]{1,0:T(8,128)S(1)}, u32[]{:S(2)}, u32[]{:S(2)}) collective-permute-start(f32[16,128]{1,0:T(8,128)S(1)} %add.238), channel_id=1, source_target_pairs={{0,32},{16,48},{32,64},{48,80},{64,96},{80,112},{96,0},{112,16},{1... | collective-permute-start | bytes 24584 | tf_op jit(solution)/shard_map/ppermute | solution.py:317
  173.3 6.4 %collective-permute-start.22 = (f32[16,128]{1,0:T(8,128)S(1)}, f32[16,128]{1,0:T(8,128)S(1)}, u32[]{:S(2)}, u32[]{:S(2)}) collective-permute-start(f32[16,128]{1,0:T(8,128)S(1)} %add.238), channel_id=1, source_target_pairs={{0,64},{16,80},{32,96},{48,112},{64,0},{80,16},{96,32},{112,48},{1... | collective-permute-start | bytes 24584 | tf_op jit(solution)/shard_map/ppermute | solution.py:317
  175.7 11.0 %collective-permute-start.17 = (f32[1,128,128]{2,1,0:T(8,128)S(1)}, f32[1,128,128]{2,1,0:T(8,128)S(1)}, u32[]{:S(2)}, u32[]{:S(2)}) collective-permute-start(f32[1,128,128]{2,1,0:T(8,128)S(1)} %get-tuple-element.33), channel_id=1, source_target_pairs={{0,32},{16,48},{32,64},{48,80},{64,96},{80,112},{96,0},{112,16},{1... | collective-permute-start | bytes 196616 | tf_op jit(solution)/shard_map/ppermute | solution.py:317
  177.1 9.6 %collective-permute-start.18 = (f32[1,128,128]{2,1,0:T(8,128)S(1)}, f32[1,128,128]{2,1,0:T(8,128)S(1)}, u32[]{:S(2)}, u32[]{:S(2)}) collective-permute-start(f32[1,128,128]{2,1,0:T(8,128)S(1)} %get-tuple-element.32), channel_id=1, source_target_pairs={{0,64},{16,80},{32,96},{48,112},{64,0},{80,16},{96,32},{112,48},{1... | collective-permute-start | bytes 196616 | tf_op jit(solution)/shard_map/ppermute | solution.py:317
  177.8 8.9 %collective-permute-start.19 = (f32[1,128,128]{2,1,0:T(8,128)S(1)}, f32[1,128,128]{2,1,0:T(8,128)S(1)}, u32[]{:S(2)}, u32[]{:S(2)}) collective-permute-start(f32[1,128,128]{2,1,0:T(8,128)S(1)} %get-tuple-element.31), channel_id=1, source_target_pairs={{0,96},{16,112},{32,0},{48,16},{64,32},{80,48},{96,64},{112,80},{1... | collective-permute-start | bytes 196616 | tf_op jit(solution)/shard_map/ppermute | solution.py:317
  189.7 32.0 %all-to-all-start.6 = ((f32[16,144,128]{2,1,0:T(8,128)}), f32[16,144,128]{2,1,0:T(8,128)S(1)}, u32[]{:S(2)}, u32[]{:S(2)}) async-start(f32[16,144,128]{2,1,0:T(8,128)} %broadcast_in_dim.55), calls=%async_computation.6 | async-start | bytes 2359296 | tf_op jit(solution)/shard_map/all_to_all | solution.py:333
  196.9 5.1 %collective-permute-start.24 = (f32[128,128]{1,0:T(8,128)S(1)}, f32[128,128]{1,0:T(8,128)S(1)}, u32[]{:S(2)}, u32[]{:S(2)}) collective-permute-start(f32[128,128]{1,0:T(8,128)S(1)} %mul.75), channel_id=1, source_target_pairs={{0,32},{16,48},{32,64},{48,80},{64,96},{80,112},{96,0},{112,16},{1... | collective-permute-start | bytes 196616 | tf_op jit(solution)/shard_map/ppermute | solution.py:317
  197.0 5.0 %collective-permute-start.25 = (f32[128,128]{1,0:T(8,128)S(1)}, f32[128,128]{1,0:T(8,128)S(1)}, u32[]{:S(2)}, u32[]{:S(2)}) collective-permute-start(f32[128,128]{1,0:T(8,128)S(1)} %mul.75), channel_id=1, source_target_pairs={{0,64},{16,80},{32,96},{48,112},{64,0},{80,16},{96,32},{112,48},{1... | collective-permute-start | bytes 196616 | tf_op jit(solution)/shard_map/ppermute | solution.py:317
  202.6 4.9 %collective-permute-start.27 = (f32[4,128,128]{2,1,0:T(8,128)S(1)}, f32[4,128,128]{2,1,0:T(8,128)S(1)}, u32[]{:S(2)}, u32[]{:S(2)}) collective-permute-start(f32[4,128,128]{2,1,0:T(8,128)S(1)} %pad_maximum_fusion.1.refs_0_), channel_id=1, source_target_pairs={{0,16},{16,0},{32,48},{48,32},{64,80},{80,64},{96,112},{112,96},{1... | collective-permute-start | bytes 786440 | tf_op jit(solution)/shard_map/ppermute | solution.py:321
  221.7 38.7 %all-to-all-start.5 = ((f32[16,128,128]{2,1,0:T(8,128)}), f32[16,128,128]{2,1,0:T(8,128)S(1)}, u32[]{:S(2)}, u32[]{:S(2)}) async-start(f32[16,128,128]{2,1,0:T(8,128)} %forward.5), calls=%async_computation.5 | async-start | bytes 2097152 | tf_op jit(solution)/shard_map/all_to_all | solution.py:333
  243.3 5.9 %collective-permute-start.28 = (f32[4,128,128]{2,1,0:T(8,128)S(1)}, f32[4,128,128]{2,1,0:T(8,128)S(1)}, u32[]{:S(2)}, u32[]{:S(2)}) collective-permute-start(f32[4,128,128]{2,1,0:T(8,128)S(1)} %slice.136), channel_id=1, source_target_pairs={{0,16},{16,0},{32,48},{48,32},{64,80},{80,64},{96,112},{112,96},{1... | collective-permute-start | bytes 786440 | tf_op jit(solution)/shard_map/ppermute | solution.py:321
  245.9 5.4 %collective-permute-start.33 = (f32[16,128]{1,0:T(8,128)S(1)}, f32[16,128]{1,0:T(8,128)S(1)}, u32[]{:S(2)}, u32[]{:S(2)}) collective-permute-start(f32[16,128]{1,0:T(8,128)S(1)} %add.243), channel_id=1, source_target_pairs={{0,32},{16,48},{32,64},{48,80},{64,96},{80,112},{96,0},{112,16},{1... | collective-permute-start | bytes 24584 | tf_op jit(solution)/shard_map/ppermute | solution.py:317
  246.7 6.6 %collective-permute-start.34 = (f32[16,128]{1,0:T(8,128)S(1)}, f32[16,128]{1,0:T(8,128)S(1)}, u32[]{:S(2)}, u32[]{:S(2)}) collective-permute-start(f32[16,128]{1,0:T(8,128)S(1)} %add.243), channel_id=1, source_target_pairs={{0,64},{16,80},{32,96},{48,112},{64,0},{80,16},{96,32},{112,48},{1... | collective-permute-start | bytes 24584 | tf_op jit(solution)/shard_map/ppermute | solution.py:317
  249.3 11.0 %collective-permute-start.29 = (f32[1,128,128]{2,1,0:T(8,128)S(1)}, f32[1,128,128]{2,1,0:T(8,128)S(1)}, u32[]{:S(2)}, u32[]{:S(2)}) collective-permute-start(f32[1,128,128]{2,1,0:T(8,128)S(1)} %get-tuple-element.29), channel_id=1, source_target_pairs={{0,32},{16,48},{32,64},{48,80},{64,96},{80,112},{96,0},{112,16},{1... | collective-permute-start | bytes 196616 | tf_op jit(solution)/shard_map/ppermute | solution.py:317
  250.9 9.5 %collective-permute-start.30 = (f32[1,128,128]{2,1,0:T(8,128)S(1)}, f32[1,128,128]{2,1,0:T(8,128)S(1)}, u32[]{:S(2)}, u32[]{:S(2)}) collective-permute-start(f32[1,128,128]{2,1,0:T(8,128)S(1)} %get-tuple-element.28), channel_id=1, source_target_pairs={{0,64},{16,80},{32,96},{48,112},{64,0},{80,16},{96,32},{112,48},{1... | collective-permute-start | bytes 196616 | tf_op jit(solution)/shard_map/ppermute | solution.py:317
  251.3 9.1 %collective-permute-start.31 = (f32[1,128,128]{2,1,0:T(8,128)S(1)}, f32[1,128,128]{2,1,0:T(8,128)S(1)}, u32[]{:S(2)}, u32[]{:S(2)}) collective-permute-start(f32[1,128,128]{2,1,0:T(8,128)S(1)} %get-tuple-element.27), channel_id=1, source_target_pairs={{0,96},{16,112},{32,0},{48,16},{64,32},{80,48},{96,64},{112,80},{1... | collective-permute-start | bytes 196616 | tf_op jit(solution)/shard_map/ppermute | solution.py:317
  270.3 5.6 %collective-permute-start.40 = (f32[16,128]{1,0:T(8,128)S(1)}, f32[16,128]{1,0:T(8,128)S(1)}, u32[]{:S(2)}, u32[]{:S(2)}) collective-permute-start(f32[16,128]{1,0:T(8,128)S(1)} %add_add_fusion.2), channel_id=1, source_target_pairs={{0,4},{1,5},{2,6},{3,7},{4,8},{5,9},{6,10},{7,11},{8,12},{9,13},{1... | collective-permute-start | bytes 24584 | tf_op jit(solution)/shard_map/ppermute | solution.py:325
  (35 other events, 155.9 us)

commit v2 on v1

v2 whole, which is shorter than its diff:
```python
import functools

import jax
import jax.numpy as jnp
from jax import lax
from jax.experimental import pallas as pl
from jax.experimental.pallas import tpu as pltpu
from jax.sharding import PartitionSpec as P

ITERS = 3
IMAGES = 32768
TILE = 128
WIDTH = 32
SLOTS = 256
ROW_BLOCKS = 32
COL_BLOCKS = 16
CHUNK = 16
TRIG_CHUNK = 8
RING = 4
HALF_SIN = (0.5, -0.020833322778344154, 0.00026040783268399537, -1.5475804957532091e-06, 5.088141019626846e-09)
HALF_COS = (0.9999999403953552, -0.1249997615814209, 0.0026039734948426485, -2.164632678613998e-05, 9.044046578310372e-08)
HIGHEST = lax.Precision.HIGHEST
MIB = 1 << 20


def horner(u, coefs):
    value = coefs[-1]
    for coef in coefs[-2::-1]:
        value = value * u + coef
    return value


def lanes(shape):
    return lax.broadcasted_iota(jnp.int32, shape, 1)


def pair_swap(x):
    even = (lanes(x.shape) // WIDTH) % 2 == 0
    return jnp.where(even, -pltpu.roll(x, TILE - WIDTH, 1), pltpu.roll(x, WIDTH, 1))


VECTOR = pl.BlockSpec(memory_space=pltpu.VMEM)
SCALAR = pl.BlockSpec(memory_space=pltpu.SMEM)


FAR = pl.BlockSpec(memory_space=pl.ANY)


def fetch(source, target, sems, c):
    part = pl.ds(c * CHUNK, CHUNK)
    return pltpu.make_async_copy(source.at[part], target.at[part], sems.at[c])


def start_fetches(source, target, sems, chunks):
    def start(c, carry):
        fetch(source, target, sems, c).start()
        return carry

    lax.fori_loop(0, chunks, start, 0)


def degree_kernel(rows_of, cols_of, live, far_ref, row_ref, col_ref, row_acc, col_acc, w_ref, sems):
    start_fetches(far_ref, w_ref, sems, SLOTS // CHUNK)
    row_acc[...] = jnp.zeros_like(row_acc)
    col_acc[...] = jnp.zeros_like(col_acc)

    def step(c, carry):
        fetch(far_ref, w_ref, sems, c).wait()
        for u in range(CHUNK):
            slot = c * CHUNK + u

            @pl.when(live[slot] > 0)
            def _():
                w = w_ref[slot].astype(jnp.float32)
                row_acc[rows_of[slot]] += w
                col_acc[cols_of[slot]] += jnp.sum(w.reshape(TILE // 8, 8, TILE), axis=0)

        return carry

    lax.fori_loop(0, SLOTS // CHUNK, step, 0)
    for p in range(ROW_BLOCKS // 2):
        sums = [jnp.sum(row_acc[2 * p + k].T, axis=0, keepdims=True) for k in range(2)]
        row_ref[p] = 0.5 * jnp.concatenate(sums * 4, axis=0)
    for p in range(COL_BLOCKS // 2):
        sums = [jnp.sum(col_acc[2 * p + k], axis=0, keepdims=True) for k in range(2)]
        col_ref[p] = 0.5 * jnp.concatenate(sums * 4, axis=0)


def degrees(rows_of, cols_of, live, weights):
    return pl.pallas_call(
        degree_kernel,
        in_specs=[SCALAR, SCALAR, SCALAR, FAR],
        out_specs=[VECTOR, VECTOR],
        scratch_shapes=[
            pltpu.VMEM((ROW_BLOCKS, TILE, TILE), jnp.float32),
            pltpu.VMEM((COL_BLOCKS, 8, TILE), jnp.float32),
            pltpu.VMEM((SLOTS, TILE, TILE), jnp.bfloat16),
            pltpu.SemaphoreType.DMA((SLOTS // CHUNK,)),
        ],
        out_shape=[
            jax.ShapeDtypeStruct((ROW_BLOCKS // 2, 8, TILE), jnp.float32),
            jax.ShapeDtypeStruct((COL_BLOCKS // 2, 8, TILE), jnp.float32),
        ],
        compiler_params=pltpu.CompilerParams(vmem_limit_bytes=58 * MIB),
        cost_estimate=pl.CostEstimate(flops=0, bytes_accessed=18 * MIB, transcendentals=0),
        name="degrees",
    )(rows_of, cols_of, live, weights)


def tiles_kernel(
    order, count, far_w, far_a, far_plain, far_turned, done_ref, w_buf, a_buf, plain, turned, in_sems, out_sems
):
    done_ref[...] = jnp.zeros_like(done_ref)
    chunks = pl.cdiv(count[0], CHUNK) * (CHUNK // TRIG_CHUNK)

    def incoming(c):
        ring = c % RING
        for u in range(TRIG_CHUNK):
            source = order[c * TRIG_CHUNK + u]
            yield pltpu.make_async_copy(far_w.at[source], w_buf.at[ring, u], in_sems.at[ring, 0, u])
            yield pltpu.make_async_copy(far_a.at[source], a_buf.at[ring, u], in_sems.at[ring, 1, u])

    def outgoing(c):
        part = pl.ds(c * TRIG_CHUNK, TRIG_CHUNK)
        yield pltpu.make_async_copy(plain.at[c % 2], far_plain.at[part], out_sems.at[c % 2, 0])
        yield pltpu.make_async_copy(turned.at[c % 2], far_turned.at[part], out_sems.at[c % 2, 1])

    def begin(c):
        @pl.when(c < chunks)
        def _():
            for copy in incoming(c):
                copy.start()

    for c in range(RING - 1):
        begin(jnp.int32(c))

    def step(c, carry):
        begin(c + RING - 1)
        for copy in incoming(c):
            copy.wait()

        @pl.when(c >= 2)
        def _():
            for copy in outgoing(c - 2):
                copy.wait()

        ring, side = c % RING, c % 2
        for u in range(TRIG_CHUNK):
            half = jnp.where(c * TRIG_CHUNK + u < count[0], 0.5, 0.0).astype(jnp.float32)
            theta = a_buf[ring, u].astype(jnp.float32)
            w = w_buf[ring, u].astype(jnp.float32) * half
            square = theta * theta
            sine = theta * horner(square, HALF_SIN)
            cosine = horner(square, HALF_COS)
            part = (w + w) * sine
            real = w - part * sine
            imag = part * cosine
            plain[side, u, :, :TILE] = real.astype(jnp.bfloat16)
            plain[side, u, :, TILE:] = imag.astype(jnp.bfloat16)
            turned[side, u, :, :TILE] = real.T.astype(jnp.bfloat16)
            turned[side, u, :, TILE:] = imag.T.astype(jnp.bfloat16)
        for copy in outgoing(c):
            copy.start()
        return carry

    lax.fori_loop(0, chunks, step, 0)
    for back in (2, 1):
        for copy in outgoing(chunks - back):
            copy.wait()


def complex_tiles(order, count, weights, angles):
    return pl.pallas_call(
        tiles_kernel,
        in_specs=[SCALAR, SCALAR, FAR, FAR],
        out_specs=[FAR, FAR, VECTOR],
        out_shape=[jax.ShapeDtypeStruct((SLOTS, TILE, 2 * TILE), jnp.bfloat16)] * 2
        + [jax.ShapeDtypeStruct((8, TILE), jnp.float32)],
        scratch_shapes=[
            pltpu.VMEM((RING, TRIG_CHUNK, TILE, TILE), jnp.bfloat16),
            pltpu.VMEM((RING, TRIG_CHUNK, TILE, TILE), jnp.bfloat16),
            pltpu.VMEM((2, TRIG_CHUNK, TILE, 2 * TILE), jnp.bfloat16),
            pltpu.VMEM((2, TRIG_CHUNK, TILE, 2 * TILE), jnp.bfloat16),
            pltpu.SemaphoreType.DMA((RING, 2, TRIG_CHUNK)),
            pltpu.SemaphoreType.DMA((2, 2)),
        ],
        compiler_params=pltpu.CompilerParams(vmem_limit_bytes=58 * MIB),
        cost_estimate=pl.CostEstimate(flops=0, bytes_accessed=50 * MIB, transcendentals=0),
        name="complex_tiles",
    )(order, count, weights, angles)


def product_kernel(sign, sizes, takes, puts, count, far_ref, *refs):
    x_refs = refs[: len(sizes)]
    out_ref, x_mat, acc, tiles_ref, sems = refs[len(sizes) :]
    chunks = pl.cdiv(count[0], CHUNK)
    start_fetches(far_ref, tiles_ref, sems, chunks)
    low = lanes((TILE, TILE)) < 2 * WIDTH
    acc[...] = jnp.zeros_like(acc)
    base = 0
    for x_ref, size in zip(x_refs, sizes):
        for p in range(size):
            value = x_ref[p, :TILE].astype(jnp.float32)
            high = value.astype(jnp.bfloat16).astype(jnp.float32)
            rest = value - high
            for k in range(2):
                if k == 0:
                    top = jnp.where(low, high, pltpu.roll(rest, 2 * WIDTH, 1))
                else:
                    top = jnp.where(low, pltpu.roll(high, 2 * WIDTH, 1), rest)
                x_mat[base + 2 * p + k, :TILE] = top.astype(jnp.bfloat16)
                x_mat[base + 2 * p + k, TILE:] = (sign * pair_swap(top)).astype(jnp.bfloat16)
        base += 2 * size

    def step(c, carry):
        fetch(far_ref, tiles_ref, sems, c).wait()
        for u in range(CHUNK):
            slot = c * CHUNK + u
            acc[puts[slot]] += jnp.dot(
                tiles_ref[slot], x_mat[takes[slot]], preferred_element_type=jnp.float32
            )
        return carry

    lax.fori_loop(0, chunks, step, 0)
    if out_ref.shape[1] > TILE:
        gram = x_refs[0][0, TILE:]
        for p in range(1, sizes[0]):
            gram = gram + x_refs[0][p, TILE:]
    for p in range(out_ref.shape[0]):
        if out_ref.shape[1] > TILE:
            out_ref[p, TILE:] = gram
        first, second = acc[2 * p], acc[2 * p + 1]
        out_ref[p, :TILE] = jnp.where(
            low,
            first + pltpu.roll(first, 2 * WIDTH, 1),
            second + pltpu.roll(second, 2 * WIDTH, 1),
        )


def products(sign, takes, puts, count, tiles, sources, out_shape, name):
    sizes = tuple(s.shape[0] for s in sources)
    return pl.pallas_call(
        functools.partial(product_kernel, sign, sizes),
        in_specs=[SCALAR, SCALAR, SCALAR, FAR] + [VECTOR] * len(sources),
        out_specs=VECTOR,
        scratch_shapes=[
            pltpu.VMEM((2 * sum(sizes), 2 * TILE, TILE), jnp.bfloat16),
            pltpu.VMEM((2 * out_shape[0], TILE, TILE), jnp.float32),
            pltpu.VMEM((SLOTS, TILE, 2 * TILE), jnp.bfloat16),
            pltpu.SemaphoreType.DMA((SLOTS // CHUNK,)),
        ],
        out_shape=jax.ShapeDtypeStruct(out_shape, jnp.float32),
        compiler_params=pltpu.CompilerParams(vmem_limit_bytes=52 * MIB),
        cost_estimate=pl.CostEstimate(flops=0, bytes_accessed=30 * MIB, transcendentals=0),
        name=name,
    )(takes, puts, count, tiles, *sources)


def gather_kernel(turned, final, n_parts, *refs):
    wide_ref, part_refs = refs[0], refs[1 : 1 + n_parts]
    scale_ref = refs[1 + n_parts]
    rest = refs[2 + n_parts :]
    total = wide_ref[0]
    for p in range(1, wide_ref.shape[0]):
        total = total + wide_ref[p]
    for ref in part_refs:
        total = total + ref[0, :TILE]
    scale = scale_ref[...]
    image = total * scale
    if turned:
        image = nt_dot(image, rest[0][...])
        rest = rest[1:]
    across = image.T
    gram = nt_dot(across, across)
    pairs = gram[: 2 * WIDTH] + pltpu.roll(gram[2 * WIDTH :], 2 * WIDTH, 1)
    upper, lower = pairs[:WIDTH], pairs[WIDTH:]
    lane = lanes(upper.shape)
    other = jnp.where(lane < WIDTH, pltpu.roll(lower, TILE - WIDTH, 1), -pltpu.roll(lower, WIDTH, 1))
    both = upper + other
    if final:
        image_ref, gram_ref = rest
        image_ref[...] = image
        row = lax.broadcasted_iota(jnp.int32, upper.shape, 0)
        packed = jnp.where(lane >= row, both, pltpu.roll(both, TILE - WIDTH, 1))
        out = packed[:8]
        group = lanes((8, TILE)) // WIDTH
        for g in range(1, 4):
            out = jnp.where(group == g, pltpu.roll(packed[8 * g : 8 * g + 8], WIDTH * g, 1), out)
        gram_ref[0] = out
    else:
        sent_ref, body_ref = rest
        value = image * scale
        sent_ref[...] = value
        body_ref[:TILE] = value
        low = lanes((WIDTH // 2, TILE)) < 2 * WIDTH
        body_ref[TILE:] = jnp.where(
            low, both[: WIDTH // 2], pltpu.roll(both[WIDTH // 2 :], 2 * WIDTH, 1)
        )


def nt_dot(left, right):
    return lax.dot_general(
        left, right, (((1,), (1,)), ((), ())), precision=HIGHEST, preferred_element_type=jnp.float32
    )


def new_image(wide, parts, scale, turn, final):
    operands = [wide, *parts, scale] + ([] if turn is None else [turn])
    second = (1, 8, TILE) if final else (TILE + WIDTH // 2, TILE)
    return pl.pallas_call(
        functools.partial(gather_kernel, turn is not None, final, len(parts)),
        out_shape=[
            jax.ShapeDtypeStruct((TILE, TILE), jnp.float32),
            jax.ShapeDtypeStruct(second, jnp.float32),
        ],
        compiler_params=pltpu.CompilerParams(vmem_limit_bytes=6 * MIB),
        cost_estimate=pl.CostEstimate(flops=0, bytes_accessed=6 * MIB, transcendentals=0),
        name="new_image",
    )(*operands)


def spread(x, lane):
    return jnp.broadcast_to(x[:, lane : lane + 1], (8, TILE))


def invert_factor(value, turn_ref):
    size = 4
    lane = lanes((WIDTH, TILE))
    place = lax.broadcasted_iota(jnp.int32, (WIDTH, TILE), 0)
    diagonal = lane == place
    trace = jnp.sum(jnp.where(diagonal, value, 0.0))
    ridge = 0.01 * trace / WIDTH + 1e-6
    value = value + jnp.where(diagonal, ridge, 0.0)
    value = value + jnp.where(lane == place + 2 * WIDTH, 1.0, 0.0)
    groups = [value[8 * g : 8 * g + 8] for g in range(4)]
    within = lax.broadcasted_iota(jnp.int32, (8, TILE), 0)
    for c in range(0, WIDTH, size):
        g, o = c // 8, c % 8
        rows = [jnp.broadcast_to(groups[g][o + r : o + r + 1], (8, TILE)) for r in range(size)]
        turned = [pair_swap(row) for row in rows]
        block = {
            (r, k): (spread(rows[r], c + k), spread(rows[r], WIDTH + c + k))
            for r in range(size)
            for k in range(r, size)
        }
        below = list(range(g if o + size < 8 else g + 1, 4))
        cols = {
            (h, k): (spread(groups[h], c + k), spread(groups[h], WIDTH + c + k))
            for h in below
            for k in range(size)
        }
        new = {h: groups[h] for h in below}
        for k in range(size):
            inverse = 1.0 / block[k, k][0]
            for r in range(k + 1, size):
                real, imag = block[k, r][0] * inverse, -block[k, r][1] * inverse
                rows[r], turned[r] = (
                    rows[r] - (real * rows[k] + imag * turned[k]),
                    turned[r] - (real * turned[k] - imag * rows[k]),
                )
                for j in range(r, size):
                    other = block[k, j]
                    block[r, j] = (
                        block[r, j][0] - (real * other[0] - imag * other[1]),
                        block[r, j][1] - (real * other[1] + imag * other[0]),
                    )
            for h in below:
                real, imag = cols[h, k][0] * inverse, cols[h, k][1] * inverse
                for j in range(k + 1, size):
                    other = block[k, j]
                    cols[h, j] = (
                        cols[h, j][0] - (real * other[0] - imag * other[1]),
                        cols[h, j][1] - (real * other[1] + imag * other[0]),
                    )
                step = real * rows[k] + imag * turned[k]
                new[h] = new[h] - (jnp.where(within >= o + size, step, 0.0) if h == g else step)
        kept = new.get(g, groups[g])
        for r in range(size):
            kept = jnp.where(within == o + r, rows[r], kept)
        for h in below:
            groups[h] = new[h]
        groups[g] = kept
    value = jnp.concatenate(groups, axis=0)
    pivot = jnp.sum(jnp.where(diagonal, value, 0.0), axis=1, keepdims=True)
    value = value * lax.rsqrt(pivot)
    second = jnp.where(lane >= 2 * WIDTH, value, 0.0)
    first = pltpu.roll(second, 2 * WIDTH, 1)
    turn_ref[0:WIDTH] = first
    turn_ref[WIDTH : 2 * WIDTH] = pair_swap(first)
    turn_ref[2 * WIDTH : 3 * WIDTH] = second
    turn_ref[3 * WIDTH :] = pair_swap(second)


def turn_kernel(*refs):
    part_refs, turn_ref = refs[:-1], refs[-1]
    packed = part_refs[0][0, TILE:]
    for ref in part_refs[1:]:
        packed = packed + ref[0, TILE:]
    packed = packed * (1.0 / IMAGES)
    value = jnp.concatenate([packed, pltpu.roll(packed, 2 * WIDTH, 1)], axis=0)
    invert_factor(jnp.where(lanes(value.shape) < 2 * WIDTH, value, 0.0), turn_ref)


def turn_of(parts):
    return pl.pallas_call(
        turn_kernel,
        out_shape=jax.ShapeDtypeStruct((TILE, TILE), jnp.float32),
        compiler_params=pltpu.CompilerParams(vmem_limit_bytes=6 * MIB),
        cost_estimate=pl.CostEstimate(flops=0, bytes_accessed=9 * MIB, transcendentals=0),
        name="turn",
    )(*parts)


def basis_kernel(image_ref, gram_ref, out_ref, turn_ref):
    packed = jnp.sum(gram_ref[...], axis=0) * (1.0 / IMAGES)
    value = jnp.concatenate(
        [packed] + [pltpu.roll(packed, TILE - WIDTH * g, 1) for g in range(1, 4)], axis=0
    )
    across = jnp.concatenate([value] + [jnp.zeros_like(value)] * 3, axis=0).T[:WIDTH]
    lane = lanes(value.shape)
    row = lax.broadcasted_iota(jnp.int32, value.shape, 0)
    real = jnp.where(lane >= row, value, across)
    imag = jnp.where(lane == row, 0.0, jnp.where(lane < row, value, -across))
    value = jnp.where(lane < WIDTH, real, 0.0)
    value = value + jnp.where((lane >= WIDTH) & (lane < 2 * WIDTH), pltpu.roll(imag, WIDTH, 1), 0.0)
    invert_factor(value, turn_ref)
    out = nt_dot(image_ref[...], turn_ref[...]).T
    for part in range(2):
        for block in range(2):
            start = (2 * block + part) * WIDTH
            out_ref[part, :, block * TILE : (block + 1) * TILE] = out[start : start + WIDTH]


def last_basis(image, grams):
    return pl.pallas_call(
        basis_kernel,
        out_shape=jax.ShapeDtypeStruct((2, WIDTH, 2 * TILE), jnp.float32),
        scratch_shapes=[pltpu.VMEM((TILE, TILE), jnp.float32)],
        compiler_params=pltpu.CompilerParams(vmem_limit_bytes=6 * MIB),
        name="basis",
    )(image, grams)


def along_x(value, step):
    return lax.ppermute(value, "row", [(i, (i + 2 * step) % 8) for i in range(8)])


def other_core(value):
    return lax.ppermute(value, "row", [(i, i ^ 1) for i in range(8)])


def to_column(value):
    return lax.all_to_all(value, "col", split_axis=0, concat_axis=0, tiled=True)


def gather_row(value):
    mine = jnp.stack([value] + [along_x(value, d) for d in (1, 2, 3)], 0)
    return mine, other_core(mine)


def reduce_row(value):
    half = value.shape[0] // 2
    mine = value[:half] + other_core(value[half:])
    return [mine[0:1]] + [along_x(mine[d : d + 1], d) for d in (1, 2, 3)]


def shards(tile_weight, tile_angle, tile_list, tile_count, init_basis):
    place = lax.axis_index("row")
    x_place, core = place // 2, place % 2
    weights = tile_weight.reshape(SLOTS, TILE, TILE)
    angles = tile_angle.reshape(SLOTS, TILE, TILE)
    listing = tile_list.reshape(SLOTS, 2)
    row_of = listing[:, 0] % ROW_BLOCKS
    col_global = listing[:, 1]
    piece = col_global // ROW_BLOCKS
    core_away = (piece % 2) ^ core
    col_from = (core_away * 4 + (x_place - piece // 2) % 4) * 2 + col_global % 2
    col_to = (core_away * 4 + (piece // 2 - x_place) % 4) * 2 + col_global % 2
    live = (jnp.arange(2)[None, :] < tile_count.reshape(SLOTS // 2, 1)).reshape(SLOTS).astype(jnp.int32)
    slots = jnp.arange(SLOTS, dtype=jnp.int32)
    earlier = slots[None, :] < slots[:, None]
    count = jnp.sum(live)
    live_before = jnp.sum(jnp.where(earlier, live[None, :], 0), axis=1)
    at = jnp.where(live > 0, live_before, count + slots - live_before)
    code = slots + SLOTS * (col_from + COL_BLOCKS * (col_to + COL_BLOCKS * row_of))
    code = jnp.sum(jnp.where(at[None, :] == slots[:, None], code[None, :], 0), axis=1)
    order = code % SLOTS
    takes_col = code // SLOTS % COL_BLOCKS
    puts_col = code // (SLOTS * COL_BLOCKS) % COL_BLOCKS
    rows = code // (SLOTS * COL_BLOCKS * COL_BLOCKS)
    count = count.reshape(1)

    row_part, col_part = degrees(row_of, col_to, live, weights)
    row_part = to_column(row_part)
    col_parts = reduce_row(col_part)
    degree = jnp.sum(row_part, axis=0) + sum(c[0] for c in col_parts)
    plain, turned, done = complex_tiles(order, count, weights, angles)
    degree = degree + done
    scale = lax.rsqrt(degree[:2])
    scale = jnp.broadcast_to(scale.T[:, :, None], (TILE, 2, 2 * WIDTH)).reshape(TILE, TILE)

    basis = jnp.transpose(init_basis.reshape(2, WIDTH, 2, TILE), (3, 2, 0, 1)).reshape(TILE, TILE)
    sent = (basis * scale).astype(jnp.bfloat16)
    body, turn = sent, None
    for rounds in range(ITERS):
        near, far = gather_row(sent)
        column = to_column(jnp.broadcast_to(body[None], (16,) + body.shape))
        forward = products(1.0, takes_col, rows, count, plain, [near, far], (16, TILE, TILE), "forward")
        mirror = products(
            -1.0, rows, puts_col, count, turned, [column], (8, body.shape[0], TILE), "mirror"
        )
        wide = to_column(forward)
        parts = reduce_row(mirror)
        if rounds > 0:
            turn = turn_of(parts)
        sent, body = new_image(wide, parts, scale, turn, rounds == ITERS - 1)
    grams = jnp.broadcast_to(body, (128, 8, TILE))
    grams = lax.all_to_all(grams, ("row", "col"), split_axis=0, concat_axis=0, tiled=True)
    return last_basis(sent, grams)


def solution(mesh):
    placed = (
        P(("row", "col"), None, None, None, None),
        P(("row", "col"), None, None, None, None),
        P(("row", "col"), None, None, None),
        P(("row", "col"), None),
        P(None, None, ("row", "col")),
    )
    return jax.shard_map(
        shards, mesh=mesh, in_specs=placed, out_specs=P(None, None, ("row", "col")), check_vma=False
    )
```

time: 299 us -> 240 us (0.80); the launches traced: 294 us -> 239 us
  local copies, waits for them, and re-layouts: 53.3 us -> 6.13 us
  blocking collectives: 0 us -> 24.8 us
  starting transfers between devices: 117 us -> 93.1 us
  Pallas kernels: 97.7 us -> 82.6 us
  waiting for transfers between devices: 20.5 us -> 27.1 us
    unnamed x29 -> x7, local copies, waits for them, and re-layouts: 47.9 us -> 0.85 us
    all_to_all x0 -> x1, blocking collectives: none -> 24.8 us  [shards(): lax.all_to_all(grams, ('row', 'col'), split_axis=0, concat_axis=0, tiled=...]
    pallas_call x3 -> x2, Pallas kernels: 19.1 us -> 3.63 us  [turn_of(): pl.pallas_call(turn_kernel, out_shape=jax.ShapeDtypeStruct((TILE, TILE),...]
    ppermute x30 -> x21, starting transfers between devices: 37.1 us -> 25.5 us  [along_x(): lax.ppermute(value, 'row', [(i, (i + 2 * step) % 8) for i in range(8)])]
    ppermute x6 -> x0, starting transfers between devices: 10.4 us -> none  [along_col(): lax.ppermute(value, 'col', [(i, (i // 4 + z_step) % 4 * 4 + (i % 4 + y_st...]
    ppermute x30 -> x21, waiting for transfers between devices: 11.1 us -> 20.2 us  [along_x(): lax.ppermute(value, 'row', [(i, (i + 2 * step) % 8) for i in range(8)])]
    ppermute x10 -> x7, starting transfers between devices: 19 us -> 15.4 us  [other_core(): return lax.ppermute(value, 'row', [(i, i ^ 1) for i in range(8)])]
    ppermute x10 -> x7, waiting for transfers between devices: 6.63 us -> 6.89 us  [other_core(): return lax.ppermute(value, 'row', [(i, i ^ 1) for i in range(8)])]
  transfers between devices with their start and end apart: 53 -> 35, of which waited for: 21 -> 23; matrix products, arithmetic and copies ran while one was open for 1% -> 1% of each run, Pallas kernels for 28% -> 29%
where the time goes in v2:
time: 240 us; the launch traced here: 239 us
  starting transfers between devices  93.1 us (39%)
  Pallas kernels  82.6 us (34%)
  waiting for transfers between devices  27.1 us (11%)
  blocking collectives  24.8 us (10%)
  local copies, waits for them, and re-layouts  6.13 us (3%)
  other arithmetic  5.16 us (2%)
    all_to_all x7, starting transfers between devices, to_column(): return lax.all_to_all(value, 'col', split_axis=0, concat_axis=0, tiled=True)  52.2 us
    pallas_call x6, Pallas kernels, products(): pl.pallas_call(functools.partial(product_kernel, sign, sizes), in_specs=[...  49.7 us
    ppermute x21, starting transfers between devices, along_x(): lax.ppermute(value, 'row', [(i, (i + 2 * step) % 8) for i in range(8)])  25.5 us
    all_to_all x1, blocking collectives, shards(): lax.all_to_all(grams, ('row', 'col'), split_axis=0, concat_axis=0, tiled=...  24.8 us
    ppermute x21, waiting for transfers between devices, along_x(): lax.ppermute(value, 'row', [(i, (i + 2 * step) % 8) for i in range(8)])  20.2 us
    pallas_call x1, Pallas kernels, complex_tiles(): pl.pallas_call(tiles_kernel, in_specs=[SCALAR, SCALAR, FAR, FAR], out_spe...  16.7 us
    ppermute x7, starting transfers between devices, other_core(): return lax.ppermute(value, 'row', [(i, i ^ 1) for i in range(8)])  15.4 us
    pallas_call x1, Pallas kernels, degrees(): pl.pallas_call(degree_kernel, in_specs=[SCALAR, SCALAR, SCALAR, FAR], out...  6.91 us
  transfers between devices with their start and end apart: 35, of which 23 were waited for; matrix products, arithmetic and copies ran while one was open for 1% of the time, Pallas kernels for 29%

profile of v2, /device:TPU:1, one launch (start us, length us, event | category | flops | bytes accessed | tf_op | source)
XLA Modules:
  0.0 239.2 jit_solution(14083405220603857200)
XLA Ops:
  3.1 6.9 %degrees.1 = (f32[16,8,128]{2,1,0:T(8,128)}, f32[8,8,128]{2,1,0:T(8,128)}) custom-call(s32[256]{0:T(256)} %get-tuple-element.50.rows_of, s32[256]{0:T(256)} %get-tuple-element.28.cols_of, s32[256]{0:T(256)} %reshape.231.live, bf16[256,128,128]{2,1,0:T(8,128)(2,1)} %bitcast.38), custom_call_target="tpu_custom_call" | custom-call | bytes 18874368 | tf_op jit(solution)/shard_map/degrees/pallas_call | solution.py:90
  12.1 8.0 %all-to-all-start = ((f32[16,8,128]{2,1,0:T(8,128)}), f32[16,8,128]{2,1,0:T(8,128)S(1)}, u32[]{:S(2)}, u32[]{:S(2)}) async-start(f32[16,8,128]{2,1,0:T(8,128)} %get-tuple-element.17), calls=%async_computation | async-start | bytes 131072 | tf_op jit(solution)/shard_map/all_to_all | solution.py:453
  23.7 2.4 collective-permute-start.2
  27.9 16.7 %complex_tiles.1 = (bf16[256,128,256]{2,1,0:T(8,128)(2,1)}, bf16[256,128,256]{2,1,0:T(8,128)(2,1)}, f32[8,128]{1,0:T(8,128)}) custom-call(s32[256]{0:T(256)} %get-tuple-element.48.order, s32[1]{0:T(128)} %bitcast.3.count, bf16[256,128,128]{2,1,0:T(8,128)(2,1)} %bitcast.39, bf16[256,128,128]{2,1,0:T(8,128)(2,1)} %bitcast.40), custom_call_target="tpu_custom_call" | custom-call | bytes 52428800 | tf_op jit(solution)/shard_map/complex_tiles/pallas_call | solution.py:173
  46.5 8.2 %all-to-all-start.2 = ((bf16[16,128,128]{2,1,0:T(8,128)(2,1)}), bf16[16,128,128]{2,1,0:T(8,128)(2,1)S(1)}, u32[]{:S(2)}, u32[]{:S(2)}) async-start(bf16[16,128,128]{2,1,0:T(8,128)(2,1)} %broadcast_in_dim.60), calls=%async_computation.2 | async-start | bytes 1048576 | tf_op jit(solution)/shard_map/all_to_all | solution.py:453
  55.2 2.1 collective-permute-start.5
  60.1 4.4 %collective-permute-start.7 = (bf16[4,128,128]{2,1,0:T(8,128)(2,1)S(1)}, bf16[4,128,128]{2,1,0:T(8,128)(2,1)S(1)}, u32[]{:S(2)}, u32[]{:S(2)}) collective-permute-start(bf16[4,128,128]{2,1,0:T(8,128)(2,1)S(1)} %pad_maximum_fusion.2.refs_0_), channel_id=1, source_target_pairs={{0,16},{16,0},{32,48},{48,32},{64,80},{80,64},{96,112},{112,96},{1... | collective-permute-start | bytes 393224 | tf_op jit(solution)/shard_map/ppermute | solution.py:449
  65.5 8.0 %forward.3 = f32[16,128,128]{2,1,0:T(8,128)} custom-call(s32[256]{0:T(256)S(1)} %get-tuple-element.49.takes, s32[256]{0:T(256)S(1)} %get-tuple-element.47.puts.takes, s32[1]{0:T(128)} %bitcast.3.count, bf16[256,128,256]{2,1,0:T(8,128)(2,1)} %get-tuple-element.16.far_ref, bf16[4,128,128]{2,1,0:T(8,128)(2,1)S(1)} %pad_maximum_fusion.2.refs_0_, ...), custom_call_target="tpu_custom_call" | custom-call | bytes 31457280 | tf_op jit(solution)/shard_map/forward/pallas_call | solution.py:242
  73.6 7.4 %all-to-all-start.1 = ((f32[16,128,128]{2,1,0:T(8,128)}), f32[16,128,128]{2,1,0:T(8,128)S(1)}, u32[]{:S(2)}, u32[]{:S(2)}) async-start(f32[16,128,128]{2,1,0:T(8,128)} %forward.3), calls=%async_computation.1 | async-start | bytes 2097152 | tf_op jit(solution)/shard_map/all_to_all | solution.py:453
  81.0 8.5 %mirror.3 = f32[8,128,128]{2,1,0:T(8,128)S(1)} custom-call(s32[256]{0:T(256)S(1)} %get-tuple-element.47.puts.takes, s32[256]{0:T(256)S(1)} %get-tuple-element.46.puts, s32[1]{0:T(128)} %bitcast.3.count, bf16[256,128,256]{2,1,0:T(8,128)(2,1)} %get-tuple-element.20.far_ref, bf16[16,128,128]{2,1,0:T(8,128)(2,1)S(1)} %all-to-all-done.2.refs_0_), custom_call_target="tpu_custom_call" | custom-call | bytes 31457280 | tf_op jit(solution)/shard_map/mirror/pallas_call | solution.py:242
  93.2 2.5 %collective-permute-start.11 = (f32[1,128,128]{2,1,0:T(8,128)S(1)}, f32[1,128,128]{2,1,0:T(8,128)S(1)}, u32[]{:S(2)}, u32[]{:S(2)}) collective-permute-start(f32[1,128,128]{2,1,0:T(8,128)S(1)} %get-tuple-element.37), channel_id=1, source_target_pairs={{0,96},{16,112},{32,0},{48,16},{64,32},{80,48},{96,64},{112,80},{1... | collective-permute-start | bytes 196616 | tf_op jit(solution)/shard_map/ppermute | solution.py:445
  98.0 2.1 collective-permute-done.9.refs_2_
  101.8 6.9 %all-to-all-start.4 = ((f32[16,144,128]{2,1,0:T(8,128)}), f32[16,144,128]{2,1,0:T(8,128)S(1)}, u32[]{:S(2)}, u32[]{:S(2)}) async-start(f32[16,144,128]{2,1,0:T(8,128)} %broadcast_in_dim.61), calls=%async_computation.4 | async-start | bytes 2359296 | tf_op jit(solution)/shard_map/all_to_all | solution.py:453
  111.5 2.3 collective-permute-done.12
  114.4 3.9 %collective-permute-start.15 = (f32[4,128,128]{2,1,0:T(8,128)S(1)}, f32[4,128,128]{2,1,0:T(8,128)S(1)}, u32[]{:S(2)}, u32[]{:S(2)}) collective-permute-start(f32[4,128,128]{2,1,0:T(8,128)S(1)} %pad_maximum_fusion.refs_0_), channel_id=1, source_target_pairs={{0,16},{16,0},{32,48},{48,32},{64,80},{80,64},{96,112},{112,96},{1... | collective-permute-start | bytes 786440 | tf_op jit(solution)/shard_map/ppermute | solution.py:449
  119.4 8.0 %forward.4 = f32[16,128,128]{2,1,0:T(8,128)} custom-call(s32[256]{0:T(256)S(1)} %get-tuple-element.49.takes, s32[256]{0:T(256)S(1)} %get-tuple-element.47.puts.takes, s32[1]{0:T(128)} %bitcast.3.count, bf16[256,128,256]{2,1,0:T(8,128)(2,1)} %get-tuple-element.16.far_ref, f32[4,128,128]{2,1,0:T(8,128)S(1)} %pad_maximum_fusion.refs_0_, ...), custom_call_target="tpu_custom_call" | custom-call | bytes 31457280 | tf_op jit(solution)/shard_map/forward/pallas_call | solution.py:242
  127.5 7.3 %all-to-all-start.3 = ((f32[16,128,128]{2,1,0:T(8,128)}), f32[16,128,128]{2,1,0:T(8,128)S(1)}, u32[]{:S(2)}, u32[]{:S(2)}) async-start(f32[16,128,128]{2,1,0:T(8,128)} %forward.4), calls=%async_computation.3 | async-start | bytes 2097152 | tf_op jit(solution)/shard_map/all_to_all | solution.py:453
  134.8 8.5 %mirror.4 = f32[8,144,128]{2,1,0:T(8,128)S(1)} custom-call(s32[256]{0:T(256)S(1)} %get-tuple-element.47.puts.takes, s32[256]{0:T(256)S(1)} %get-tuple-element.46.puts, s32[1]{0:T(128)} %bitcast.3.count, bf16[256,128,256]{2,1,0:T(8,128)(2,1)} %get-tuple-element.20.far_ref, f32[16,144,128]{2,1,0:T(8,128)S(1)} %all-to-all-done.4.refs_0_), custom_call_target="tpu_custom_call" | custom-call | bytes 31457280 | tf_op jit(solution)/shard_map/mirror/pallas_call | solution.py:242
  146.9 2.1 collective-permute-start.18
  150.2 2.6 %collective-permute-done.18.refs_2_.refs_3_ = f32[1,144,128]{2,1,0:T(8,128)S(1)} collective-permute-done((f32[1,144,128]{2,1,0:T(8,128)S(1)}, f32[1,144,128]{2,1,0:T(8,128)S(1)}, u32[]{:S(2)}, u32[]{:S(2)}) %collective-permute-start.18) | collective-permute-done | bytes 73760 | tf_op jit(solution)/shard_map/ppermute | solution.py:445
  153.1 1.8 turn.2.refs_6_
  157.0 7.0 %all-to-all-start.6 = ((f32[16,144,128]{2,1,0:T(8,128)}), f32[16,144,128]{2,1,0:T(8,128)S(1)}, u32[]{:S(2)}, u32[]{:S(2)}) async-start(f32[16,144,128]{2,1,0:T(8,128)} %broadcast_in_dim.62), calls=%async_computation.6 | async-start | bytes 2359296 | tf_op jit(solution)/shard_map/all_to_all | solution.py:453
  164.5 3.6 %collective-permute-start.21 = (f32[128,128]{1,0:T(8,128)S(1)}, f32[128,128]{1,0:T(8,128)S(1)}, u32[]{:S(2)}, u32[]{:S(2)}) collective-permute-start(f32[128,128]{1,0:T(8,128)S(1)} %get-tuple-element.23), channel_id=1, source_target_pairs={{0,64},{16,80},{32,96},{48,112},{64,0},{80,16},{96,32},{112,48},{1... | collective-permute-start | bytes 196616 | tf_op jit(solution)/shard_map/ppermute | solution.py:445
  168.6 1.9 collective-permute-done.21
  172.0 2.2 collective-permute-start.23
  175.3 8.0 %forward.5 = f32[16,128,128]{2,1,0:T(8,128)} custom-call(s32[256]{0:T(256)S(1)} %get-tuple-element.49.takes, s32[256]{0:T(256)S(1)} %get-tuple-element.47.puts.takes, s32[1]{0:T(128)} %bitcast.3.count, bf16[256,128,256]{2,1,0:T(8,128)(2,1)} %get-tuple-element.16.far_ref, f32[4,128,128]{2,1,0:T(8,128)S(1)} %pad_maximum_fusion.1.refs_0_, ...), custom_call_target="tpu_custom_call" | custom-call | bytes 31457280 | tf_op jit(solution)/shard_map/forward/pallas_call | solution.py:242
  183.4 7.3 %all-to-all-start.5 = ((f32[16,128,128]{2,1,0:T(8,128)}), f32[16,128,128]{2,1,0:T(8,128)S(1)}, u32[]{:S(2)}, u32[]{:S(2)}) async-start(f32[16,128,128]{2,1,0:T(8,128)} %forward.5), calls=%async_computation.5 | async-start | bytes 2097152 | tf_op jit(solution)/shard_map/all_to_all | solution.py:453
  190.7 8.7 %mirror.5 = f32[8,144,128]{2,1,0:T(8,128)S(1)} custom-call(s32[256]{0:T(256)S(1)} %get-tuple-element.47.puts.takes, s32[256]{0:T(256)S(1)} %get-tuple-element.46.puts, s32[1]{0:T(128)} %bitcast.3.count, bf16[256,128,256]{2,1,0:T(8,128)(2,1)} %get-tuple-element.20.far_ref, f32[16,144,128]{2,1,0:T(8,128)S(1)} %all-to-all-done.6.refs_0_), custom_call_target="tpu_custom_call" | custom-call | bytes 31457280 | tf_op jit(solution)/shard_map/mirror/pallas_call | solution.py:242
  202.0 2.5 %collective-permute-start.26 = (f32[1,144,128]{2,1,0:T(8,128)S(1)}, f32[1,144,128]{2,1,0:T(8,128)S(1)}, u32[]{:S(2)}, u32[]{:S(2)}) collective-permute-start(f32[1,144,128]{2,1,0:T(8,128)S(1)} %get-tuple-element.30), channel_id=1, source_target_pairs={{0,64},{16,80},{32,96},{48,112},{64,0},{80,16},{96,32},{112,48},{1... | collective-permute-start | bytes 221192 | tf_op jit(solution)/shard_map/ppermute | solution.py:445
  206.4 1.9 collective-permute-done.26.refs_2_.refs_3_
  211.4 24.8 %all_to_all.40.gram_ref = f32[128,8,128]{2,1,0:T(8,128)S(1)} all-to-all(f32[128,8,128]{2,1,0:T(8,128)S(1)} %broadcast_in_dim.64), channel_id=1, replica_groups=mesh['row'=8,'col'=16] {'row','col'}, dimensions={0} | all-to-all | bytes 1048576 | tf_op jit(solution)/shard_map/all_to_all | solution.py:518
  236.2 3.1 %basis.1 = f32[2,32,256]{2,1,0:T(8,128)} custom-call(f32[128,128]{1,0:T(8,128)S(1)} %get-tuple-element.25.image_ref, f32[128,8,128]{2,1,0:T(8,128)S(1)} %all_to_all.40.gram_ref), custom_call_target="tpu_custom_call" | custom-call | tf_op jit(solution)/shard_map/basis/pallas_call | solution.py:435
  (101 shorter events, 47.1 us)
Async XLA Ops:
  10.7 11.0 %collective-permute-start = (f32[4,8,128]{2,1,0:T(8,128)S(1)}, f32[4,8,128]{2,1,0:T(8,128)S(1)}, u32[]{:S(2)}, u32[]{:S(2)}) collective-permute-start(f32[4,8,128]{2,1,0:T(8,128)S(1)} %slice.84), channel_id=1, source_target_pairs={{0,16},{16,0},{32,48},{48,32},{64,80},{80,64},{96,112},{112,96},{1... | collective-permute-start | bytes 49160 | tf_op jit(solution)/shard_map/ppermute | solution.py:449
  12.1 32.6 %all-to-all-start = ((f32[16,8,128]{2,1,0:T(8,128)}), f32[16,8,128]{2,1,0:T(8,128)S(1)}, u32[]{:S(2)}, u32[]{:S(2)}) async-start(f32[16,8,128]{2,1,0:T(8,128)} %get-tuple-element.17), calls=%async_computation | async-start | bytes 131072 | tf_op jit(solution)/shard_map/all_to_all | solution.py:453
  22.5 22.2 %collective-permute-start.1 = (f32[1,8,128]{2,1,0:T(8,128)S(1)}, f32[1,8,128]{2,1,0:T(8,128)S(1)}, u32[]{:S(2)}, u32[]{:S(2)}) collective-permute-start(f32[1,8,128]{2,1,0:T(8,128)S(1)} %get-tuple-element.41), channel_id=1, source_target_pairs={{0,32},{16,48},{32,64},{48,80},{64,96},{80,112},{96,0},{112,16},{1... | collective-permute-start | bytes 12296 | tf_op jit(solution)/shard_map/ppermute | solution.py:445
  23.7 21.0 %collective-permute-start.2 = (f32[1,8,128]{2,1,0:T(8,128)S(1)}, f32[1,8,128]{2,1,0:T(8,128)S(1)}, u32[]{:S(2)}, u32[]{:S(2)}) collective-permute-start(f32[1,8,128]{2,1,0:T(8,128)S(1)} %get-tuple-element.43), channel_id=1, source_target_pairs={{0,64},{16,80},{32,96},{48,112},{64,0},{80,16},{96,32},{112,48},{1... | collective-permute-start | bytes 12296 | tf_op jit(solution)/shard_map/ppermute | solution.py:445
  26.1 18.6 %collective-permute-start.3 = (f32[1,8,128]{2,1,0:T(8,128)S(1)}, f32[1,8,128]{2,1,0:T(8,128)S(1)}, u32[]{:S(2)}, u32[]{:S(2)}) collective-permute-start(f32[1,8,128]{2,1,0:T(8,128)S(1)} %get-tuple-element.42), channel_id=1, source_target_pairs={{0,96},{16,112},{32,0},{48,16},{64,32},{80,48},{96,64},{112,80},{1... | collective-permute-start | bytes 12296 | tf_op jit(solution)/shard_map/ppermute | solution.py:445
  46.5 27.1 %all-to-all-start.2 = ((bf16[16,128,128]{2,1,0:T(8,128)(2,1)}), bf16[16,128,128]{2,1,0:T(8,128)(2,1)S(1)}, u32[]{:S(2)}, u32[]{:S(2)}) async-start(bf16[16,128,128]{2,1,0:T(8,128)(2,1)} %broadcast_in_dim.60), calls=%async_computation.2 | async-start | bytes 1048576 | tf_op jit(solution)/shard_map/all_to_all | solution.py:453
  54.8 4.0 %collective-permute-start.4 = (bf16[128,128]{1,0:T(8,128)(2,1)S(1)}, bf16[128,128]{1,0:T(8,128)(2,1)S(1)}, u32[]{:S(2)}, u32[]{:S(2)}) collective-permute-start(bf16[128,128]{1,0:T(8,128)(2,1)S(1)} %multiply_convert_fusion), channel_id=1, source_target_pairs={{0,32},{16,48},{32,64},{48,80},{64,96},{80,112},{96,0},{112,16},{1... | collective-permute-start | bytes 98312 | tf_op jit(solution)/shard_map/ppermute | solution.py:445
  55.2 4.5 %collective-permute-start.5 = (bf16[128,128]{1,0:T(8,128)(2,1)S(1)}, bf16[128,128]{1,0:T(8,128)(2,1)S(1)}, u32[]{:S(2)}, u32[]{:S(2)}) collective-permute-start(bf16[128,128]{1,0:T(8,128)(2,1)S(1)} %multiply_convert_fusion), channel_id=1, source_target_pairs={{0,64},{16,80},{32,96},{48,112},{64,0},{80,16},{96,32},{112,48},{1... | collective-permute-start | bytes 98312 | tf_op jit(solution)/shard_map/ppermute | solution.py:445
  57.3 2.8 %collective-permute-start.6 = (bf16[128,128]{1,0:T(8,128)(2,1)S(1)}, bf16[128,128]{1,0:T(8,128)(2,1)S(1)}, u32[]{:S(2)}, u32[]{:S(2)}) collective-permute-start(bf16[128,128]{1,0:T(8,128)(2,1)S(1)} %multiply_convert_fusion), channel_id=1, source_target_pairs={{0,96},{16,112},{32,0},{48,16},{64,32},{80,48},{96,64},{112,80},{1... | collective-permute-start | bytes 98312 | tf_op jit(solution)/shard_map/ppermute | solution.py:445
  60.1 5.4 %collective-permute-start.7 = (bf16[4,128,128]{2,1,0:T(8,128)(2,1)S(1)}, bf16[4,128,128]{2,1,0:T(8,128)(2,1)S(1)}, u32[]{:S(2)}, u32[]{:S(2)}) collective-permute-start(bf16[4,128,128]{2,1,0:T(8,128)(2,1)S(1)} %pad_maximum_fusion.2.refs_0_), channel_id=1, source_target_pairs={{0,16},{16,0},{32,48},{48,32},{64,80},{80,64},{96,112},{112,96},{1... | collective-permute-start | bytes 393224 | tf_op jit(solution)/shard_map/ppermute | solution.py:449
  73.6 26.5 %all-to-all-start.1 = ((f32[16,128,128]{2,1,0:T(8,128)}), f32[16,128,128]{2,1,0:T(8,128)S(1)}, u32[]{:S(2)}, u32[]{:S(2)}) async-start(f32[16,128,128]{2,1,0:T(8,128)} %forward.3), calls=%async_computation.1 | async-start | bytes 2097152 | tf_op jit(solution)/shard_map/all_to_all | solution.py:453
  91.9 4.7 %collective-permute-start.10 = (f32[1,128,128]{2,1,0:T(8,128)S(1)}, f32[1,128,128]{2,1,0:T(8,128)S(1)}, u32[]{:S(2)}, u32[]{:S(2)}) collective-permute-start(f32[1,128,128]{2,1,0:T(8,128)S(1)} %get-tuple-element.38), channel_id=1, source_target_pairs={{0,64},{16,80},{32,96},{48,112},{64,0},{80,16},{96,32},{112,48},{1... | collective-permute-start | bytes 196616 | tf_op jit(solution)/shard_map/ppermute | solution.py:445
  93.2 4.8 %collective-permute-start.11 = (f32[1,128,128]{2,1,0:T(8,128)S(1)}, f32[1,128,128]{2,1,0:T(8,128)S(1)}, u32[]{:S(2)}, u32[]{:S(2)}) collective-permute-start(f32[1,128,128]{2,1,0:T(8,128)S(1)} %get-tuple-element.37), channel_id=1, source_target_pairs={{0,96},{16,112},{32,0},{48,16},{64,32},{80,48},{96,64},{112,80},{1... | collective-permute-start | bytes 196616 | tf_op jit(solution)/shard_map/ppermute | solution.py:445
  95.7 4.3 %collective-permute-start.9 = (f32[1,128,128]{2,1,0:T(8,128)S(1)}, f32[1,128,128]{2,1,0:T(8,128)S(1)}, u32[]{:S(2)}, u32[]{:S(2)}) collective-permute-start(f32[1,128,128]{2,1,0:T(8,128)S(1)} %get-tuple-element.39), channel_id=1, source_target_pairs={{0,32},{16,48},{32,64},{48,80},{64,96},{80,112},{96,0},{112,16},{1... | collective-permute-start | bytes 196616 | tf_op jit(solution)/shard_map/ppermute | solution.py:445
  101.8 25.7 %all-to-all-start.4 = ((f32[16,144,128]{2,1,0:T(8,128)}), f32[16,144,128]{2,1,0:T(8,128)S(1)}, u32[]{:S(2)}, u32[]{:S(2)}) async-start(f32[16,144,128]{2,1,0:T(8,128)} %broadcast_in_dim.61), calls=%async_computation.4 | async-start | bytes 2359296 | tf_op jit(solution)/shard_map/all_to_all | solution.py:453
  108.7 5.1 %collective-permute-start.12 = (f32[128,128]{1,0:T(8,128)S(1)}, f32[128,128]{1,0:T(8,128)S(1)}, u32[]{:S(2)}, u32[]{:S(2)}) collective-permute-start(f32[128,128]{1,0:T(8,128)S(1)} %get-tuple-element.21), channel_id=1, source_target_pairs={{0,32},{16,48},{32,64},{48,80},{64,96},{80,112},{96,0},{112,16},{1... | collective-permute-start | bytes 196616 | tf_op jit(solution)/shard_map/ppermute | solution.py:445
  108.8 5.0 %collective-permute-start.13 = (f32[128,128]{1,0:T(8,128)S(1)}, f32[128,128]{1,0:T(8,128)S(1)}, u32[]{:S(2)}, u32[]{:S(2)}) collective-permute-start(f32[128,128]{1,0:T(8,128)S(1)} %get-tuple-element.21), channel_id=1, source_target_pairs={{0,64},{16,80},{32,96},{48,112},{64,0},{80,16},{96,32},{112,48},{1... | collective-permute-start | bytes 196616 | tf_op jit(solution)/shard_map/ppermute | solution.py:445
  110.4 4.0 %collective-permute-start.14 = (f32[128,128]{1,0:T(8,128)S(1)}, f32[128,128]{1,0:T(8,128)S(1)}, u32[]{:S(2)}, u32[]{:S(2)}) collective-permute-start(f32[128,128]{1,0:T(8,128)S(1)} %get-tuple-element.21), channel_id=1, source_target_pairs={{0,96},{16,112},{32,0},{48,16},{64,32},{80,48},{96,64},{112,80},{1... | collective-permute-start | bytes 196616 | tf_op jit(solution)/shard_map/ppermute | solution.py:445
  114.4 5.0 %collective-permute-start.15 = (f32[4,128,128]{2,1,0:T(8,128)S(1)}, f32[4,128,128]{2,1,0:T(8,128)S(1)}, u32[]{:S(2)}, u32[]{:S(2)}) collective-permute-start(f32[4,128,128]{2,1,0:T(8,128)S(1)} %pad_maximum_fusion.refs_0_), channel_id=1, source_target_pairs={{0,16},{16,0},{32,48},{48,32},{64,80},{80,64},{96,112},{112,96},{1... | collective-permute-start | bytes 786440 | tf_op jit(solution)/shard_map/ppermute | solution.py:449
  127.5 27.5 %all-to-all-start.3 = ((f32[16,128,128]{2,1,0:T(8,128)}), f32[16,128,128]{2,1,0:T(8,128)S(1)}, u32[]{:S(2)}, u32[]{:S(2)}) async-start(f32[16,128,128]{2,1,0:T(8,128)} %forward.4), calls=%async_computation.3 | async-start | bytes 2097152 | tf_op jit(solution)/shard_map/all_to_all | solution.py:453
  145.8 4.5 %collective-permute-start.17 = (f32[1,144,128]{2,1,0:T(8,128)S(1)}, f32[1,144,128]{2,1,0:T(8,128)S(1)}, u32[]{:S(2)}, u32[]{:S(2)}) collective-permute-start(f32[1,144,128]{2,1,0:T(8,128)S(1)} %get-tuple-element.35), channel_id=1, source_target_pairs={{0,32},{16,48},{32,64},{48,80},{64,96},{80,112},{96,0},{112,16},{1... | collective-permute-start | bytes 221192 | tf_op jit(solution)/shard_map/ppermute | solution.py:445
  146.9 6.0 %collective-permute-start.18 = (f32[1,144,128]{2,1,0:T(8,128)S(1)}, f32[1,144,128]{2,1,0:T(8,128)S(1)}, u32[]{:S(2)}, u32[]{:S(2)}) collective-permute-start(f32[1,144,128]{2,1,0:T(8,128)S(1)} %get-tuple-element.34), channel_id=1, source_target_pairs={{0,64},{16,80},{32,96},{48,112},{64,0},{80,16},{96,32},{112,48},{1... | collective-permute-start | bytes 221192 | tf_op jit(solution)/shard_map/ppermute | solution.py:445
  149.0 4.2 %collective-permute-start.19 = (f32[1,144,128]{2,1,0:T(8,128)S(1)}, f32[1,144,128]{2,1,0:T(8,128)S(1)}, u32[]{:S(2)}, u32[]{:S(2)}) collective-permute-start(f32[1,144,128]{2,1,0:T(8,128)S(1)} %get-tuple-element.33), channel_id=1, source_target_pairs={{0,96},{16,112},{32,0},{48,16},{64,32},{80,48},{96,64},{112,80},{1... | collective-permute-start | bytes 221192 | tf_op jit(solution)/shard_map/ppermute | solution.py:445
  157.0 26.3 %all-to-all-start.6 = ((f32[16,144,128]{2,1,0:T(8,128)}), f32[16,144,128]{2,1,0:T(8,128)S(1)}, u32[]{:S(2)}, u32[]{:S(2)}) async-start(f32[16,144,128]{2,1,0:T(8,128)} %broadcast_in_dim.62), calls=%async_computation.6 | async-start | bytes 2359296 | tf_op jit(solution)/shard_map/all_to_all | solution.py:453
  164.1 4.6 %collective-permute-start.20 = (f32[128,128]{1,0:T(8,128)S(1)}, f32[128,128]{1,0:T(8,128)S(1)}, u32[]{:S(2)}, u32[]{:S(2)}) collective-permute-start(f32[128,128]{1,0:T(8,128)S(1)} %get-tuple-element.23), channel_id=1, source_target_pairs={{0,32},{16,48},{32,64},{48,80},{64,96},{80,112},{96,0},{112,16},{1... | collective-permute-start | bytes 196616 | tf_op jit(solution)/shard_map/ppermute | solution.py:445
  164.5 6.0 %collective-permute-start.21 = (f32[128,128]{1,0:T(8,128)S(1)}, f32[128,128]{1,0:T(8,128)S(1)}, u32[]{:S(2)}, u32[]{:S(2)}) collective-permute-start(f32[128,128]{1,0:T(8,128)S(1)} %get-tuple-element.23), channel_id=1, source_target_pairs={{0,64},{16,80},{32,96},{48,112},{64,0},{80,16},{96,32},{112,48},{1... | collective-permute-start | bytes 196616 | tf_op jit(solution)/shard_map/ppermute | solution.py:445
  168.2 3.8 %collective-permute-start.22 = (f32[128,128]{1,0:T(8,128)S(1)}, f32[128,128]{1,0:T(8,128)S(1)}, u32[]{:S(2)}, u32[]{:S(2)}) collective-permute-start(f32[128,128]{1,0:T(8,128)S(1)} %get-tuple-element.23), channel_id=1, source_target_pairs={{0,96},{16,112},{32,0},{48,16},{64,32},{80,48},{96,64},{112,80},{1... | collective-permute-start | bytes 196616 | tf_op jit(solution)/shard_map/ppermute | solution.py:445
  172.0 3.4 %collective-permute-start.23 = (f32[4,128,128]{2,1,0:T(8,128)S(1)}, f32[4,128,128]{2,1,0:T(8,128)S(1)}, u32[]{:S(2)}, u32[]{:S(2)}) collective-permute-start(f32[4,128,128]{2,1,0:T(8,128)S(1)} %pad_maximum_fusion.1.refs_0_), channel_id=1, source_target_pairs={{0,16},{16,0},{32,48},{48,32},{64,80},{80,64},{96,112},{112,96},{1... | collective-permute-start | bytes 786440 | tf_op jit(solution)/shard_map/ppermute | solution.py:449
  183.4 26.9 %all-to-all-start.5 = ((f32[16,128,128]{2,1,0:T(8,128)}), f32[16,128,128]{2,1,0:T(8,128)S(1)}, u32[]{:S(2)}, u32[]{:S(2)}) async-start(f32[16,128,128]{2,1,0:T(8,128)} %forward.5), calls=%async_computation.5 | async-start | bytes 2097152 | tf_op jit(solution)/shard_map/all_to_all | solution.py:453
  201.9 4.5 %collective-permute-start.25 = (f32[1,144,128]{2,1,0:T(8,128)S(1)}, f32[1,144,128]{2,1,0:T(8,128)S(1)}, u32[]{:S(2)}, u32[]{:S(2)}) collective-permute-start(f32[1,144,128]{2,1,0:T(8,128)S(1)} %get-tuple-element.31), channel_id=1, source_target_pairs={{0,32},{16,48},{32,64},{48,80},{64,96},{80,112},{96,0},{112,16},{1... | collective-permute-start | bytes 221192 | tf_op jit(solution)/shard_map/ppermute | solution.py:445
  202.0 6.3 %collective-permute-start.26 = (f32[1,144,128]{2,1,0:T(8,128)S(1)}, f32[1,144,128]{2,1,0:T(8,128)S(1)}, u32[]{:S(2)}, u32[]{:S(2)}) collective-permute-start(f32[1,144,128]{2,1,0:T(8,128)S(1)} %get-tuple-element.30), channel_id=1, source_target_pairs={{0,64},{16,80},{32,96},{48,112},{64,0},{80,16},{96,32},{112,48},{1... | collective-permute-start | bytes 221192 | tf_op jit(solution)/shard_map/ppermute | solution.py:445
  204.4 4.0 %collective-permute-start.27 = (f32[1,144,128]{2,1,0:T(8,128)S(1)}, f32[1,144,128]{2,1,0:T(8,128)S(1)}, u32[]{:S(2)}, u32[]{:S(2)}) collective-permute-start(f32[1,144,128]{2,1,0:T(8,128)S(1)} %get-tuple-element.29), channel_id=1, source_target_pairs={{0,96},{16,112},{32,0},{48,16},{64,32},{80,48},{96,64},{112,80},{1... | collective-permute-start | bytes 221192 | tf_op jit(solution)/shard_map/ppermute | solution.py:445
  (6 other events, 72.7 us)

commit v3 on v2

--- a/solution.py
+++ b/solution.py
@@ -16,7 +16,6 @@
 COL_BLOCKS = 16
 CHUNK = 16
 TRIG_CHUNK = 8
-RING = 4
 HALF_SIN = (0.5, -0.020833322778344154, 0.00026040783268399537, -1.5475804957532091e-06, 5.088141019626846e-09)
 HALF_COS = (0.9999999403953552, -0.1249997615814209, 0.0026039734948426485, -2.164632678613998e-05, 9.044046578310372e-08)
 HIGHEST = lax.Precision.HIGHEST
@@ -59,144 +58,109 @@
     lax.fori_loop(0, chunks, start, 0)
 
 
-def degree_kernel(rows_of, cols_of, live, far_ref, row_ref, col_ref, row_acc, col_acc, w_ref, sems):
-    start_fetches(far_ref, w_ref, sems, SLOTS // CHUNK)
+def tiles_kernel(
+    order, rows, cols, count, far_w, far_a, far_plain, far_turned, row_ref, col_ref,
+    w_ref, a_ref, plain, turned, row_acc, col_acc, w_sems, a_sems, out_sems,
+):
+    def start(c, carry):
+        fetch(far_w, w_ref, w_sems, c).start()
+        fetch(far_a, a_ref, a_sems, c).start()
+        return carry
+
+    lax.fori_loop(0, SLOTS // CHUNK, start, 0)
     row_acc[...] = jnp.zeros_like(row_acc)
     col_acc[...] = jnp.zeros_like(col_acc)
-
-    def step(c, carry):
-        fetch(far_ref, w_ref, sems, c).wait()
-        for u in range(CHUNK):
-            slot = c * CHUNK + u
-
-            @pl.when(live[slot] > 0)
-            def _():
-                w = w_ref[slot].astype(jnp.float32)
-                row_acc[rows_of[slot]] += w
-                col_acc[cols_of[slot]] += jnp.sum(w.reshape(TILE // 8, 8, TILE), axis=0)
-
+    chunks = pl.cdiv(count[0], CHUNK) * (CHUNK // TRIG_CHUNK)
+
+    def outgoing(c):
+        part = pl.ds(c * TRIG_CHUNK, TRIG_CHUNK)
+        yield pltpu.make_async_copy(plain.at[c % 2], far_plain.at[part], out_sems.at[c % 2, 0])
+        yield pltpu.make_async_copy(turned.at[c % 2], far_turned.at[part], out_sems.at[c % 2, 1])
+
+    def arrive(c, carry):
+        fetch(far_w, w_ref, w_sems, c).wait()
+        fetch(far_a, a_ref, a_sems, c).wait()
         return carry
 
-    lax.fori_loop(0, SLOTS // CHUNK, step, 0)
+    def step(c, here):
+        reach = order[c * TRIG_CHUNK + TRIG_CHUNK - 1] // CHUNK + 1
+        need = jnp.where(c >= chunks - CHUNK // TRIG_CHUNK, SLOTS // CHUNK, reach)
+        lax.fori_loop(here, need, arrive, 0)
+
+        @pl.when(c >= 2)
+        def _():
+            for copy in outgoing(c - 2):
+                copy.wait()
+
+        side = c % 2
+        for u in range(TRIG_CHUNK):
+            slot = c * TRIG_CHUNK + u
+            source = order[slot]
+            theta = a_ref[source].astype(jnp.float32)
+            w = w_ref[source].astype(jnp.float32)
+            square = theta * theta
+            sine = theta * horner(square, HALF_SIN)
+            cosine = horner(square, HALF_COS)
+            part = w * sine
+            real = (0.5 * w - part * sine).astype(jnp.bfloat16)
+            imag = (part * cosine).astype(jnp.bfloat16)
+            plain[side, u, :, :TILE] = real
+            plain[side, u, :, TILE:] = imag
+            turned[side, u, :, :TILE] = real.T
+            turned[side, u, :, TILE:] = imag.T
+            row_acc[rows[slot]] += w
+            col_acc[cols[slot]] += jnp.sum(w.reshape(TILE // 8, 8, TILE), axis=0)
+        for copy in outgoing(c):
+            copy.start()
+        return need
+
+    lax.fori_loop(0, chunks, step, 0)
     for p in range(ROW_BLOCKS // 2):
         sums = [jnp.sum(row_acc[2 * p + k].T, axis=0, keepdims=True) for k in range(2)]
         row_ref[p] = 0.5 * jnp.concatenate(sums * 4, axis=0)
     for p in range(COL_BLOCKS // 2):
         sums = [jnp.sum(col_acc[2 * p + k], axis=0, keepdims=True) for k in range(2)]
         col_ref[p] = 0.5 * jnp.concatenate(sums * 4, axis=0)
-
-
-def degrees(rows_of, cols_of, live, weights):
+    for back in (2, 1):
+        for copy in outgoing(chunks - back):
+            copy.wait()
+
+
+def complex_tiles(order, rows, cols, count, weights, angles):
     return pl.pallas_call(
-        degree_kernel,
-        in_specs=[SCALAR, SCALAR, SCALAR, FAR],
-        out_specs=[VECTOR, VECTOR],
-        scratch_shapes=[
-            pltpu.VMEM((ROW_BLOCKS, TILE, TILE), jnp.float32),
-            pltpu.VMEM((COL_BLOCKS, 8, TILE), jnp.float32),
-            pltpu.VMEM((SLOTS, TILE, TILE), jnp.bfloat16),
-            pltpu.SemaphoreType.DMA((SLOTS // CHUNK,)),
-        ],
-        out_shape=[
+        tiles_kernel,
+        in_specs=[SCALAR] * 4 + [FAR, FAR],
+        out_specs=[FAR, FAR, VECTOR, VECTOR],
+        out_shape=[jax.ShapeDtypeStruct((SLOTS, TILE, 2 * TILE), jnp.bfloat16)] * 2
+        + [
             jax.ShapeDtypeStruct((ROW_BLOCKS // 2, 8, TILE), jnp.float32),
             jax.ShapeDtypeStruct((COL_BLOCKS // 2, 8, TILE), jnp.float32),
         ],
-        compiler_params=pltpu.CompilerParams(vmem_limit_bytes=58 * MIB),
-        cost_estimate=pl.CostEstimate(flops=0, bytes_accessed=18 * MIB, transcendentals=0),
-        name="degrees",
-    )(rows_of, cols_of, live, weights)
-
-
-def tiles_kernel(
-    order, count, far_w, far_a, far_plain, far_turned, done_ref, w_buf, a_buf, plain, turned, in_sems, out_sems
-):
-    done_ref[...] = jnp.zeros_like(done_ref)
-    chunks = pl.cdiv(count[0], CHUNK) * (CHUNK // TRIG_CHUNK)
-
-    def incoming(c):
-        ring = c % RING
-        for u in range(TRIG_CHUNK):
-            source = order[c * TRIG_CHUNK + u]
-            yield pltpu.make_async_copy(far_w.at[source], w_buf.at[ring, u], in_sems.at[ring, 0, u])
-            yield pltpu.make_async_copy(far_a.at[source], a_buf.at[ring, u], in_sems.at[ring, 1, u])
-
-    def outgoing(c):
-        part = pl.ds(c * TRIG_CHUNK, TRIG_CHUNK)
-        yield pltpu.make_async_copy(plain.at[c % 2], far_plain.at[part], out_sems.at[c % 2, 0])
-        yield pltpu.make_async_copy(turned.at[c % 2], far_turned.at[part], out_sems.at[c % 2, 1])
-
-    def begin(c):
-        @pl.when(c < chunks)
-        def _():
-            for copy in incoming(c):
-                copy.start()
-
-    for c in range(RING - 1):
-        begin(jnp.int32(c))
-
-    def step(c, carry):
-        begin(c + RING - 1)
-        for copy in incoming(c):
-            copy.wait()
-
-        @pl.when(c >= 2)
-        def _():
-            for copy in outgoing(c - 2):
-                copy.wait()
-
-        ring, side = c % RING, c % 2
-        for u in range(TRIG_CHUNK):
-            half = jnp.where(c * TRIG_CHUNK + u < count[0], 0.5, 0.0).astype(jnp.float32)
-            theta = a_buf[ring, u].astype(jnp.float32)
-            w = w_buf[ring, u].astype(jnp.float32) * half
-            square = theta * theta
-            sine = theta * horner(square, HALF_SIN)
-            cosine = horner(square, HALF_COS)
-            part = (w + w) * sine
-            real = w - part * sine
-            imag = part * cosine
-            plain[side, u, :, :TILE] = real.astype(jnp.bfloat16)
-            plain[side, u, :, TILE:] = imag.astype(jnp.bfloat16)
-            turned[side, u, :, :TILE] = real.T.astype(jnp.bfloat16)
-            turned[side, u, :, TILE:] = imag.T.astype(jnp.bfloat16)
-        for copy in outgoing(c):
-            copy.start()
-        return carry
-
-    lax.fori_loop(0, chunks, step, 0)
-    for back in (2, 1):
-        for copy in outgoing(chunks - back):
-            copy.wait()
-
-
-def complex_tiles(order, count, weights, angles):
-    return pl.pallas_call(
-        tiles_kernel,
-        in_specs=[SCALAR, SCALAR, FAR, FAR],
-        out_specs=[FAR, FAR, VECTOR],
-        out_shape=[jax.ShapeDtypeStruct((SLOTS, TILE, 2 * TILE), jnp.bfloat16)] * 2
-        + [jax.ShapeDtypeStruct((8, TILE), jnp.float32)],
         scratch_shapes=[
-            pltpu.VMEM((RING, TRIG_CHUNK, TILE, TILE), jnp.bfloat16),
-            pltpu.VMEM((RING, TRIG_CHUNK, TILE, TILE), jnp.bfloat16),
+            pltpu.VMEM((SLOTS, TILE, TILE), jnp.bfloat16),
+            pltpu.VMEM((SLOTS, TILE, TILE), jnp.bfloat16),
             pltpu.VMEM((2, TRIG_CHUNK, TILE, 2 * TILE), jnp.bfloat16),
             pltpu.VMEM((2, TRIG_CHUNK, TILE, 2 * TILE), jnp.bfloat16),
-            pltpu.SemaphoreType.DMA((RING, 2, TRIG_CHUNK)),
+            pltpu.VMEM((ROW_BLOCKS + 1, TILE, TILE), jnp.float32),
+            pltpu.VMEM((COL_BLOCKS + 1, 8, TILE), jnp.float32),
+            pltpu.SemaphoreType.DMA((SLOTS // CHUNK,)),
+            pltpu.SemaphoreType.DMA((SLOTS // CHUNK,)),
             pltpu.SemaphoreType.DMA((2, 2)),
         ],
         compiler_params=pltpu.CompilerParams(vmem_limit_bytes=58 * MIB),
         cost_estimate=pl.CostEstimate(flops=0, bytes_accessed=50 * MIB, transcendentals=0),
         name="complex_tiles",
-    )(order, count, weights, angles)
-
-
-def product_kernel(sign, sizes, takes, puts, count, far_ref, *refs):
+    )(order, rows, cols, count, weights, angles)
+
+
+def product_kernel(sign, sizes, apart, takes, puts, count, far_ref, *refs):
     x_refs = refs[: len(sizes)]
-    out_ref, x_mat, acc, tiles_ref, sems = refs[len(sizes) :]
+    out_ref, x_mat, acc, tiles_ref, sems = refs[len(sizes) :][:5]
     chunks = pl.cdiv(count[0], CHUNK)
     start_fetches(far_ref, tiles_ref, sems, chunks)
     low = lanes((TILE, TILE)) < 2 * WIDTH
     acc[...] = jnp.zeros_like(acc)
+    x_mat[2 * sum(sizes)] = jnp.zeros_like(x_mat[0])
     base = 0
     for x_ref, size in zip(x_refs, sizes):
         for p in range(size):
@@ -222,33 +186,41 @@
         return carry
 
     lax.fori_loop(0, chunks, step, 0)
+    near, out_sems = refs[len(sizes) :][5:] if apart else (out_ref, None)
     if out_ref.shape[1] > TILE:
-        gram = x_refs[0][0, TILE:]
-        for p in range(1, sizes[0]):
-            gram = gram + x_refs[0][p, TILE:]
+        gram = sum(x_ref[p, TILE:] for x_ref, size in zip(x_refs, sizes) for p in range(size))
+    copies = []
     for p in range(out_ref.shape[0]):
         if out_ref.shape[1] > TILE:
-            out_ref[p, TILE:] = gram
+            near[p, TILE:] = gram
         first, second = acc[2 * p], acc[2 * p + 1]
-        out_ref[p, :TILE] = jnp.where(
+        near[p, :TILE] = jnp.where(
             low,
             first + pltpu.roll(first, 2 * WIDTH, 1),
             second + pltpu.roll(second, 2 * WIDTH, 1),
         )
-
-
-def products(sign, takes, puts, count, tiles, sources, out_shape, name):
+        if apart:
+            copies.append(pltpu.make_async_copy(near.at[p], out_ref.at[p], out_sems.at[p]))
+            copies[-1].start()
+    for copy in copies:
+        copy.wait()
+
+
+def products(sign, takes, puts, count, tiles, sources, out_shape, apart, name):
     sizes = tuple(s.shape[0] for s in sources)
+    scratch = [
+        pltpu.VMEM((2 * sum(sizes) + 1, 2 * TILE, TILE), jnp.bfloat16),
+        pltpu.VMEM((2 * out_shape[0] + 1, TILE, TILE), jnp.float32),
+        pltpu.VMEM((SLOTS, TILE, 2 * TILE), jnp.bfloat16),
+        pltpu.SemaphoreType.DMA((SLOTS // CHUNK,)),
+    ]
+    if apart:
+        scratch += [pltpu.VMEM(out_shape, jnp.float32), pltpu.SemaphoreType.DMA((out_shape[0],))]
     return pl.pallas_call(
-        functools.partial(product_kernel, sign, sizes),
+        functools.partial(product_kernel, sign, sizes, apart),
         in_specs=[SCALAR, SCALAR, SCALAR, FAR] + [VECTOR] * len(sources),
-        out_specs=VECTOR,
-        scratch_shapes=[
-            pltpu.VMEM((2 * sum(sizes), 2 * TILE, TILE), jnp.bfloat16),
-            pltpu.VMEM((2 * out_shape[0], TILE, TILE), jnp.float32),
-            pltpu.VMEM((SLOTS, TILE, 2 * TILE), jnp.bfloat16),
-            pltpu.SemaphoreType.DMA((SLOTS // CHUNK,)),
-        ],
+        out_specs=FAR if apart else VECTOR,
+        scratch_shapes=scratch,
         out_shape=jax.ShapeDtypeStruct(out_shape, jnp.float32),
         compiler_params=pltpu.CompilerParams(vmem_limit_bytes=52 * MIB),
         cost_estimate=pl.CostEstimate(flops=0, bytes_accessed=30 * MIB, transcendentals=0),
@@ -260,11 +232,11 @@
     wide_ref, part_refs = refs[0], refs[1 : 1 + n_parts]
     scale_ref = refs[1 + n_parts]
     rest = refs[2 + n_parts :]
-    total = wide_ref[0]
+    total = wide_ref[0, :TILE]
     for p in range(1, wide_ref.shape[0]):
-        total = total + wide_ref[p]
+        total = total + wide_ref[p, :TILE]
     for ref in part_refs:
-        total = total + ref[0, :TILE]
+        total = total + ref[0]
     scale = scale_ref[...]
     image = total * scale
     if turned:
@@ -391,24 +363,23 @@
     turn_ref[3 * WIDTH :] = pair_swap(second)
 
 
-def turn_kernel(*refs):
-    part_refs, turn_ref = refs[:-1], refs[-1]
-    packed = part_refs[0][0, TILE:]
-    for ref in part_refs[1:]:
-        packed = packed + ref[0, TILE:]
+def turn_kernel(wide_ref, turn_ref):
+    packed = wide_ref[0, TILE:]
+    for p in range(1, wide_ref.shape[0]):
+        packed = packed + wide_ref[p, TILE:]
     packed = packed * (1.0 / IMAGES)
     value = jnp.concatenate([packed, pltpu.roll(packed, 2 * WIDTH, 1)], axis=0)
     invert_factor(jnp.where(lanes(value.shape) < 2 * WIDTH, value, 0.0), turn_ref)
 
 
-def turn_of(parts):
+def turn_of(wide):
     return pl.pallas_call(
         turn_kernel,
         out_shape=jax.ShapeDtypeStruct((TILE, TILE), jnp.float32),
         compiler_params=pltpu.CompilerParams(vmem_limit_bytes=6 * MIB),
-        cost_estimate=pl.CostEstimate(flops=0, bytes_accessed=9 * MIB, transcendentals=0),
+        cost_estimate=pl.CostEstimate(flops=0, bytes_accessed=6 * MIB, transcendentals=0),
         name="turn",
-    )(*parts)
+    )(wide)
 
 
 def basis_kernel(image_ref, gram_ref, out_ref, turn_ref):
@@ -488,14 +459,14 @@
     takes_col = code // SLOTS % COL_BLOCKS
     puts_col = code // (SLOTS * COL_BLOCKS) % COL_BLOCKS
     rows = code // (SLOTS * COL_BLOCKS * COL_BLOCKS)
+    puts_col = jnp.where(slots < count, puts_col, COL_BLOCKS)
+    rows = jnp.where(slots < count, rows, ROW_BLOCKS)
     count = count.reshape(1)
 
-    row_part, col_part = degrees(row_of, col_to, live, weights)
+    plain, turned, row_part, col_part = complex_tiles(order, rows, puts_col, count, weights, angles)
     row_part = to_column(row_part)
     col_parts = reduce_row(col_part)
     degree = jnp.sum(row_part, axis=0) + sum(c[0] for c in col_parts)
-    plain, turned, done = complex_tiles(order, count, weights, angles)
-    degree = degree + done
     scale = lax.rsqrt(degree[:2])
     scale = jnp.broadcast_to(scale.T[:, :, None], (TILE, 2, 2 * WIDTH)).reshape(TILE, TILE)
 
@@ -503,16 +474,18 @@
     sent = (basis * scale).astype(jnp.bfloat16)
     body, turn = sent, None
     for rounds in range(ITERS):
-        near, far = gather_row(sent)
-        column = to_column(jnp.broadcast_to(body[None], (16,) + body.shape))
-        forward = products(1.0, takes_col, rows, count, plain, [near, far], (16, TILE, TILE), "forward")
+        near, far = gather_row(body)
+        column = to_column(jnp.broadcast_to(sent[None], (16, TILE, TILE)))
+        forward = products(
+            1.0, takes_col, rows, count, plain, [near, far], (16, body.shape[0], TILE), True, "forward"
+        )
         mirror = products(
-            -1.0, rows, puts_col, count, turned, [column], (8, body.shape[0], TILE), "mirror"
+            -1.0, rows, puts_col, count, turned, [column], (8, TILE, TILE), False, "mirror"
         )
         wide = to_column(forward)
         parts = reduce_row(mirror)
         if rounds > 0:
-            turn = turn_of(parts)
+            turn = turn_of(wide)
         sent, body = new_image(wide, parts, scale, turn, rounds == ITERS - 1)
     grams = jnp.broadcast_to(body, (128, 8, TILE))
     grams = lax.all_to_all(grams, ("row", "col"), split_axis=0, concat_axis=0, tiled=True)

time: 240 us -> 229 us (0.954)
  waiting for transfers between devices: 27.1 us -> 38.9 us
  Pallas kernels: 82.6 us -> 74.7 us
  starting transfers between devices: 93.1 us -> 85.8 us
  blocking collectives: 24.8 us -> 18 us
    all_to_all x7, waiting for transfers between devices: 0.02 us -> 20 us  [to_column(): return lax.all_to_all(value, 'col', split_axis=0, concat_axis=0, tiled=True)]
    ppermute x21, waiting for transfers between devices: 20.2 us -> 11 us  [along_x(): lax.ppermute(value, 'row', [(i, (i + 2 * step) % 8) for i in range(8)])]
    pallas_call x8 -> x7, Pallas kernels: 73.3 us -> 65.4 us  [the longest x6 48.7 us: products(): pl.pallas_call(functools.partial(product_kernel, sign, sizes, apart), in_...]
    all_to_all x1, blocking collectives: 24.8 us -> 18 us  [shards(): lax.all_to_all(grams, ('row', 'col'), split_axis=0, concat_axis=0, tiled=...]
    all_to_all x7, starting transfers between devices: 52.2 us -> 47.5 us  [to_column(): return lax.all_to_all(value, 'col', split_axis=0, concat_axis=0, tiled=True)]
    ppermute x7, starting transfers between devices: 15.4 us -> 11.6 us  [other_core(): return lax.ppermute(value, 'row', [(i, i ^ 1) for i in range(8)])]
  transfers between devices with their start and end apart: 35 -> 35, of which waited for: 23 -> 17; matrix products, arithmetic and copies ran while one was open for 1% -> 1% of each run, Pallas kernels for 29% -> 23%
where the time goes in v3:
time: 229 us; the launch traced here: 228 us
  starting transfers between devices  85.8 us (37%)
  Pallas kernels  74.7 us (33%)
  waiting for transfers between devices  38.9 us (17%)
  blocking collectives  18 us (8%)
  local copies, waits for them, and re-layouts  5.43 us (2%)
  other arithmetic  5.05 us (2%)
    pallas_call x6, Pallas kernels, products(): pl.pallas_call(functools.partial(product_kernel, sign, sizes, apart), in_...  48.7 us
    all_to_all x7, starting transfers between devices, to_column(): return lax.all_to_all(value, 'col', split_axis=0, concat_axis=0, tiled=True)  47.5 us
    ppermute x21, starting transfers between devices, along_x(): lax.ppermute(value, 'row', [(i, (i + 2 * step) % 8) for i in range(8)])  26.7 us
    all_to_all x7, waiting for transfers between devices, to_column(): return lax.all_to_all(value, 'col', split_axis=0, concat_axis=0, tiled=True)  20 us
    all_to_all x1, blocking collectives, shards(): lax.all_to_all(grams, ('row', 'col'), split_axis=0, concat_axis=0, tiled=...  18 us
    pallas_call x1, Pallas kernels, complex_tiles(): pl.pallas_call(tiles_kernel, in_specs=[SCALAR] * 4 + [FAR, FAR], out_spec...  16.7 us
    ppermute x7, starting transfers between devices, other_core(): return lax.ppermute(value, 'row', [(i, i ^ 1) for i in range(8)])  11.6 us
    ppermute x21, waiting for transfers between devices, along_x(): lax.ppermute(value, 'row', [(i, (i + 2 * step) % 8) for i in range(8)])  11 us
  transfers between devices with their start and end apart: 35, of which 17 were waited for; matrix products, arithmetic and copies ran while one was open for 1% of the time, Pallas kernels for 23%

profile of v3, /device:TPU:1, one launch (start us, length us, event | category | flops | bytes accessed | tf_op | source)
XLA Modules:
  0.0 228.3 jit_solution(17758606692121023152)
XLA Ops:
  5.3 16.7 %complex_tiles.1 = (bf16[256,128,256]{2,1,0:T(8,128)(2,1)}, bf16[256,128,256]{2,1,0:T(8,128)(2,1)}, f32[16,8,128]{2,1,0:T(8,128)}, f32[8,8,128]{2,1,0:T(8,128)}) custom-call(s32[256]{0:T(256)} %get-tuple-element.43.order, s32[256]{0:T(256)} %get-tuple-element.45.rows.puts.takes, s32[256]{0:T(256)} %get-tuple-element.42.cols.puts, s32[1]{0:T(128)} %bitcast.3.count, ...), custom_call_target="tpu_custom_call" | custom-call | bytes 52428800 | tf_op jit(solution)/shard_map/complex_tiles/pallas_call | solution.py:130
  24.1 10.3 %all-to-all-start = ((f32[16,8,128]{2,1,0:T(8,128)}), f32[16,8,128]{2,1,0:T(8,128)S(1)}, u32[]{:S(2)}, u32[]{:S(2)}) async-start(f32[16,8,128]{2,1,0:T(8,128)} %get-tuple-element.16), calls=%async_computation | async-start | bytes 131072 | tf_op jit(solution)/shard_map/all_to_all | solution.py:424
  35.5 2.7 %collective-permute-start.2 = (f32[1,8,128]{2,1,0:T(8,128)S(1)}, f32[1,8,128]{2,1,0:T(8,128)S(1)}, u32[]{:S(2)}, u32[]{:S(2)}) collective-permute-start(f32[1,8,128]{2,1,0:T(8,128)S(1)} %get-tuple-element.39), channel_id=1, source_target_pairs={{0,64},{16,80},{32,96},{48,112},{64,0},{80,16},{96,32},{112,48},{1... | collective-permute-start | bytes 12296 | tf_op jit(solution)/shard_map/ppermute | solution.py:416
  38.2 2.0 collective-permute-start.3
  42.1 6.6 %all-to-all-start.2 = ((bf16[16,128,128]{2,1,0:T(8,128)(2,1)}), bf16[16,128,128]{2,1,0:T(8,128)(2,1)S(1)}, u32[]{:S(2)}, u32[]{:S(2)}) async-start(bf16[16,128,128]{2,1,0:T(8,128)(2,1)} %broadcast_in_dim.63), calls=%async_computation.2 | async-start | bytes 1048576 | tf_op jit(solution)/shard_map/all_to_all | solution.py:424
  49.6 3.4 %collective-permute-start.5 = (bf16[128,128]{1,0:T(8,128)(2,1)S(1)}, bf16[128,128]{1,0:T(8,128)(2,1)S(1)}, u32[]{:S(2)}, u32[]{:S(2)}) collective-permute-start(bf16[128,128]{1,0:T(8,128)(2,1)S(1)} %multiply_convert_fusion), channel_id=1, source_target_pairs={{0,64},{16,80},{32,96},{48,112},{64,0},{80,16},{96,32},{112,48},{1... | collective-permute-start | bytes 98312 | tf_op jit(solution)/shard_map/ppermute | solution.py:416
  56.1 4.4 %collective-permute-start.7 = (bf16[4,128,128]{2,1,0:T(8,128)(2,1)S(1)}, bf16[4,128,128]{2,1,0:T(8,128)(2,1)S(1)}, u32[]{:S(2)}, u32[]{:S(2)}) collective-permute-start(bf16[4,128,128]{2,1,0:T(8,128)(2,1)S(1)} %pad_maximum_fusion.2.refs_0_), channel_id=1, source_target_pairs={{0,16},{16,0},{32,48},{48,32},{64,80},{80,64},{96,112},{112,96},{1... | collective-permute-start | bytes 393224 | tf_op jit(solution)/shard_map/ppermute | solution.py:420
  61.5 7.8 %forward.3 = f32[16,128,128]{2,1,0:T(8,128)} custom-call(s32[256]{0:T(256)S(1)} %get-tuple-element.44.takes, s32[256]{0:T(256)S(1)} %copy-done, s32[1]{0:T(128)} %bitcast.3.count, bf16[256,128,256]{2,1,0:T(8,128)(2,1)} %get-tuple-element.15.far_ref, bf16[4,128,128]{2,1,0:T(8,128)(2,1)S(1)} %pad_maximum_fusion.2.refs_0_, ...), custom_call_target="tpu_custom_call" | custom-call | bytes 31457280 | tf_op jit(solution)/shard_map/forward/pallas_call | solution.py:219
  69.3 7.8 %all-to-all-start.1 = ((f32[16,128,128]{2,1,0:T(8,128)}), f32[16,128,128]{2,1,0:T(8,128)S(1)}, u32[]{:S(2)}, u32[]{:S(2)}) async-start(f32[16,128,128]{2,1,0:T(8,128)} %forward.3), calls=%async_computation.1 | async-start | bytes 2097152 | tf_op jit(solution)/shard_map/all_to_all | solution.py:424
  77.1 8.4 %mirror.3 = f32[8,128,128]{2,1,0:T(8,128)S(1)} custom-call(s32[256]{0:T(256)S(1)} %copy-done, s32[256]{0:T(256)S(1)} %copy-done.1, s32[1]{0:T(128)} %bitcast.3.count, bf16[256,128,256]{2,1,0:T(8,128)(2,1)} %get-tuple-element.18.far_ref, bf16[16,128,128]{2,1,0:T(8,128)(2,1)S(1)} %all-to-all-done.2.refs_0_), custom_call_target="tpu_custom_call" | custom-call | bytes 31457280 | tf_op jit(solution)/shard_map/mirror/pallas_call | solution.py:219
  90.5 1.9 collective-permute-done.10.refs_3_
  93.4 3.6 %all-to-all-done.1.refs_0_ = f32[16,128,128]{2,1,0:T(8,128)S(1)} async-done(((f32[16,128,128]{2,1,0:T(8,128)}), f32[16,128,128]{2,1,0:T(8,128)S(1)}, u32[]{:S(2)}, u32[]{:S(2)}) %all-to-all-start.1) | async-done | bytes 1048608 | tf_op jit(solution)/shard_map/all_to_all | solution.py:424
  98.6 3.9 %all-to-all-start.4 = ((f32[16,128,128]{2,1,0:T(8,128)}), f32[16,128,128]{2,1,0:T(8,128)S(1)}, u32[]{:S(2)}, u32[]{:S(2)}) async-start(f32[16,128,128]{2,1,0:T(8,128)} %broadcast_in_dim.64), calls=%async_computation.4 | async-start | bytes 2097152 | tf_op jit(solution)/shard_map/all_to_all | solution.py:424
  102.9 2.1 collective-permute-start.13
  105.0 2.0 collective-permute-start.14
  108.6 3.7 %collective-permute-start.15 = (f32[4,144,128]{2,1,0:T(8,128)S(1)}, f32[4,144,128]{2,1,0:T(8,128)S(1)}, u32[]{:S(2)}, u32[]{:S(2)}) collective-permute-start(f32[4,144,128]{2,1,0:T(8,128)S(1)} %pad_maximum_fusion.refs_0_), channel_id=1, source_target_pairs={{0,16},{16,0},{32,48},{48,32},{64,80},{80,64},{96,112},{112,96},{1... | collective-permute-start | bytes 884744 | tf_op jit(solution)/shard_map/ppermute | solution.py:420
  113.5 7.8 %forward.4 = f32[16,144,128]{2,1,0:T(8,128)} custom-call(s32[256]{0:T(256)S(1)} %get-tuple-element.44.takes, s32[256]{0:T(256)S(1)} %copy-done, s32[1]{0:T(128)} %bitcast.3.count, bf16[256,128,256]{2,1,0:T(8,128)(2,1)} %get-tuple-element.15.far_ref, f32[4,144,128]{2,1,0:T(8,128)S(1)} %pad_maximum_fusion.refs_0_, ...), custom_call_target="tpu_custom_call" | custom-call | bytes 31457280 | tf_op jit(solution)/shard_map/forward/pallas_call | solution.py:219
  121.3 7.6 %all-to-all-start.3 = ((f32[16,144,128]{2,1,0:T(8,128)}), f32[16,144,128]{2,1,0:T(8,128)S(1)}, u32[]{:S(2)}, u32[]{:S(2)}) async-start(f32[16,144,128]{2,1,0:T(8,128)} %forward.4), calls=%async_computation.3 | async-start | bytes 2359296 | tf_op jit(solution)/shard_map/all_to_all | solution.py:424
  128.9 8.4 %mirror.4 = f32[8,128,128]{2,1,0:T(8,128)S(1)} custom-call(s32[256]{0:T(256)S(1)} %copy-done, s32[256]{0:T(256)S(1)} %copy-done.1, s32[1]{0:T(128)} %bitcast.3.count, bf16[256,128,256]{2,1,0:T(8,128)(2,1)} %get-tuple-element.18.far_ref, f32[16,128,128]{2,1,0:T(8,128)S(1)} %all-to-all-done.4.refs_0_), custom_call_target="tpu_custom_call" | custom-call | bytes 31457280 | tf_op jit(solution)/shard_map/mirror/pallas_call | solution.py:219
  139.9 2.6 %collective-permute-start.18 = (f32[1,128,128]{2,1,0:T(8,128)S(1)}, f32[1,128,128]{2,1,0:T(8,128)S(1)}, u32[]{:S(2)}, u32[]{:S(2)}) collective-permute-start(f32[1,128,128]{2,1,0:T(8,128)S(1)} %get-tuple-element.30), channel_id=1, source_target_pairs={{0,64},{16,80},{32,96},{48,112},{64,0},{80,16},{96,32},{112,48},{1... | collective-permute-start | bytes 196616 | tf_op jit(solution)/shard_map/ppermute | solution.py:416
  142.5 8.0 %all-to-all-done.3.wide_ref.refs_0_ = f32[16,144,128]{2,1,0:T(8,128)S(1)} async-done(((f32[16,144,128]{2,1,0:T(8,128)}), f32[16,144,128]{2,1,0:T(8,128)S(1)}, u32[]{:S(2)}, u32[]{:S(2)}) %all-to-all-start.3) | async-done | bytes 1179680 | tf_op jit(solution)/shard_map/all_to_all | solution.py:424
  150.5 1.8 turn.2.refs_6_
  154.3 3.7 %all-to-all-start.6 = ((f32[16,128,128]{2,1,0:T(8,128)}), f32[16,128,128]{2,1,0:T(8,128)S(1)}, u32[]{:S(2)}, u32[]{:S(2)}) async-start(f32[16,128,128]{2,1,0:T(8,128)} %broadcast_in_dim.65), calls=%async_computation.6 | async-start | bytes 2097152 | tf_op jit(solution)/shard_map/all_to_all | solution.py:424
  160.9 3.5 %collective-permute-done.20 = f32[144,128]{1,0:T(8,128)S(1)} collective-permute-done((f32[144,128]{1,0:T(8,128)S(1)}, f32[144,128]{1,0:T(8,128)S(1)}, u32[]{:S(2)}, u32[]{:S(2)}) %collective-permute-start.20) | collective-permute-done | bytes 73760 | tf_op jit(solution)/shard_map/ppermute | solution.py:416
  167.4 7.8 %forward.5 = f32[16,144,128]{2,1,0:T(8,128)} custom-call(s32[256]{0:T(256)S(1)} %get-tuple-element.44.takes, s32[256]{0:T(256)S(1)} %copy-done, s32[1]{0:T(128)} %bitcast.3.count, bf16[256,128,256]{2,1,0:T(8,128)(2,1)} %get-tuple-element.15.far_ref, f32[4,144,128]{2,1,0:T(8,128)S(1)} %pad_maximum_fusion.1.refs_0_, ...), custom_call_target="tpu_custom_call" | custom-call | bytes 31457280 | tf_op jit(solution)/shard_map/forward/pallas_call | solution.py:219
  175.2 7.6 %all-to-all-start.5 = ((f32[16,144,128]{2,1,0:T(8,128)}), f32[16,144,128]{2,1,0:T(8,128)S(1)}, u32[]{:S(2)}, u32[]{:S(2)}) async-start(f32[16,144,128]{2,1,0:T(8,128)} %forward.5), calls=%async_computation.5 | async-start | bytes 2359296 | tf_op jit(solution)/shard_map/all_to_all | solution.py:424
  182.8 8.6 %mirror.5 = f32[8,128,128]{2,1,0:T(8,128)S(1)} custom-call(s32[256]{0:T(256)S(1)} %copy-done, s32[256]{0:T(256)S(1)} %copy-done.1, s32[1]{0:T(128)} %bitcast.3.count, bf16[256,128,256]{2,1,0:T(8,128)(2,1)} %get-tuple-element.18.far_ref, f32[16,128,128]{2,1,0:T(8,128)S(1)} %all-to-all-done.6.refs_0_), custom_call_target="tpu_custom_call" | custom-call | bytes 31457280 | tf_op jit(solution)/shard_map/mirror/pallas_call | solution.py:219
  194.0 2.6 %collective-permute-start.26 = (f32[1,128,128]{2,1,0:T(8,128)S(1)}, f32[1,128,128]{2,1,0:T(8,128)S(1)}, u32[]{:S(2)}, u32[]{:S(2)}) collective-permute-start(f32[1,128,128]{2,1,0:T(8,128)S(1)} %get-tuple-element.26), channel_id=1, source_target_pairs={{0,64},{16,80},{32,96},{48,112},{64,0},{80,16},{96,32},{112,48},{1... | collective-permute-start | bytes 196616 | tf_op jit(solution)/shard_map/ppermute | solution.py:416
  196.6 7.7 %all-to-all-done.5.wide_ref.refs_0_ = f32[16,144,128]{2,1,0:T(8,128)S(1)} async-done(((f32[16,144,128]{2,1,0:T(8,128)}), f32[16,144,128]{2,1,0:T(8,128)S(1)}, u32[]{:S(2)}, u32[]{:S(2)}) %all-to-all-start.5) | async-done | bytes 1179680 | tf_op jit(solution)/shard_map/all_to_all | solution.py:424
  204.3 1.8 turn.3.refs_6_
  207.3 18.0 %all_to_all.40.gram_ref = f32[128,8,128]{2,1,0:T(8,128)S(1)} all-to-all(f32[128,8,128]{2,1,0:T(8,128)S(1)} %broadcast_in_dim.67), channel_id=1, replica_groups=mesh['row'=8,'col'=16] {'row','col'}, dimensions={0} | all-to-all | bytes 1048576 | tf_op jit(solution)/shard_map/all_to_all | solution.py:491
  225.3 3.1 %basis.1 = f32[2,32,256]{2,1,0:T(8,128)} custom-call(f32[128,128]{1,0:T(8,128)S(1)} %get-tuple-element.23.image_ref, f32[128,8,128]{2,1,0:T(8,128)S(1)} %all_to_all.40.gram_ref), custom_call_target="tpu_custom_call" | custom-call | tf_op jit(solution)/shard_map/basis/pallas_call | solution.py:406
  (99 shorter events, 40.0 us)
Async XLA Ops:
  22.7 11.8 %collective-permute-start = (f32[4,8,128]{2,1,0:T(8,128)S(1)}, f32[4,8,128]{2,1,0:T(8,128)S(1)}, u32[]{:S(2)}, u32[]{:S(2)}) collective-permute-start(f32[4,8,128]{2,1,0:T(8,128)S(1)} %slice.84), channel_id=1, source_target_pairs={{0,16},{16,0},{32,48},{48,32},{64,80},{80,64},{96,112},{112,96},{1... | collective-permute-start | bytes 49160 | tf_op jit(solution)/shard_map/ppermute | solution.py:420
  24.1 16.9 %all-to-all-start = ((f32[16,8,128]{2,1,0:T(8,128)}), f32[16,8,128]{2,1,0:T(8,128)S(1)}, u32[]{:S(2)}, u32[]{:S(2)}) async-start(f32[16,8,128]{2,1,0:T(8,128)} %get-tuple-element.16), calls=%async_computation | async-start | bytes 131072 | tf_op jit(solution)/shard_map/all_to_all | solution.py:424
  35.2 5.8 %collective-permute-start.1 = (f32[1,8,128]{2,1,0:T(8,128)S(1)}, f32[1,8,128]{2,1,0:T(8,128)S(1)}, u32[]{:S(2)}, u32[]{:S(2)}) collective-permute-start(f32[1,8,128]{2,1,0:T(8,128)S(1)} %get-tuple-element.37), channel_id=1, source_target_pairs={{0,32},{16,48},{32,64},{48,80},{64,96},{80,112},{96,0},{112,16},{1... | collective-permute-start | bytes 12296 | tf_op jit(solution)/shard_map/ppermute | solution.py:416
  35.5 5.5 %collective-permute-start.2 = (f32[1,8,128]{2,1,0:T(8,128)S(1)}, f32[1,8,128]{2,1,0:T(8,128)S(1)}, u32[]{:S(2)}, u32[]{:S(2)}) collective-permute-start(f32[1,8,128]{2,1,0:T(8,128)S(1)} %get-tuple-element.39), channel_id=1, source_target_pairs={{0,64},{16,80},{32,96},{48,112},{64,0},{80,16},{96,32},{112,48},{1... | collective-permute-start | bytes 12296 | tf_op jit(solution)/shard_map/ppermute | solution.py:416
  38.2 2.8 %collective-permute-start.3 = (f32[1,8,128]{2,1,0:T(8,128)S(1)}, f32[1,8,128]{2,1,0:T(8,128)S(1)}, u32[]{:S(2)}, u32[]{:S(2)}) collective-permute-start(f32[1,8,128]{2,1,0:T(8,128)S(1)} %get-tuple-element.38), channel_id=1, source_target_pairs={{0,96},{16,112},{32,0},{48,16},{64,32},{80,48},{96,64},{112,80},{1... | collective-permute-start | bytes 12296 | tf_op jit(solution)/shard_map/ppermute | solution.py:416
  42.1 27.2 %all-to-all-start.2 = ((bf16[16,128,128]{2,1,0:T(8,128)(2,1)}), bf16[16,128,128]{2,1,0:T(8,128)(2,1)S(1)}, u32[]{:S(2)}, u32[]{:S(2)}) async-start(bf16[16,128,128]{2,1,0:T(8,128)(2,1)} %broadcast_in_dim.63), calls=%async_computation.2 | async-start | bytes 1048576 | tf_op jit(solution)/shard_map/all_to_all | solution.py:424
  48.7 4.4 %collective-permute-start.4 = (bf16[128,128]{1,0:T(8,128)(2,1)S(1)}, bf16[128,128]{1,0:T(8,128)(2,1)S(1)}, u32[]{:S(2)}, u32[]{:S(2)}) collective-permute-start(bf16[128,128]{1,0:T(8,128)(2,1)S(1)} %multiply_convert_fusion), channel_id=1, source_target_pairs={{0,32},{16,48},{32,64},{48,80},{64,96},{80,112},{96,0},{112,16},{1... | collective-permute-start | bytes 98312 | tf_op jit(solution)/shard_map/ppermute | solution.py:416
  49.6 5.0 %collective-permute-start.5 = (bf16[128,128]{1,0:T(8,128)(2,1)S(1)}, bf16[128,128]{1,0:T(8,128)(2,1)S(1)}, u32[]{:S(2)}, u32[]{:S(2)}) collective-permute-start(bf16[128,128]{1,0:T(8,128)(2,1)S(1)} %multiply_convert_fusion), channel_id=1, source_target_pairs={{0,64},{16,80},{32,96},{48,112},{64,0},{80,16},{96,32},{112,48},{1... | collective-permute-start | bytes 98312 | tf_op jit(solution)/shard_map/ppermute | solution.py:416
  53.0 3.1 %collective-permute-start.6 = (bf16[128,128]{1,0:T(8,128)(2,1)S(1)}, bf16[128,128]{1,0:T(8,128)(2,1)S(1)}, u32[]{:S(2)}, u32[]{:S(2)}) collective-permute-start(bf16[128,128]{1,0:T(8,128)(2,1)S(1)} %multiply_convert_fusion), channel_id=1, source_target_pairs={{0,96},{16,112},{32,0},{48,16},{64,32},{80,48},{96,64},{112,80},{1... | collective-permute-start | bytes 98312 | tf_op jit(solution)/shard_map/ppermute | solution.py:416
  56.1 5.4 %collective-permute-start.7 = (bf16[4,128,128]{2,1,0:T(8,128)(2,1)S(1)}, bf16[4,128,128]{2,1,0:T(8,128)(2,1)S(1)}, u32[]{:S(2)}, u32[]{:S(2)}) collective-permute-start(bf16[4,128,128]{2,1,0:T(8,128)(2,1)S(1)} %pad_maximum_fusion.2.refs_0_), channel_id=1, source_target_pairs={{0,16},{16,0},{32,48},{48,32},{64,80},{80,64},{96,112},{112,96},{1... | collective-permute-start | bytes 393224 | tf_op jit(solution)/shard_map/ppermute | solution.py:420
  69.3 27.7 %all-to-all-start.1 = ((f32[16,128,128]{2,1,0:T(8,128)}), f32[16,128,128]{2,1,0:T(8,128)S(1)}, u32[]{:S(2)}, u32[]{:S(2)}) async-start(f32[16,128,128]{2,1,0:T(8,128)} %forward.3), calls=%async_computation.1 | async-start | bytes 2097152 | tf_op jit(solution)/shard_map/all_to_all | solution.py:424
  87.3 5.1 %collective-permute-start.10 = (f32[1,128,128]{2,1,0:T(8,128)S(1)}, f32[1,128,128]{2,1,0:T(8,128)S(1)}, u32[]{:S(2)}, u32[]{:S(2)}) collective-permute-start(f32[1,128,128]{2,1,0:T(8,128)S(1)} %get-tuple-element.34), channel_id=1, source_target_pairs={{0,64},{16,80},{32,96},{48,112},{64,0},{80,16},{96,32},{112,48},{1... | collective-permute-start | bytes 196616 | tf_op jit(solution)/shard_map/ppermute | solution.py:416
  89.0 3.4 %collective-permute-start.11 = (f32[1,128,128]{2,1,0:T(8,128)S(1)}, f32[1,128,128]{2,1,0:T(8,128)S(1)}, u32[]{:S(2)}, u32[]{:S(2)}) collective-permute-start(f32[1,128,128]{2,1,0:T(8,128)S(1)} %get-tuple-element.33), channel_id=1, source_target_pairs={{0,96},{16,112},{32,0},{48,16},{64,32},{80,48},{96,64},{112,80},{1... | collective-permute-start | bytes 196616 | tf_op jit(solution)/shard_map/ppermute | solution.py:416
  89.0 4.4 %collective-permute-start.9 = (f32[1,128,128]{2,1,0:T(8,128)S(1)}, f32[1,128,128]{2,1,0:T(8,128)S(1)}, u32[]{:S(2)}, u32[]{:S(2)}) collective-permute-start(f32[1,128,128]{2,1,0:T(8,128)S(1)} %get-tuple-element.35), channel_id=1, source_target_pairs={{0,32},{16,48},{32,64},{48,80},{64,96},{80,112},{96,0},{112,16},{1... | collective-permute-start | bytes 196616 | tf_op jit(solution)/shard_map/ppermute | solution.py:416
  98.6 22.6 %all-to-all-start.4 = ((f32[16,128,128]{2,1,0:T(8,128)}), f32[16,128,128]{2,1,0:T(8,128)S(1)}, u32[]{:S(2)}, u32[]{:S(2)}) async-start(f32[16,128,128]{2,1,0:T(8,128)} %broadcast_in_dim.64), calls=%async_computation.4 | async-start | bytes 2097152 | tf_op jit(solution)/shard_map/all_to_all | solution.py:424
  102.6 5.5 %collective-permute-start.12 = (f32[144,128]{1,0:T(8,128)S(1)}, f32[144,128]{1,0:T(8,128)S(1)}, u32[]{:S(2)}, u32[]{:S(2)}) collective-permute-start(f32[144,128]{1,0:T(8,128)S(1)} %get-tuple-element.19), channel_id=1, source_target_pairs={{0,32},{16,48},{32,64},{48,80},{64,96},{80,112},{96,0},{112,16},{1... | collective-permute-start | bytes 221192 | tf_op jit(solution)/shard_map/ppermute | solution.py:416
  102.9 5.1 %collective-permute-start.13 = (f32[144,128]{1,0:T(8,128)S(1)}, f32[144,128]{1,0:T(8,128)S(1)}, u32[]{:S(2)}, u32[]{:S(2)}) collective-permute-start(f32[144,128]{1,0:T(8,128)S(1)} %get-tuple-element.19), channel_id=1, source_target_pairs={{0,64},{16,80},{32,96},{48,112},{64,0},{80,16},{96,32},{112,48},{1... | collective-permute-start | bytes 221192 | tf_op jit(solution)/shard_map/ppermute | solution.py:416
  105.0 3.6 %collective-permute-start.14 = (f32[144,128]{1,0:T(8,128)S(1)}, f32[144,128]{1,0:T(8,128)S(1)}, u32[]{:S(2)}, u32[]{:S(2)}) collective-permute-start(f32[144,128]{1,0:T(8,128)S(1)} %get-tuple-element.19), channel_id=1, source_target_pairs={{0,96},{16,112},{32,0},{48,16},{64,32},{80,48},{96,64},{112,80},{1... | collective-permute-start | bytes 221192 | tf_op jit(solution)/shard_map/ppermute | solution.py:416
  108.6 4.9 %collective-permute-start.15 = (f32[4,144,128]{2,1,0:T(8,128)S(1)}, f32[4,144,128]{2,1,0:T(8,128)S(1)}, u32[]{:S(2)}, u32[]{:S(2)}) collective-permute-start(f32[4,144,128]{2,1,0:T(8,128)S(1)} %pad_maximum_fusion.refs_0_), channel_id=1, source_target_pairs={{0,16},{16,0},{32,48},{48,32},{64,80},{80,64},{96,112},{112,96},{1... | collective-permute-start | bytes 884744 | tf_op jit(solution)/shard_map/ppermute | solution.py:420
  121.3 29.2 %all-to-all-start.3 = ((f32[16,144,128]{2,1,0:T(8,128)}), f32[16,144,128]{2,1,0:T(8,128)S(1)}, u32[]{:S(2)}, u32[]{:S(2)}) async-start(f32[16,144,128]{2,1,0:T(8,128)} %forward.4), calls=%async_computation.3 | async-start | bytes 2359296 | tf_op jit(solution)/shard_map/all_to_all | solution.py:424
  139.0 13.3 %collective-permute-start.17 = (f32[1,128,128]{2,1,0:T(8,128)S(1)}, f32[1,128,128]{2,1,0:T(8,128)S(1)}, u32[]{:S(2)}, u32[]{:S(2)}) collective-permute-start(f32[1,128,128]{2,1,0:T(8,128)S(1)} %get-tuple-element.31), channel_id=1, source_target_pairs={{0,32},{16,48},{32,64},{48,80},{64,96},{80,112},{96,0},{112,16},{1... | collective-permute-start | bytes 196616 | tf_op jit(solution)/shard_map/ppermute | solution.py:416
  139.9 12.4 %collective-permute-start.18 = (f32[1,128,128]{2,1,0:T(8,128)S(1)}, f32[1,128,128]{2,1,0:T(8,128)S(1)}, u32[]{:S(2)}, u32[]{:S(2)}) collective-permute-start(f32[1,128,128]{2,1,0:T(8,128)S(1)} %get-tuple-element.30), channel_id=1, source_target_pairs={{0,64},{16,80},{32,96},{48,112},{64,0},{80,16},{96,32},{112,48},{1... | collective-permute-start | bytes 196616 | tf_op jit(solution)/shard_map/ppermute | solution.py:416
  142.5 9.8 %collective-permute-start.19 = (f32[1,128,128]{2,1,0:T(8,128)S(1)}, f32[1,128,128]{2,1,0:T(8,128)S(1)}, u32[]{:S(2)}, u32[]{:S(2)}) collective-permute-start(f32[1,128,128]{2,1,0:T(8,128)S(1)} %get-tuple-element.29), channel_id=1, source_target_pairs={{0,96},{16,112},{32,0},{48,16},{64,32},{80,48},{96,64},{112,80},{1... | collective-permute-start | bytes 196616 | tf_op jit(solution)/shard_map/ppermute | solution.py:416
  154.3 20.9 %all-to-all-start.6 = ((f32[16,128,128]{2,1,0:T(8,128)}), f32[16,128,128]{2,1,0:T(8,128)S(1)}, u32[]{:S(2)}, u32[]{:S(2)}) async-start(f32[16,128,128]{2,1,0:T(8,128)} %broadcast_in_dim.65), calls=%async_computation.6 | async-start | bytes 2097152 | tf_op jit(solution)/shard_map/all_to_all | solution.py:424
  158.0 6.4 %collective-permute-start.20 = (f32[144,128]{1,0:T(8,128)S(1)}, f32[144,128]{1,0:T(8,128)S(1)}, u32[]{:S(2)}, u32[]{:S(2)}) collective-permute-start(f32[144,128]{1,0:T(8,128)S(1)} %get-tuple-element.21), channel_id=1, source_target_pairs={{0,32},{16,48},{32,64},{48,80},{64,96},{80,112},{96,0},{112,16},{1... | collective-permute-start | bytes 221192 | tf_op jit(solution)/shard_map/ppermute | solution.py:416
  158.1 6.3 %collective-permute-start.21 = (f32[144,128]{1,0:T(8,128)S(1)}, f32[144,128]{1,0:T(8,128)S(1)}, u32[]{:S(2)}, u32[]{:S(2)}) collective-permute-start(f32[144,128]{1,0:T(8,128)S(1)} %get-tuple-element.21), channel_id=1, source_target_pairs={{0,64},{16,80},{32,96},{48,112},{64,0},{80,16},{96,32},{112,48},{1... | collective-permute-start | bytes 221192 | tf_op jit(solution)/shard_map/ppermute | solution.py:416
  159.2 5.2 %collective-permute-start.22 = (f32[144,128]{1,0:T(8,128)S(1)}, f32[144,128]{1,0:T(8,128)S(1)}, u32[]{:S(2)}, u32[]{:S(2)}) collective-permute-start(f32[144,128]{1,0:T(8,128)S(1)} %get-tuple-element.21), channel_id=1, source_target_pairs={{0,96},{16,112},{32,0},{48,16},{64,32},{80,48},{96,64},{112,80},{1... | collective-permute-start | bytes 221192 | tf_op jit(solution)/shard_map/ppermute | solution.py:416
  164.4 3.0 %collective-permute-start.23 = (f32[4,144,128]{2,1,0:T(8,128)S(1)}, f32[4,144,128]{2,1,0:T(8,128)S(1)}, u32[]{:S(2)}, u32[]{:S(2)}) collective-permute-start(f32[4,144,128]{2,1,0:T(8,128)S(1)} %pad_maximum_fusion.1.refs_0_), channel_id=1, source_target_pairs={{0,16},{16,0},{32,48},{48,32},{64,80},{80,64},{96,112},{112,96},{1... | collective-permute-start | bytes 884744 | tf_op jit(solution)/shard_map/ppermute | solution.py:420
  175.2 29.1 %all-to-all-start.5 = ((f32[16,144,128]{2,1,0:T(8,128)}), f32[16,144,128]{2,1,0:T(8,128)S(1)}, u32[]{:S(2)}, u32[]{:S(2)}) async-start(f32[16,144,128]{2,1,0:T(8,128)} %forward.5), calls=%async_computation.5 | async-start | bytes 2359296 | tf_op jit(solution)/shard_map/all_to_all | solution.py:424
  193.1 13.0 %collective-permute-start.25 = (f32[1,128,128]{2,1,0:T(8,128)S(1)}, f32[1,128,128]{2,1,0:T(8,128)S(1)}, u32[]{:S(2)}, u32[]{:S(2)}) collective-permute-start(f32[1,128,128]{2,1,0:T(8,128)S(1)} %get-tuple-element.27), channel_id=1, source_target_pairs={{0,32},{16,48},{32,64},{48,80},{64,96},{80,112},{96,0},{112,16},{1... | collective-permute-start | bytes 196616 | tf_op jit(solution)/shard_map/ppermute | solution.py:416
  194.0 12.2 %collective-permute-start.26 = (f32[1,128,128]{2,1,0:T(8,128)S(1)}, f32[1,128,128]{2,1,0:T(8,128)S(1)}, u32[]{:S(2)}, u32[]{:S(2)}) collective-permute-start(f32[1,128,128]{2,1,0:T(8,128)S(1)} %get-tuple-element.26), channel_id=1, source_target_pairs={{0,64},{16,80},{32,96},{48,112},{64,0},{80,16},{96,32},{112,48},{1... | collective-permute-start | bytes 196616 | tf_op jit(solution)/shard_map/ppermute | solution.py:416
  196.6 9.6 %collective-permute-start.27 = (f32[1,128,128]{2,1,0:T(8,128)S(1)}, f32[1,128,128]{2,1,0:T(8,128)S(1)}, u32[]{:S(2)}, u32[]{:S(2)}) collective-permute-start(f32[1,128,128]{2,1,0:T(8,128)S(1)} %get-tuple-element.25), channel_id=1, source_target_pairs={{0,96},{16,112},{32,0},{48,16},{64,32},{80,48},{96,64},{112,80},{1... | collective-permute-start | bytes 196616 | tf_op jit(solution)/shard_map/ppermute | solution.py:416
  (6 other events, 111.6 us)

commit v4 on v3

--- a/solution.py
+++ b/solution.py
@@ -176,16 +176,25 @@
                 x_mat[base + 2 * p + k, TILE:] = (sign * pair_swap(top)).astype(jnp.bfloat16)
         base += 2 * size
 
-    def step(c, carry):
-        fetch(far_ref, tiles_ref, sems, c).wait()
-        for u in range(CHUNK):
+    def add(c, size):
+        for part in range(size):
+            fetch(far_ref, tiles_ref, sems, c + part).wait()
+        for u in range(CHUNK * size):
             slot = c * CHUNK + u
             acc[puts[slot]] += jnp.dot(
                 tiles_ref[slot], x_mat[takes[slot]], preferred_element_type=jnp.float32
             )
+
+    def step(c, carry):
+        add(2 * c, 2)
         return carry
 
-    lax.fori_loop(0, chunks, step, 0)
+    lax.fori_loop(0, chunks // 2, step, 0)
+
+    @pl.when(chunks % 2 == 1)
+    def _():
+        add(chunks - 1, 1)
+
     near, out_sems = refs[len(sizes) :][5:] if apart else (out_ref, None)
     if out_ref.shape[1] > TILE:
         gram = sum(x_ref[p, TILE:] for x_ref, size in zip(x_refs, sizes) for p in range(size))
@@ -487,8 +496,15 @@
         if rounds > 0:
             turn = turn_of(wide)
         sent, body = new_image(wide, parts, scale, turn, rounds == ITERS - 1)
-    grams = jnp.broadcast_to(body, (128, 8, TILE))
-    grams = lax.all_to_all(grams, ("row", "col"), split_axis=0, concat_axis=0, tiled=True)
+    body = body + other_core(body)
+    grams = lax.all_to_all(
+        jnp.broadcast_to(body, (64, 8, TILE)),
+        ("row", "col"),
+        split_axis=0,
+        concat_axis=0,
+        tiled=True,
+        axis_index_groups=[[16 * r + c for r in range(core, 8, 2) for c in range(16)] for core in (0, 1)],
+    )
     return last_basis(sent, grams)
 
 

time: 229 us -> 222 us (0.969)
  waiting for transfers between devices: 38.9 us -> 29.9 us
  starting transfers between devices: 85.8 us -> 88.7 us
  blocking collectives: 18 us -> 15.4 us
    all_to_all x7, waiting for transfers between devices: 20 us -> 8.28 us  [to_column(): return lax.all_to_all(value, 'col', split_axis=0, concat_axis=0, tiled=True)]
    ppermute x7 -> x8, starting transfers between devices: 11.6 us -> 17.3 us  [other_core(): return lax.ppermute(value, 'row', [(i, i ^ 1) for i in range(8)])]
    ppermute x21, waiting for transfers between devices: 11 us -> 13.9 us  [along_x(): lax.ppermute(value, 'row', [(i, (i + 2 * step) % 8) for i in range(8)])]
    all_to_all x1, blocking collectives: 18 us -> 15.4 us  [shards(): lax.all_to_all(jnp.broadcast_to(body, (64, 8, TILE)), ('row', 'col'), spl...]
    ppermute x7 -> x8, waiting for transfers between devices: 7.97 us -> 7.72 us  [other_core(): return lax.ppermute(value, 'row', [(i, i ^ 1) for i in range(8)])]
  transfers between devices with their start and end apart: 35 -> 36, of which waited for: 17 -> 24; matrix products, arithmetic and copies ran while one was open for 1% -> 1% of each run, Pallas kernels for 23% -> 23%
where the time goes in v4:
time: 222 us; the launch traced here: 220 us
  starting transfers between devices  88.7 us (40%)
  Pallas kernels  75.2 us (34%)
  waiting for transfers between devices  29.9 us (13%)
  blocking collectives  15.4 us (7%)
  local copies, waits for them, and re-layouts  5.41 us (2%)
  other arithmetic  5.24 us (2%)
    pallas_call x6, Pallas kernels, products(): pl.pallas_call(functools.partial(product_kernel, sign, sizes, apart), in_...  47.7 us
    all_to_all x7, starting transfers between devices, to_column(): return lax.all_to_all(value, 'col', split_axis=0, concat_axis=0, tiled=True)  46.3 us
    ppermute x21, starting transfers between devices, along_x(): lax.ppermute(value, 'row', [(i, (i + 2 * step) % 8) for i in range(8)])  25.2 us
    pallas_call x1, Pallas kernels, complex_tiles(): pl.pallas_call(tiles_kernel, in_specs=[SCALAR] * 4 + [FAR, FAR], out_spec...  18.3 us
    ppermute x8, starting transfers between devices, other_core(): return lax.ppermute(value, 'row', [(i, i ^ 1) for i in range(8)])  17.3 us
    all_to_all x1, blocking collectives, shards(): lax.all_to_all(jnp.broadcast_to(body, (64, 8, TILE)), ('row', 'col'), spl...  15.4 us
    ppermute x21, waiting for transfers between devices, along_x(): lax.ppermute(value, 'row', [(i, (i + 2 * step) % 8) for i in range(8)])  13.9 us
    all_to_all x7, waiting for transfers between devices, to_column(): return lax.all_to_all(value, 'col', split_axis=0, concat_axis=0, tiled=True)  8.28 us
  transfers between devices with their start and end apart: 36, of which 24 were waited for; matrix products, arithmetic and copies ran while one was open for 1% of the time, Pallas kernels for 23%

profile of v4, /device:TPU:1, one launch (start us, length us, event | category | flops | bytes accessed | tf_op | source)
XLA Modules:
  0.0 220.4 jit_solution(5702479646686857795)
XLA Ops:
  5.5 18.3 %complex_tiles.1 = (bf16[256,128,256]{2,1,0:T(8,128)(2,1)}, bf16[256,128,256]{2,1,0:T(8,128)(2,1)}, f32[16,8,128]{2,1,0:T(8,128)}, f32[8,8,128]{2,1,0:T(8,128)}) custom-call(s32[256]{0:T(256)} %get-tuple-element.43.order, s32[256]{0:T(256)} %get-tuple-element.45.rows.puts.takes, s32[256]{0:T(256)} %get-tuple-element.42.cols.puts, s32[1]{0:T(128)} %bitcast.3.count, ...), custom_call_target="tpu_custom_call" | custom-call | bytes 52428800 | tf_op jit(solution)/shard_map/complex_tiles/pallas_call | solution.py:130
  25.9 7.9 %all-to-all-start = ((f32[16,8,128]{2,1,0:T(8,128)}), f32[16,8,128]{2,1,0:T(8,128)S(1)}, u32[]{:S(2)}, u32[]{:S(2)}) async-start(f32[16,8,128]{2,1,0:T(8,128)} %get-tuple-element.16), calls=%async_computation | async-start | bytes 131072 | tf_op jit(solution)/shard_map/all_to_all | solution.py:433
  36.0 3.4 %collective-permute-start.2 = (f32[1,8,128]{2,1,0:T(8,128)S(1)}, f32[1,8,128]{2,1,0:T(8,128)S(1)}, u32[]{:S(2)}, u32[]{:S(2)}) collective-permute-start(f32[1,8,128]{2,1,0:T(8,128)S(1)} %get-tuple-element.39), channel_id=1, source_target_pairs={{0,64},{16,80},{32,96},{48,112},{64,0},{80,16},{96,32},{112,48},{1... | collective-permute-start | bytes 12296 | tf_op jit(solution)/shard_map/ppermute | solution.py:425
  42.9 6.7 %all-to-all-start.2 = ((bf16[16,128,128]{2,1,0:T(8,128)(2,1)}), bf16[16,128,128]{2,1,0:T(8,128)(2,1)S(1)}, u32[]{:S(2)}, u32[]{:S(2)}) async-start(bf16[16,128,128]{2,1,0:T(8,128)(2,1)} %broadcast_in_dim.63), calls=%async_computation.2 | async-start | bytes 1048576 | tf_op jit(solution)/shard_map/all_to_all | solution.py:433
  49.7 2.7 %collective-permute-start.5 = (bf16[128,128]{1,0:T(8,128)(2,1)S(1)}, bf16[128,128]{1,0:T(8,128)(2,1)S(1)}, u32[]{:S(2)}, u32[]{:S(2)}) collective-permute-start(bf16[128,128]{1,0:T(8,128)(2,1)S(1)} %multiply_convert_fusion), channel_id=1, source_target_pairs={{0,64},{16,80},{32,96},{48,112},{64,0},{80,16},{96,32},{112,48},{1... | collective-permute-start | bytes 98312 | tf_op jit(solution)/shard_map/ppermute | solution.py:425
  55.2 3.8 %collective-permute-start.7 = (bf16[4,128,128]{2,1,0:T(8,128)(2,1)S(1)}, bf16[4,128,128]{2,1,0:T(8,128)(2,1)S(1)}, u32[]{:S(2)}, u32[]{:S(2)}) collective-permute-start(bf16[4,128,128]{2,1,0:T(8,128)(2,1)S(1)} %pad_maximum_fusion.2.refs_0_), channel_id=1, source_target_pairs={{0,16},{16,0},{32,48},{48,32},{64,80},{80,64},{96,112},{112,96},{1... | collective-permute-start | bytes 393224 | tf_op jit(solution)/shard_map/ppermute | solution.py:429
  60.0 7.6 %forward.3 = f32[16,128,128]{2,1,0:T(8,128)} custom-call(s32[256]{0:T(256)S(1)} %get-tuple-element.44.takes, s32[256]{0:T(256)S(1)} %copy-done, s32[1]{0:T(128)} %bitcast.3.count, bf16[256,128,256]{2,1,0:T(8,128)(2,1)} %get-tuple-element.15.far_ref, bf16[4,128,128]{2,1,0:T(8,128)(2,1)S(1)} %pad_maximum_fusion.2.refs_0_, ...), custom_call_target="tpu_custom_call" | custom-call | bytes 31457280 | tf_op jit(solution)/shard_map/forward/pallas_call | solution.py:228
  67.6 6.7 %all-to-all-start.1 = ((f32[16,128,128]{2,1,0:T(8,128)}), f32[16,128,128]{2,1,0:T(8,128)S(1)}, u32[]{:S(2)}, u32[]{:S(2)}) async-start(f32[16,128,128]{2,1,0:T(8,128)} %forward.3), calls=%async_computation.1 | async-start | bytes 2097152 | tf_op jit(solution)/shard_map/all_to_all | solution.py:433
  74.3 8.3 %mirror.3 = f32[8,128,128]{2,1,0:T(8,128)S(1)} custom-call(s32[256]{0:T(256)S(1)} %copy-done, s32[256]{0:T(256)S(1)} %copy-done.1, s32[1]{0:T(128)} %bitcast.3.count, bf16[256,128,256]{2,1,0:T(8,128)(2,1)} %get-tuple-element.18.far_ref, bf16[16,128,128]{2,1,0:T(8,128)(2,1)S(1)} %all-to-all-done.2.refs_0_), custom_call_target="tpu_custom_call" | custom-call | bytes 31457280 | tf_op jit(solution)/shard_map/mirror/pallas_call | solution.py:228
  85.9 2.0 collective-permute-start.11
  90.8 1.7 collective-permute-done.9.refs_2_
  94.1 6.7 %all-to-all-start.4 = ((f32[16,128,128]{2,1,0:T(8,128)}), f32[16,128,128]{2,1,0:T(8,128)S(1)}, u32[]{:S(2)}, u32[]{:S(2)}) async-start(f32[16,128,128]{2,1,0:T(8,128)} %broadcast_in_dim.64), calls=%async_computation.4 | async-start | bytes 2097152 | tf_op jit(solution)/shard_map/all_to_all | solution.py:433
  100.9 3.1 %collective-permute-start.13 = (f32[144,128]{1,0:T(8,128)S(1)}, f32[144,128]{1,0:T(8,128)S(1)}, u32[]{:S(2)}, u32[]{:S(2)}) collective-permute-start(f32[144,128]{1,0:T(8,128)S(1)} %get-tuple-element.19), channel_id=1, source_target_pairs={{0,64},{16,80},{32,96},{48,112},{64,0},{80,16},{96,32},{112,48},{1... | collective-permute-start | bytes 221192 | tf_op jit(solution)/shard_map/ppermute | solution.py:425
  107.3 3.3 %collective-permute-start.15 = (f32[4,144,128]{2,1,0:T(8,128)S(1)}, f32[4,144,128]{2,1,0:T(8,128)S(1)}, u32[]{:S(2)}, u32[]{:S(2)}) collective-permute-start(f32[4,144,128]{2,1,0:T(8,128)S(1)} %pad_maximum_fusion.refs_0_), channel_id=1, source_target_pairs={{0,16},{16,0},{32,48},{48,32},{64,80},{80,64},{96,112},{112,96},{1... | collective-permute-start | bytes 884744 | tf_op jit(solution)/shard_map/ppermute | solution.py:429
  111.8 7.6 %forward.4 = f32[16,144,128]{2,1,0:T(8,128)} custom-call(s32[256]{0:T(256)S(1)} %get-tuple-element.44.takes, s32[256]{0:T(256)S(1)} %copy-done, s32[1]{0:T(128)} %bitcast.3.count, bf16[256,128,256]{2,1,0:T(8,128)(2,1)} %get-tuple-element.15.far_ref, f32[4,144,128]{2,1,0:T(8,128)S(1)} %pad_maximum_fusion.refs_0_, ...), custom_call_target="tpu_custom_call" | custom-call | bytes 31457280 | tf_op jit(solution)/shard_map/forward/pallas_call | solution.py:228
  119.4 6.6 %all-to-all-start.3 = ((f32[16,144,128]{2,1,0:T(8,128)}), f32[16,144,128]{2,1,0:T(8,128)S(1)}, u32[]{:S(2)}, u32[]{:S(2)}) async-start(f32[16,144,128]{2,1,0:T(8,128)} %forward.4), calls=%async_computation.3 | async-start | bytes 2359296 | tf_op jit(solution)/shard_map/all_to_all | solution.py:433
  126.0 8.3 %mirror.4 = f32[8,128,128]{2,1,0:T(8,128)S(1)} custom-call(s32[256]{0:T(256)S(1)} %copy-done, s32[256]{0:T(256)S(1)} %copy-done.1, s32[1]{0:T(128)} %bitcast.3.count, bf16[256,128,256]{2,1,0:T(8,128)(2,1)} %get-tuple-element.18.far_ref, f32[16,128,128]{2,1,0:T(8,128)S(1)} %all-to-all-done.4.refs_0_), custom_call_target="tpu_custom_call" | custom-call | bytes 31457280 | tf_op jit(solution)/shard_map/mirror/pallas_call | solution.py:228
  137.0 2.6 %collective-permute-start.18 = (f32[1,128,128]{2,1,0:T(8,128)S(1)}, f32[1,128,128]{2,1,0:T(8,128)S(1)}, u32[]{:S(2)}, u32[]{:S(2)}) collective-permute-start(f32[1,128,128]{2,1,0:T(8,128)S(1)} %get-tuple-element.30), channel_id=1, source_target_pairs={{0,64},{16,80},{32,96},{48,112},{64,0},{80,16},{96,32},{112,48},{1... | collective-permute-start | bytes 196616 | tf_op jit(solution)/shard_map/ppermute | solution.py:425
  139.7 3.8 %all-to-all-done.3.wide_ref.refs_0_ = f32[16,144,128]{2,1,0:T(8,128)S(1)} async-done(((f32[16,144,128]{2,1,0:T(8,128)}), f32[16,144,128]{2,1,0:T(8,128)S(1)}, u32[]{:S(2)}, u32[]{:S(2)}) %all-to-all-start.3) | async-done | bytes 1179680 | tf_op jit(solution)/shard_map/all_to_all | solution.py:433
  143.4 1.8 turn.2.refs_6_
  147.3 5.3 %all-to-all-start.6 = ((f32[16,128,128]{2,1,0:T(8,128)}), f32[16,128,128]{2,1,0:T(8,128)S(1)}, u32[]{:S(2)}, u32[]{:S(2)}) async-start(f32[16,128,128]{2,1,0:T(8,128)} %broadcast_in_dim.65), calls=%async_computation.6 | async-start | bytes 2097152 | tf_op jit(solution)/shard_map/all_to_all | solution.py:433
  153.7 2.5 %collective-permute-start.21 = (f32[144,128]{1,0:T(8,128)S(1)}, f32[144,128]{1,0:T(8,128)S(1)}, u32[]{:S(2)}, u32[]{:S(2)}) collective-permute-start(f32[144,128]{1,0:T(8,128)S(1)} %get-tuple-element.21), channel_id=1, source_target_pairs={{0,64},{16,80},{32,96},{48,112},{64,0},{80,16},{96,32},{112,48},{1... | collective-permute-start | bytes 221192 | tf_op jit(solution)/shard_map/ppermute | solution.py:425
  159.6 3.0 %collective-permute-start.23 = (f32[4,144,128]{2,1,0:T(8,128)S(1)}, f32[4,144,128]{2,1,0:T(8,128)S(1)}, u32[]{:S(2)}, u32[]{:S(2)}) collective-permute-start(f32[4,144,128]{2,1,0:T(8,128)S(1)} %pad_maximum_fusion.1.refs_0_), channel_id=1, source_target_pairs={{0,16},{16,0},{32,48},{48,32},{64,80},{80,64},{96,112},{112,96},{1... | collective-permute-start | bytes 884744 | tf_op jit(solution)/shard_map/ppermute | solution.py:429
  163.8 7.6 %forward.5 = f32[16,144,128]{2,1,0:T(8,128)} custom-call(s32[256]{0:T(256)S(1)} %get-tuple-element.44.takes, s32[256]{0:T(256)S(1)} %copy-done, s32[1]{0:T(128)} %bitcast.3.count, bf16[256,128,256]{2,1,0:T(8,128)(2,1)} %get-tuple-element.15.far_ref, f32[4,144,128]{2,1,0:T(8,128)S(1)} %pad_maximum_fusion.1.refs_0_, ...), custom_call_target="tpu_custom_call" | custom-call | bytes 31457280 | tf_op jit(solution)/shard_map/forward/pallas_call | solution.py:228
  171.5 6.6 %all-to-all-start.5 = ((f32[16,144,128]{2,1,0:T(8,128)}), f32[16,144,128]{2,1,0:T(8,128)S(1)}, u32[]{:S(2)}, u32[]{:S(2)}) async-start(f32[16,144,128]{2,1,0:T(8,128)} %forward.5), calls=%async_computation.5 | async-start | bytes 2359296 | tf_op jit(solution)/shard_map/all_to_all | solution.py:433
  178.0 8.3 %mirror.5 = f32[8,128,128]{2,1,0:T(8,128)S(1)} custom-call(s32[256]{0:T(256)S(1)} %copy-done, s32[256]{0:T(256)S(1)} %copy-done.1, s32[1]{0:T(128)} %bitcast.3.count, bf16[256,128,256]{2,1,0:T(8,128)(2,1)} %get-tuple-element.18.far_ref, f32[16,128,128]{2,1,0:T(8,128)S(1)} %all-to-all-done.6.refs_0_), custom_call_target="tpu_custom_call" | custom-call | bytes 31457280 | tf_op jit(solution)/shard_map/mirror/pallas_call | solution.py:228
  188.8 2.6 %collective-permute-start.26 = (f32[1,128,128]{2,1,0:T(8,128)S(1)}, f32[1,128,128]{2,1,0:T(8,128)S(1)}, u32[]{:S(2)}, u32[]{:S(2)}) collective-permute-start(f32[1,128,128]{2,1,0:T(8,128)S(1)} %get-tuple-element.26), channel_id=1, source_target_pairs={{0,64},{16,80},{32,96},{48,112},{64,0},{80,16},{96,32},{112,48},{1... | collective-permute-start | bytes 196616 | tf_op jit(solution)/shard_map/ppermute | solution.py:425
  191.7 3.8 %all-to-all-done.5.wide_ref.refs_0_ = f32[16,144,128]{2,1,0:T(8,128)S(1)} async-done(((f32[16,144,128]{2,1,0:T(8,128)}), f32[16,144,128]{2,1,0:T(8,128)S(1)}, u32[]{:S(2)}, u32[]{:S(2)}) %all-to-all-start.5) | async-done | bytes 1179680 | tf_op jit(solution)/shard_map/all_to_all | solution.py:433
  195.5 1.8 turn.3.refs_6_
  198.4 2.8 %collective-permute-start.28 = (f32[1,8,128]{2,1,0:T(8,128)S(1)}, f32[1,8,128]{2,1,0:T(8,128)S(1)}, u32[]{:S(2)}, u32[]{:S(2)}) collective-permute-start(f32[1,8,128]{2,1,0:T(8,128)S(1)} %get-tuple-element.24), channel_id=1, source_target_pairs={{0,16},{16,0},{32,48},{48,32},{64,80},{80,64},{96,112},{112,96},{1... | collective-permute-start | bytes 12296 | tf_op jit(solution)/shard_map/ppermute | solution.py:429
  202.0 15.4 %all_to_all.40.gram_ref = f32[64,8,128]{2,1,0:T(8,128)S(1)} all-to-all(f32[64,8,128]{2,1,0:T(8,128)S(1)} %broadcast_in_dim.67), channel_id=1, replica_groups={{0,1,2,3,4,5,6,7,8,9,10,11,12,13,14,15,32,33,34,35,36,37,38,39,40,41,42..., dimensions={0} | all-to-all | bytes 524288 | tf_op jit(solution)/shard_map/all_to_all | solution.py:500
  217.4 3.0 %basis.1 = f32[2,32,256]{2,1,0:T(8,128)} custom-call(f32[128,128]{1,0:T(8,128)S(1)} %get-tuple-element.23.image_ref, f32[64,8,128]{2,1,0:T(8,128)S(1)} %all_to_all.40.gram_ref), custom_call_target="tpu_custom_call" | custom-call | tf_op jit(solution)/shard_map/basis/pallas_call | solution.py:415
  (102 shorter events, 44.6 us)
Async XLA Ops:
  24.5 9.3 %collective-permute-start = (f32[4,8,128]{2,1,0:T(8,128)S(1)}, f32[4,8,128]{2,1,0:T(8,128)S(1)}, u32[]{:S(2)}, u32[]{:S(2)}) collective-permute-start(f32[4,8,128]{2,1,0:T(8,128)S(1)} %slice.84), channel_id=1, source_target_pairs={{0,16},{16,0},{32,48},{48,32},{64,80},{80,64},{96,112},{112,96},{1... | collective-permute-start | bytes 49160 | tf_op jit(solution)/shard_map/ppermute | solution.py:429
  25.9 14.4 %all-to-all-start = ((f32[16,8,128]{2,1,0:T(8,128)}), f32[16,8,128]{2,1,0:T(8,128)S(1)}, u32[]{:S(2)}, u32[]{:S(2)}) async-start(f32[16,8,128]{2,1,0:T(8,128)} %get-tuple-element.16), calls=%async_computation | async-start | bytes 131072 | tf_op jit(solution)/shard_map/all_to_all | solution.py:433
  34.5 5.8 %collective-permute-start.1 = (f32[1,8,128]{2,1,0:T(8,128)S(1)}, f32[1,8,128]{2,1,0:T(8,128)S(1)}, u32[]{:S(2)}, u32[]{:S(2)}) collective-permute-start(f32[1,8,128]{2,1,0:T(8,128)S(1)} %get-tuple-element.37), channel_id=1, source_target_pairs={{0,32},{16,48},{32,64},{48,80},{64,96},{80,112},{96,0},{112,16},{1... | collective-permute-start | bytes 12296 | tf_op jit(solution)/shard_map/ppermute | solution.py:425
  36.0 4.7 %collective-permute-start.2 = (f32[1,8,128]{2,1,0:T(8,128)S(1)}, f32[1,8,128]{2,1,0:T(8,128)S(1)}, u32[]{:S(2)}, u32[]{:S(2)}) collective-permute-start(f32[1,8,128]{2,1,0:T(8,128)S(1)} %get-tuple-element.39), channel_id=1, source_target_pairs={{0,64},{16,80},{32,96},{48,112},{64,0},{80,16},{96,32},{112,48},{1... | collective-permute-start | bytes 12296 | tf_op jit(solution)/shard_map/ppermute | solution.py:425
  42.9 24.7 %all-to-all-start.2 = ((bf16[16,128,128]{2,1,0:T(8,128)(2,1)}), bf16[16,128,128]{2,1,0:T(8,128)(2,1)S(1)}, u32[]{:S(2)}, u32[]{:S(2)}) async-start(bf16[16,128,128]{2,1,0:T(8,128)(2,1)} %broadcast_in_dim.63), calls=%async_computation.2 | async-start | bytes 1048576 | tf_op jit(solution)/shard_map/all_to_all | solution.py:433
  49.7 4.0 %collective-permute-start.4 = (bf16[128,128]{1,0:T(8,128)(2,1)S(1)}, bf16[128,128]{1,0:T(8,128)(2,1)S(1)}, u32[]{:S(2)}, u32[]{:S(2)}) collective-permute-start(bf16[128,128]{1,0:T(8,128)(2,1)S(1)} %multiply_convert_fusion), channel_id=1, source_target_pairs={{0,32},{16,48},{32,64},{48,80},{64,96},{80,112},{96,0},{112,16},{1... | collective-permute-start | bytes 98312 | tf_op jit(solution)/shard_map/ppermute | solution.py:425
  49.7 4.3 %collective-permute-start.5 = (bf16[128,128]{1,0:T(8,128)(2,1)S(1)}, bf16[128,128]{1,0:T(8,128)(2,1)S(1)}, u32[]{:S(2)}, u32[]{:S(2)}) collective-permute-start(bf16[128,128]{1,0:T(8,128)(2,1)S(1)} %multiply_convert_fusion), channel_id=1, source_target_pairs={{0,64},{16,80},{32,96},{48,112},{64,0},{80,16},{96,32},{112,48},{1... | collective-permute-start | bytes 98312 | tf_op jit(solution)/shard_map/ppermute | solution.py:425
  52.4 2.8 %collective-permute-start.6 = (bf16[128,128]{1,0:T(8,128)(2,1)S(1)}, bf16[128,128]{1,0:T(8,128)(2,1)S(1)}, u32[]{:S(2)}, u32[]{:S(2)}) collective-permute-start(bf16[128,128]{1,0:T(8,128)(2,1)S(1)} %multiply_convert_fusion), channel_id=1, source_target_pairs={{0,96},{16,112},{32,0},{48,16},{64,32},{80,48},{96,64},{112,80},{1... | collective-permute-start | bytes 98312 | tf_op jit(solution)/shard_map/ppermute | solution.py:425
  55.2 4.8 %collective-permute-start.7 = (bf16[4,128,128]{2,1,0:T(8,128)(2,1)S(1)}, bf16[4,128,128]{2,1,0:T(8,128)(2,1)S(1)}, u32[]{:S(2)}, u32[]{:S(2)}) collective-permute-start(bf16[4,128,128]{2,1,0:T(8,128)(2,1)S(1)} %pad_maximum_fusion.2.refs_0_), channel_id=1, source_target_pairs={{0,16},{16,0},{32,48},{48,32},{64,80},{80,64},{96,112},{112,96},{1... | collective-permute-start | bytes 393224 | tf_op jit(solution)/shard_map/ppermute | solution.py:429
  67.6 24.9 %all-to-all-start.1 = ((f32[16,128,128]{2,1,0:T(8,128)}), f32[16,128,128]{2,1,0:T(8,128)S(1)}, u32[]{:S(2)}, u32[]{:S(2)}) async-start(f32[16,128,128]{2,1,0:T(8,128)} %forward.3), calls=%async_computation.1 | async-start | bytes 2097152 | tf_op jit(solution)/shard_map/all_to_all | solution.py:433
  84.8 4.7 %collective-permute-start.10 = (f32[1,128,128]{2,1,0:T(8,128)S(1)}, f32[1,128,128]{2,1,0:T(8,128)S(1)}, u32[]{:S(2)}, u32[]{:S(2)}) collective-permute-start(f32[1,128,128]{2,1,0:T(8,128)S(1)} %get-tuple-element.34), channel_id=1, source_target_pairs={{0,64},{16,80},{32,96},{48,112},{64,0},{80,16},{96,32},{112,48},{1... | collective-permute-start | bytes 196616 | tf_op jit(solution)/shard_map/ppermute | solution.py:425
  85.9 4.9 %collective-permute-start.11 = (f32[1,128,128]{2,1,0:T(8,128)S(1)}, f32[1,128,128]{2,1,0:T(8,128)S(1)}, u32[]{:S(2)}, u32[]{:S(2)}) collective-permute-start(f32[1,128,128]{2,1,0:T(8,128)S(1)} %get-tuple-element.33), channel_id=1, source_target_pairs={{0,96},{16,112},{32,0},{48,16},{64,32},{80,48},{96,64},{112,80},{1... | collective-permute-start | bytes 196616 | tf_op jit(solution)/shard_map/ppermute | solution.py:425
  87.9 4.6 %collective-permute-start.9 = (f32[1,128,128]{2,1,0:T(8,128)S(1)}, f32[1,128,128]{2,1,0:T(8,128)S(1)}, u32[]{:S(2)}, u32[]{:S(2)}) collective-permute-start(f32[1,128,128]{2,1,0:T(8,128)S(1)} %get-tuple-element.35), channel_id=1, source_target_pairs={{0,32},{16,48},{32,64},{48,80},{64,96},{80,112},{96,0},{112,16},{1... | collective-permute-start | bytes 196616 | tf_op jit(solution)/shard_map/ppermute | solution.py:425
  94.1 25.3 %all-to-all-start.4 = ((f32[16,128,128]{2,1,0:T(8,128)}), f32[16,128,128]{2,1,0:T(8,128)S(1)}, u32[]{:S(2)}, u32[]{:S(2)}) async-start(f32[16,128,128]{2,1,0:T(8,128)} %broadcast_in_dim.64), calls=%async_computation.4 | async-start | bytes 2097152 | tf_op jit(solution)/shard_map/all_to_all | solution.py:433
  100.8 4.5 %collective-permute-start.12 = (f32[144,128]{1,0:T(8,128)S(1)}, f32[144,128]{1,0:T(8,128)S(1)}, u32[]{:S(2)}, u32[]{:S(2)}) collective-permute-start(f32[144,128]{1,0:T(8,128)S(1)} %get-tuple-element.19), channel_id=1, source_target_pairs={{0,32},{16,48},{32,64},{48,80},{64,96},{80,112},{96,0},{112,16},{1... | collective-permute-start | bytes 221192 | tf_op jit(solution)/shard_map/ppermute | solution.py:425
  100.9 5.9 %collective-permute-start.13 = (f32[144,128]{1,0:T(8,128)S(1)}, f32[144,128]{1,0:T(8,128)S(1)}, u32[]{:S(2)}, u32[]{:S(2)}) collective-permute-start(f32[144,128]{1,0:T(8,128)S(1)} %get-tuple-element.19), channel_id=1, source_target_pairs={{0,64},{16,80},{32,96},{48,112},{64,0},{80,16},{96,32},{112,48},{1... | collective-permute-start | bytes 221192 | tf_op jit(solution)/shard_map/ppermute | solution.py:425
  104.0 3.2 %collective-permute-start.14 = (f32[144,128]{1,0:T(8,128)S(1)}, f32[144,128]{1,0:T(8,128)S(1)}, u32[]{:S(2)}, u32[]{:S(2)}) collective-permute-start(f32[144,128]{1,0:T(8,128)S(1)} %get-tuple-element.19), channel_id=1, source_target_pairs={{0,96},{16,112},{32,0},{48,16},{64,32},{80,48},{96,64},{112,80},{1... | collective-permute-start | bytes 221192 | tf_op jit(solution)/shard_map/ppermute | solution.py:425
  107.3 4.5 %collective-permute-start.15 = (f32[4,144,128]{2,1,0:T(8,128)S(1)}, f32[4,144,128]{2,1,0:T(8,128)S(1)}, u32[]{:S(2)}, u32[]{:S(2)}) collective-permute-start(f32[4,144,128]{2,1,0:T(8,128)S(1)} %pad_maximum_fusion.refs_0_), channel_id=1, source_target_pairs={{0,16},{16,0},{32,48},{48,32},{64,80},{80,64},{96,112},{112,96},{1... | collective-permute-start | bytes 884744 | tf_op jit(solution)/shard_map/ppermute | solution.py:429
  119.4 24.0 %all-to-all-start.3 = ((f32[16,144,128]{2,1,0:T(8,128)}), f32[16,144,128]{2,1,0:T(8,128)S(1)}, u32[]{:S(2)}, u32[]{:S(2)}) async-start(f32[16,144,128]{2,1,0:T(8,128)} %forward.4), calls=%async_computation.3 | async-start | bytes 2359296 | tf_op jit(solution)/shard_map/all_to_all | solution.py:433
  136.6 8.7 %collective-permute-start.17 = (f32[1,128,128]{2,1,0:T(8,128)S(1)}, f32[1,128,128]{2,1,0:T(8,128)S(1)}, u32[]{:S(2)}, u32[]{:S(2)}) collective-permute-start(f32[1,128,128]{2,1,0:T(8,128)S(1)} %get-tuple-element.31), channel_id=1, source_target_pairs={{0,32},{16,48},{32,64},{48,80},{64,96},{80,112},{96,0},{112,16},{1... | collective-permute-start | bytes 196616 | tf_op jit(solution)/shard_map/ppermute | solution.py:425
  137.0 8.2 %collective-permute-start.18 = (f32[1,128,128]{2,1,0:T(8,128)S(1)}, f32[1,128,128]{2,1,0:T(8,128)S(1)}, u32[]{:S(2)}, u32[]{:S(2)}) collective-permute-start(f32[1,128,128]{2,1,0:T(8,128)S(1)} %get-tuple-element.30), channel_id=1, source_target_pairs={{0,64},{16,80},{32,96},{48,112},{64,0},{80,16},{96,32},{112,48},{1... | collective-permute-start | bytes 196616 | tf_op jit(solution)/shard_map/ppermute | solution.py:425
  139.7 5.6 %collective-permute-start.19 = (f32[1,128,128]{2,1,0:T(8,128)S(1)}, f32[1,128,128]{2,1,0:T(8,128)S(1)}, u32[]{:S(2)}, u32[]{:S(2)}) collective-permute-start(f32[1,128,128]{2,1,0:T(8,128)S(1)} %get-tuple-element.29), channel_id=1, source_target_pairs={{0,96},{16,112},{32,0},{48,16},{64,32},{80,48},{96,64},{112,80},{1... | collective-permute-start | bytes 196616 | tf_op jit(solution)/shard_map/ppermute | solution.py:425
  147.3 24.2 %all-to-all-start.6 = ((f32[16,128,128]{2,1,0:T(8,128)}), f32[16,128,128]{2,1,0:T(8,128)S(1)}, u32[]{:S(2)}, u32[]{:S(2)}) async-start(f32[16,128,128]{2,1,0:T(8,128)} %broadcast_in_dim.65), calls=%async_computation.6 | async-start | bytes 2097152 | tf_op jit(solution)/shard_map/all_to_all | solution.py:433
  152.6 4.5 %collective-permute-start.20 = (f32[144,128]{1,0:T(8,128)S(1)}, f32[144,128]{1,0:T(8,128)S(1)}, u32[]{:S(2)}, u32[]{:S(2)}) collective-permute-start(f32[144,128]{1,0:T(8,128)S(1)} %get-tuple-element.21), channel_id=1, source_target_pairs={{0,32},{16,48},{32,64},{48,80},{64,96},{80,112},{96,0},{112,16},{1... | collective-permute-start | bytes 221192 | tf_op jit(solution)/shard_map/ppermute | solution.py:425
  153.7 5.0 %collective-permute-start.21 = (f32[144,128]{1,0:T(8,128)S(1)}, f32[144,128]{1,0:T(8,128)S(1)}, u32[]{:S(2)}, u32[]{:S(2)}) collective-permute-start(f32[144,128]{1,0:T(8,128)S(1)} %get-tuple-element.21), channel_id=1, source_target_pairs={{0,64},{16,80},{32,96},{48,112},{64,0},{80,16},{96,32},{112,48},{1... | collective-permute-start | bytes 221192 | tf_op jit(solution)/shard_map/ppermute | solution.py:425
  156.1 3.5 %collective-permute-start.22 = (f32[144,128]{1,0:T(8,128)S(1)}, f32[144,128]{1,0:T(8,128)S(1)}, u32[]{:S(2)}, u32[]{:S(2)}) collective-permute-start(f32[144,128]{1,0:T(8,128)S(1)} %get-tuple-element.21), channel_id=1, source_target_pairs={{0,96},{16,112},{32,0},{48,16},{64,32},{80,48},{96,64},{112,80},{1... | collective-permute-start | bytes 221192 | tf_op jit(solution)/shard_map/ppermute | solution.py:425
  159.6 4.2 %collective-permute-start.23 = (f32[4,144,128]{2,1,0:T(8,128)S(1)}, f32[4,144,128]{2,1,0:T(8,128)S(1)}, u32[]{:S(2)}, u32[]{:S(2)}) collective-permute-start(f32[4,144,128]{2,1,0:T(8,128)S(1)} %pad_maximum_fusion.1.refs_0_), channel_id=1, source_target_pairs={{0,16},{16,0},{32,48},{48,32},{64,80},{80,64},{96,112},{112,96},{1... | collective-permute-start | bytes 884744 | tf_op jit(solution)/shard_map/ppermute | solution.py:429
  171.5 24.0 %all-to-all-start.5 = ((f32[16,144,128]{2,1,0:T(8,128)}), f32[16,144,128]{2,1,0:T(8,128)S(1)}, u32[]{:S(2)}, u32[]{:S(2)}) async-start(f32[16,144,128]{2,1,0:T(8,128)} %forward.5), calls=%async_computation.5 | async-start | bytes 2359296 | tf_op jit(solution)/shard_map/all_to_all | solution.py:433
  188.6 8.7 %collective-permute-start.25 = (f32[1,128,128]{2,1,0:T(8,128)S(1)}, f32[1,128,128]{2,1,0:T(8,128)S(1)}, u32[]{:S(2)}, u32[]{:S(2)}) collective-permute-start(f32[1,128,128]{2,1,0:T(8,128)S(1)} %get-tuple-element.27), channel_id=1, source_target_pairs={{0,32},{16,48},{32,64},{48,80},{64,96},{80,112},{96,0},{112,16},{1... | collective-permute-start | bytes 196616 | tf_op jit(solution)/shard_map/ppermute | solution.py:425
  188.8 8.5 %collective-permute-start.26 = (f32[1,128,128]{2,1,0:T(8,128)S(1)}, f32[1,128,128]{2,1,0:T(8,128)S(1)}, u32[]{:S(2)}, u32[]{:S(2)}) collective-permute-start(f32[1,128,128]{2,1,0:T(8,128)S(1)} %get-tuple-element.26), channel_id=1, source_target_pairs={{0,64},{16,80},{32,96},{48,112},{64,0},{80,16},{96,32},{112,48},{1... | collective-permute-start | bytes 196616 | tf_op jit(solution)/shard_map/ppermute | solution.py:425
  191.4 5.9 %collective-permute-start.27 = (f32[1,128,128]{2,1,0:T(8,128)S(1)}, f32[1,128,128]{2,1,0:T(8,128)S(1)}, u32[]{:S(2)}, u32[]{:S(2)}) collective-permute-start(f32[1,128,128]{2,1,0:T(8,128)S(1)} %get-tuple-element.25), channel_id=1, source_target_pairs={{0,96},{16,112},{32,0},{48,16},{64,32},{80,48},{96,64},{112,80},{1... | collective-permute-start | bytes 196616 | tf_op jit(solution)/shard_map/ppermute | solution.py:425
  198.4 3.6 %collective-permute-start.28 = (f32[1,8,128]{2,1,0:T(8,128)S(1)}, f32[1,8,128]{2,1,0:T(8,128)S(1)}, u32[]{:S(2)}, u32[]{:S(2)}) collective-permute-start(f32[1,8,128]{2,1,0:T(8,128)S(1)} %get-tuple-element.24), channel_id=1, source_target_pairs={{0,16},{16,0},{32,48},{48,32},{64,80},{80,64},{96,112},{112,96},{1... | collective-permute-start | bytes 12296 | tf_op jit(solution)/shard_map/ppermute | solution.py:429
  (7 other events, 111.8 us)

commit v5 on v4

--- a/solution.py
+++ b/solution.py
@@ -15,7 +15,7 @@
 ROW_BLOCKS = 32
 COL_BLOCKS = 16
 CHUNK = 16
-TRIG_CHUNK = 8
+TRIG_CHUNK = 16
 HALF_SIN = (0.5, -0.020833322778344154, 0.00026040783268399537, -1.5475804957532091e-06, 5.088141019626846e-09)
 HALF_COS = (0.9999999403953552, -0.1249997615814209, 0.0026039734948426485, -2.164632678613998e-05, 9.044046578310372e-08)
 HIGHEST = lax.Precision.HIGHEST
@@ -59,7 +59,7 @@
 
 
 def tiles_kernel(
-    order, rows, cols, count, far_w, far_a, far_plain, far_turned, row_ref, col_ref,
+    order, rows, cols, count, far_w, far_a, far_plain, far_turned, row_ref, own_ref, other_ref,
     w_ref, a_ref, plain, turned, row_acc, col_acc, w_sems, a_sems, out_sems,
 ):
     def start(c, carry):
@@ -120,21 +120,28 @@
         row_ref[p] = 0.5 * jnp.concatenate(sums * 4, axis=0)
     for p in range(COL_BLOCKS // 2):
         sums = [jnp.sum(col_acc[2 * p + k], axis=0, keepdims=True) for k in range(2)]
-        col_ref[p] = 0.5 * jnp.concatenate(sums * 4, axis=0)
-    for back in (2, 1):
-        for copy in outgoing(chunks - back):
+        col_ref = own_ref if p < 4 else other_ref
+        col_ref[p % 4] = 0.5 * jnp.concatenate(sums * 4, axis=0)
+
+    @pl.when(chunks >= 2)
+    def _():
+        for copy in outgoing(chunks - 2):
             copy.wait()
+
+    for copy in outgoing(chunks - 1):
+        copy.wait()
 
 
 def complex_tiles(order, rows, cols, count, weights, angles):
     return pl.pallas_call(
         tiles_kernel,
         in_specs=[SCALAR] * 4 + [FAR, FAR],
-        out_specs=[FAR, FAR, VECTOR, VECTOR],
+        out_specs=[FAR, FAR, VECTOR, VECTOR, VECTOR],
         out_shape=[jax.ShapeDtypeStruct((SLOTS, TILE, 2 * TILE), jnp.bfloat16)] * 2
         + [
             jax.ShapeDtypeStruct((ROW_BLOCKS // 2, 8, TILE), jnp.float32),
-            jax.ShapeDtypeStruct((COL_BLOCKS // 2, 8, TILE), jnp.float32),
+            jax.ShapeDtypeStruct((COL_BLOCKS // 4, 8, TILE), jnp.float32),
+            jax.ShapeDtypeStruct((COL_BLOCKS // 4, 8, TILE), jnp.float32),
         ],
         scratch_shapes=[
             pltpu.VMEM((SLOTS, TILE, TILE), jnp.bfloat16),
@@ -251,6 +258,11 @@
     if turned:
         image = nt_dot(image, rest[0][...])
         rest = rest[1:]
+    copies = []
+    if not final:
+        body_ref, far_ref, sems = rest
+        body_ref[:TILE] = image * scale
+        copies = spread_copies(body_ref.at[pl.ds(0, TILE)], far_ref, sems)
     across = image.T
     gram = nt_dot(across, across)
     pairs = gram[: 2 * WIDTH] + pltpu.roll(gram[2 * WIDTH :], 2 * WIDTH, 1)
@@ -269,14 +281,53 @@
             out = jnp.where(group == g, pltpu.roll(packed[8 * g : 8 * g + 8], WIDTH * g, 1), out)
         gram_ref[0] = out
     else:
-        sent_ref, body_ref = rest
-        value = image * scale
-        sent_ref[...] = value
-        body_ref[:TILE] = value
         low = lanes((WIDTH // 2, TILE)) < 2 * WIDTH
         body_ref[TILE:] = jnp.where(
             low, both[: WIDTH // 2], pltpu.roll(both[WIDTH // 2 :], 2 * WIDTH, 1)
         )
+    for copy in copies:
+        copy.wait()
+
+
+def spread_copies(source, target, sems):
+    copies = [pltpu.make_async_copy(source, target.at[p], sems.at[p]) for p in range(16)]
+    for copy in copies:
+        copy.start()
+    return copies
+
+
+def first_kernel(n_parts, *refs):
+    wide_ref, part_refs = refs[0], refs[1 : 1 + n_parts]
+    basis_ref, scale_ref, sent_ref, far_ref, sems = refs[1 + n_parts :]
+    degree = wide_ref[0]
+    for p in range(1, wide_ref.shape[0]):
+        degree = degree + wide_ref[p]
+    for ref in part_refs:
+        degree = degree + ref[0]
+    factor = lax.rsqrt(degree)
+    row = lax.broadcasted_iota(jnp.int32, (TILE, TILE), 0)
+    scale = jnp.where(row < 2 * WIDTH, factor[0:1], factor[1:2]).T
+    scale_ref[...] = scale
+    sent_ref[...] = (basis_ref[...] * scale).astype(jnp.bfloat16)
+    for copy in spread_copies(sent_ref, far_ref, sems):
+        copy.wait()
+
+
+def first_block(wide, parts, basis):
+    return pl.pallas_call(
+        functools.partial(first_kernel, len(parts)),
+        in_specs=[VECTOR] * (len(parts) + 2),
+        out_specs=[VECTOR, VECTOR, FAR],
+        out_shape=[
+            jax.ShapeDtypeStruct((TILE, TILE), jnp.float32),
+            jax.ShapeDtypeStruct((TILE, TILE), jnp.bfloat16),
+            jax.ShapeDtypeStruct((16, TILE, TILE), jnp.bfloat16),
+        ],
+        scratch_shapes=[pltpu.SemaphoreType.DMA((16,))],
+        compiler_params=pltpu.CompilerParams(vmem_limit_bytes=6 * MIB),
+        cost_estimate=pl.CostEstimate(flops=0, bytes_accessed=6 * MIB, transcendentals=0),
+        name="first_block",
+    )(wide, *parts, basis)
 
 
 def nt_dot(left, right):
@@ -287,13 +338,16 @@
 
 def new_image(wide, parts, scale, turn, final):
     operands = [wide, *parts, scale] + ([] if turn is None else [turn])
-    second = (1, 8, TILE) if final else (TILE + WIDTH // 2, TILE)
+    if final:
+        shapes = [(TILE, TILE), (1, 8, TILE)]
+    else:
+        shapes = [(TILE + WIDTH // 2, TILE), (16, TILE, TILE)]
     return pl.pallas_call(
         functools.partial(gather_kernel, turn is not None, final, len(parts)),
-        out_shape=[
-            jax.ShapeDtypeStruct((TILE, TILE), jnp.float32),
-            jax.ShapeDtypeStruct(second, jnp.float32),
-        ],
+        in_specs=[VECTOR] * len(operands),
+        out_specs=[VECTOR, VECTOR if final else FAR],
+        out_shape=[jax.ShapeDtypeStruct(shape, jnp.float32) for shape in shapes],
+        scratch_shapes=[] if final else [pltpu.SemaphoreType.DMA((16,))],
         compiler_params=pltpu.CompilerParams(vmem_limit_bytes=6 * MIB),
         cost_estimate=pl.CostEstimate(flops=0, bytes_accessed=6 * MIB, transcendentals=0),
         name="new_image",
@@ -440,7 +494,11 @@
 
 def reduce_row(value):
     half = value.shape[0] // 2
-    mine = value[:half] + other_core(value[half:])
+    return scatter_x(value[:half], value[half:])
+
+
+def scatter_x(own, other):
+    mine = own + other_core(other)
     return [mine[0:1]] + [along_x(mine[d : d + 1], d) for d in (1, 2, 3)]
 
 
@@ -472,21 +530,18 @@
     rows = jnp.where(slots < count, rows, ROW_BLOCKS)
     count = count.reshape(1)
 
-    plain, turned, row_part, col_part = complex_tiles(order, rows, puts_col, count, weights, angles)
+    plain, turned, row_part, own_part, other_part = complex_tiles(order, rows, puts_col, count, weights, angles)
     row_part = to_column(row_part)
-    col_parts = reduce_row(col_part)
-    degree = jnp.sum(row_part, axis=0) + sum(c[0] for c in col_parts)
-    scale = lax.rsqrt(degree[:2])
-    scale = jnp.broadcast_to(scale.T[:, :, None], (TILE, 2, 2 * WIDTH)).reshape(TILE, TILE)
-
+    col_parts = scatter_x(own_part, other_part)
     basis = jnp.transpose(init_basis.reshape(2, WIDTH, 2, TILE), (3, 2, 0, 1)).reshape(TILE, TILE)
-    sent = (basis * scale).astype(jnp.bfloat16)
-    body, turn = sent, None
+    scale, sent, spread_out = first_block(row_part, col_parts, basis)
+    body, turn = None, None
     for rounds in range(ITERS):
-        near, far = gather_row(body)
-        column = to_column(jnp.broadcast_to(sent[None], (16, TILE, TILE)))
+        extra = 0 if body is None else WIDTH // 2
+        near, far = gather_row(sent if body is None else body)
+        column = to_column(spread_out)
         forward = products(
-            1.0, takes_col, rows, count, plain, [near, far], (16, body.shape[0], TILE), True, "forward"
+            1.0, takes_col, rows, count, plain, [near, far], (16, TILE + extra, TILE), True, "forward"
         )
         mirror = products(
             -1.0, rows, puts_col, count, turned, [column], (8, TILE, TILE), False, "mirror"
@@ -495,10 +550,13 @@
         parts = reduce_row(mirror)
         if rounds > 0:
             turn = turn_of(wide)
-        sent, body = new_image(wide, parts, scale, turn, rounds == ITERS - 1)
-    body = body + other_core(body)
+        if rounds < ITERS - 1:
+            body, spread_out = new_image(wide, parts, scale, turn, False)
+        else:
+            sent, gram = new_image(wide, parts, scale, turn, True)
+    gram = gram + other_core(gram)
     grams = lax.all_to_all(
-        jnp.broadcast_to(body, (64, 8, TILE)),
+        jnp.broadcast_to(gram, (64, 8, TILE)),
         ("row", "col"),
         split_axis=0,
         concat_axis=0,

time: 222 us -> 216 us (0.973)
  waiting for transfers between devices: 29.9 us -> 42.8 us
  starting transfers between devices: 88.7 us -> 80.8 us
  Pallas kernels: 75.2 us -> 71 us
  local copies, waits for them, and re-layouts: 5.41 us -> 1.38 us
    ppermute x21, starting transfers between devices: 25.2 us -> 15.6 us  [along_x(): lax.ppermute(value, 'row', [(i, (i + 2 * step) % 8) for i in range(8)])]
    ppermute x21, waiting for transfers between devices: 13.9 us -> 21 us  [along_x(): lax.ppermute(value, 'row', [(i, (i + 2 * step) % 8) for i in range(8)])]
    all_to_all x7, waiting for transfers between devices: 8.28 us -> 14 us  [to_column(): return lax.all_to_all(value, 'col', split_axis=0, concat_axis=0, tiled=True)]
    pallas_call x1, Pallas kernels: 18.3 us -> 14.9 us  [complex_tiles(): pl.pallas_call(tiles_kernel, in_specs=[SCALAR] * 4 + [FAR, FAR], out_spec...]
    broadcast_in_dim x5 -> x1, local copies, waits for them, and re-layouts: 3.06 us -> 0.02 us  [shards(): jnp.broadcast_to(gram, (64, 8, TILE))]
    pallas_call x6, Pallas kernels: 47.7 us -> 44.7 us  [products(): pl.pallas_call(functools.partial(product_kernel, sign, sizes, apart), in_...]
  transfers between devices with their start and end apart: 36 -> 36, of which waited for: 24 -> 22; matrix products, arithmetic and copies ran while one was open for 1% -> 1% of each run, Pallas kernels for 23% -> 22%
where the time goes in v5:
time: 216 us; the launch traced here: 215 us
  starting transfers between devices  80.8 us (37%)
  Pallas kernels  71 us (33%)
  waiting for transfers between devices  42.8 us (20%)
  blocking collectives  13.9 us (6%)
  other arithmetic  4.99 us (2%)
    all_to_all x7, starting transfers between devices, to_column(): return lax.all_to_all(value, 'col', split_axis=0, concat_axis=0, tiled=True)  46.2 us
    pallas_call x6, Pallas kernels, products(): pl.pallas_call(functools.partial(product_kernel, sign, sizes, apart), in_...  44.7 us
    ppermute x21, waiting for transfers between devices, along_x(): lax.ppermute(value, 'row', [(i, (i + 2 * step) % 8) for i in range(8)])  21 us
    ppermute x8, starting transfers between devices, other_core(): return lax.ppermute(value, 'row', [(i, i ^ 1) for i in range(8)])  18.9 us
    ppermute x21, starting transfers between devices, along_x(): lax.ppermute(value, 'row', [(i, (i + 2 * step) % 8) for i in range(8)])  15.6 us
    pallas_call x1, Pallas kernels, complex_tiles(): pl.pallas_call(tiles_kernel, in_specs=[SCALAR] * 4 + [FAR, FAR], out_spec...  14.9 us
    all_to_all x7, waiting for transfers between devices, to_column(): return lax.all_to_all(value, 'col', split_axis=0, concat_axis=0, tiled=True)  14 us
    all_to_all x1, blocking collectives, shards(): lax.all_to_all(jnp.broadcast_to(gram, (64, 8, TILE)), ('row', 'col'), spl...  13.9 us
  transfers between devices with their start and end apart: 36, of which 22 were waited for; matrix products, arithmetic and copies ran while one was open for 1% of the time, Pallas kernels for 22%

profile of v5, /device:TPU:1, one launch (start us, length us, event | category | flops | bytes accessed | tf_op | source)
XLA Modules:
  0.0 215.2 jit_solution(3946539103418665608)
XLA Ops:
  5.3 14.9 %complex_tiles.1 = (bf16[256,128,256]{2,1,0:T(8,128)(2,1)}, bf16[256,128,256]{2,1,0:T(8,128)(2,1)}, f32[16,8,128]{2,1,0:T(8,128)}, f32[4,8,128]{2,1,0:T(8,128)}, f32[4,8,128]{2,1,0:T(8,128)}) custom-call(s32[256]{0:T(256)} %get-tuple-element.52.order, s32[256]{0:T(256)} %get-tuple-element.54.rows.puts.takes, s32[256]{0:T(256)} %get-tuple-element.51.cols.puts, ...), custom_call_target="tpu_custom_call" | custom-call | bytes 52428800 | tf_op jit(solution)/shard_map/complex_tiles/pallas_call | solution.py:136
  20.1 3.9 %collective-permute-start = (f32[4,8,128]{2,1,0:T(8,128)}, f32[4,8,128]{2,1,0:T(8,128)S(1)}, u32[]{:S(2)}, u32[]{:S(2)}) collective-permute-start(f32[4,8,128]{2,1,0:T(8,128)} %get-tuple-element.22), channel_id=1, source_target_pairs={{0,16},{16,0},{32,48},{48,32},{64,80},{80,64},{96,112},{112,96},{1... | collective-permute-start | bytes 49160 | tf_op jit(solution)/shard_map/ppermute | solution.py:483
  24.0 7.0 %all-to-all-start = ((f32[16,8,128]{2,1,0:T(8,128)}), f32[16,8,128]{2,1,0:T(8,128)S(1)}, u32[]{:S(2)}, u32[]{:S(2)}) async-start(f32[16,8,128]{2,1,0:T(8,128)} %get-tuple-element.20), calls=%async_computation | async-start | bytes 131072 | tf_op jit(solution)/shard_map/all_to_all | solution.py:487
  31.8 3.3 %collective-permute-start.3 = (f32[1,8,128]{2,1,0:T(8,128)S(1)}, f32[1,8,128]{2,1,0:T(8,128)S(1)}, u32[]{:S(2)}, u32[]{:S(2)}) collective-permute-start(f32[1,8,128]{2,1,0:T(8,128)S(1)} %get-tuple-element.45), channel_id=1, source_target_pairs={{0,96},{16,112},{32,0},{48,16},{64,32},{80,48},{96,64},{112,80},{1... | collective-permute-start | bytes 12296 | tf_op jit(solution)/shard_map/ppermute | solution.py:479
  35.9 3.1 %collective-permute-done.2.refs_3_ = f32[1,8,128]{2,1,0:T(8,128)S(1)} collective-permute-done((f32[1,8,128]{2,1,0:T(8,128)S(1)}, f32[1,8,128]{2,1,0:T(8,128)S(1)}, u32[]{:S(2)}, u32[]{:S(2)}) %collective-permute-start.2) | collective-permute-done | bytes 4128 | tf_op jit(solution)/shard_map/ppermute | solution.py:479
  40.2 6.7 %all-to-all-start.2 = ((bf16[16,128,128]{2,1,0:T(8,128)(2,1)}), bf16[16,128,128]{2,1,0:T(8,128)(2,1)S(1)}, u32[]{:S(2)}, u32[]{:S(2)}) async-start(bf16[16,128,128]{2,1,0:T(8,128)(2,1)} %get-tuple-element.25), calls=%async_computation.2 | async-start | bytes 1048576 | tf_op jit(solution)/shard_map/all_to_all | solution.py:487
  49.7 2.1 collective-permute-done.5
  52.4 4.1 %collective-permute-start.7 = (bf16[4,128,128]{2,1,0:T(8,128)(2,1)S(1)}, bf16[4,128,128]{2,1,0:T(8,128)(2,1)S(1)}, u32[]{:S(2)}, u32[]{:S(2)}) collective-permute-start(bf16[4,128,128]{2,1,0:T(8,128)(2,1)S(1)} %pad_maximum_fusion.2.refs_0_), channel_id=1, source_target_pairs={{0,16},{16,0},{32,48},{48,32},{64,80},{80,64},{96,112},{112,96},{1... | collective-permute-start | bytes 393224 | tf_op jit(solution)/shard_map/ppermute | solution.py:483
  57.5 7.1 %forward.3 = f32[16,128,128]{2,1,0:T(8,128)} custom-call(s32[256]{0:T(256)S(1)} %get-tuple-element.53.takes, s32[256]{0:T(256)S(1)} %copy-done, s32[1]{0:T(128)} %bitcast.3.count, bf16[256,128,256]{2,1,0:T(8,128)(2,1)} %get-tuple-element.19.far_ref, bf16[4,128,128]{2,1,0:T(8,128)(2,1)S(1)} %pad_maximum_fusion.2.refs_0_, ...), custom_call_target="tpu_custom_call" | custom-call | bytes 31457280 | tf_op jit(solution)/shard_map/forward/pallas_call | solution.py:235
  64.7 7.3 %all-to-all-start.1 = ((f32[16,128,128]{2,1,0:T(8,128)}), f32[16,128,128]{2,1,0:T(8,128)S(1)}, u32[]{:S(2)}, u32[]{:S(2)}) async-start(f32[16,128,128]{2,1,0:T(8,128)} %forward.3), calls=%async_computation.1 | async-start | bytes 2097152 | tf_op jit(solution)/shard_map/all_to_all | solution.py:487
  72.0 7.8 %mirror.3 = f32[8,128,128]{2,1,0:T(8,128)S(1)} custom-call(s32[256]{0:T(256)S(1)} %copy-done, s32[256]{0:T(256)S(1)} %copy-done.1, s32[1]{0:T(128)} %bitcast.3.count, bf16[256,128,256]{2,1,0:T(8,128)(2,1)} %get-tuple-element.24.far_ref, bf16[16,128,128]{2,1,0:T(8,128)(2,1)S(1)} %all-to-all-done.2.refs_0_), custom_call_target="tpu_custom_call" | custom-call | bytes 31457280 | tf_op jit(solution)/shard_map/mirror/pallas_call | solution.py:235
  84.2 1.6 collective-permute-done.11.refs_4_
  85.9 2.4 %collective-permute-done.10.refs_3_ = f32[1,128,128]{2,1,0:T(8,128)S(1)} collective-permute-done((f32[1,128,128]{2,1,0:T(8,128)S(1)}, f32[1,128,128]{2,1,0:T(8,128)S(1)}, u32[]{:S(2)}, u32[]{:S(2)}) %collective-permute-start.10) | collective-permute-done | bytes 65568 | tf_op jit(solution)/shard_map/ppermute | solution.py:479
  91.0 7.1 %all-to-all-start.4 = ((f32[16,128,128]{2,1,0:T(8,128)}), f32[16,128,128]{2,1,0:T(8,128)S(1)}, u32[]{:S(2)}, u32[]{:S(2)}) async-start(f32[16,128,128]{2,1,0:T(8,128)} %get-tuple-element.28), calls=%async_computation.4 | async-start | bytes 2097152 | tf_op jit(solution)/shard_map/all_to_all | solution.py:487
  99.6 1.7 collective-permute-done.14
  104.1 3.0 %collective-permute-start.15 = (f32[4,144,128]{2,1,0:T(8,128)S(1)}, f32[4,144,128]{2,1,0:T(8,128)S(1)}, u32[]{:S(2)}, u32[]{:S(2)}) collective-permute-start(f32[4,144,128]{2,1,0:T(8,128)S(1)} %pad_maximum_fusion.refs_0_), channel_id=1, source_target_pairs={{0,16},{16,0},{32,48},{48,32},{64,80},{80,64},{96,112},{112,96},{1... | collective-permute-start | bytes 884744 | tf_op jit(solution)/shard_map/ppermute | solution.py:483
  108.3 7.1 %forward.4 = f32[16,144,128]{2,1,0:T(8,128)} custom-call(s32[256]{0:T(256)S(1)} %get-tuple-element.53.takes, s32[256]{0:T(256)S(1)} %copy-done, s32[1]{0:T(128)} %bitcast.3.count, bf16[256,128,256]{2,1,0:T(8,128)(2,1)} %get-tuple-element.19.far_ref, f32[4,144,128]{2,1,0:T(8,128)S(1)} %pad_maximum_fusion.refs_0_, ...), custom_call_target="tpu_custom_call" | custom-call | bytes 31457280 | tf_op jit(solution)/shard_map/forward/pallas_call | solution.py:235
  115.5 7.3 %all-to-all-start.3 = ((f32[16,144,128]{2,1,0:T(8,128)}), f32[16,144,128]{2,1,0:T(8,128)S(1)}, u32[]{:S(2)}, u32[]{:S(2)}) async-start(f32[16,144,128]{2,1,0:T(8,128)} %forward.4), calls=%async_computation.3 | async-start | bytes 2359296 | tf_op jit(solution)/shard_map/all_to_all | solution.py:487
  122.7 7.8 %mirror.4 = f32[8,128,128]{2,1,0:T(8,128)S(1)} custom-call(s32[256]{0:T(256)S(1)} %copy-done, s32[256]{0:T(256)S(1)} %copy-done.1, s32[1]{0:T(128)} %bitcast.3.count, bf16[256,128,256]{2,1,0:T(8,128)(2,1)} %get-tuple-element.24.far_ref, f32[16,128,128]{2,1,0:T(8,128)S(1)} %all-to-all-done.4.refs_0_), custom_call_target="tpu_custom_call" | custom-call | bytes 31457280 | tf_op jit(solution)/shard_map/mirror/pallas_call | solution.py:235
  135.0 7.0 %all-to-all-done.3.wide_ref.refs_0_ = f32[16,144,128]{2,1,0:T(8,128)S(1)} async-done(((f32[16,144,128]{2,1,0:T(8,128)}), f32[16,144,128]{2,1,0:T(8,128)S(1)}, u32[]{:S(2)}, u32[]{:S(2)}) %all-to-all-start.3) | async-done | bytes 1179680 | tf_op jit(solution)/shard_map/all_to_all | solution.py:487
  142.0 1.8 turn.2.refs_6_
  145.4 3.8 %all-to-all-start.6 = ((f32[16,128,128]{2,1,0:T(8,128)}), f32[16,128,128]{2,1,0:T(8,128)S(1)}, u32[]{:S(2)}, u32[]{:S(2)}) async-start(f32[16,128,128]{2,1,0:T(8,128)} %get-tuple-element.30), calls=%async_computation.6 | async-start | bytes 2097152 | tf_op jit(solution)/shard_map/all_to_all | solution.py:487
  150.7 1.7 collective-permute-done.22
  152.4 1.9 collective-permute-done.21
  155.4 2.9 %collective-permute-start.23 = (f32[4,144,128]{2,1,0:T(8,128)S(1)}, f32[4,144,128]{2,1,0:T(8,128)S(1)}, u32[]{:S(2)}, u32[]{:S(2)}) collective-permute-start(f32[4,144,128]{2,1,0:T(8,128)S(1)} %pad_maximum_fusion.1.refs_0_), channel_id=1, source_target_pairs={{0,16},{16,0},{32,48},{48,32},{64,80},{80,64},{96,112},{112,96},{1... | collective-permute-start | bytes 884744 | tf_op jit(solution)/shard_map/ppermute | solution.py:483
  159.5 7.1 %forward.5 = f32[16,144,128]{2,1,0:T(8,128)} custom-call(s32[256]{0:T(256)S(1)} %get-tuple-element.53.takes, s32[256]{0:T(256)S(1)} %copy-done, s32[1]{0:T(128)} %bitcast.3.count, bf16[256,128,256]{2,1,0:T(8,128)(2,1)} %get-tuple-element.19.far_ref, f32[4,144,128]{2,1,0:T(8,128)S(1)} %pad_maximum_fusion.1.refs_0_, ...), custom_call_target="tpu_custom_call" | custom-call | bytes 31457280 | tf_op jit(solution)/shard_map/forward/pallas_call | solution.py:235
  166.7 7.1 %all-to-all-start.5 = ((f32[16,144,128]{2,1,0:T(8,128)}), f32[16,144,128]{2,1,0:T(8,128)S(1)}, u32[]{:S(2)}, u32[]{:S(2)}) async-start(f32[16,144,128]{2,1,0:T(8,128)} %forward.5), calls=%async_computation.5 | async-start | bytes 2359296 | tf_op jit(solution)/shard_map/all_to_all | solution.py:487
  173.8 7.8 %mirror.5 = f32[8,128,128]{2,1,0:T(8,128)S(1)} custom-call(s32[256]{0:T(256)S(1)} %copy-done, s32[256]{0:T(256)S(1)} %copy-done.1, s32[1]{0:T(128)} %bitcast.3.count, bf16[256,128,256]{2,1,0:T(8,128)(2,1)} %get-tuple-element.24.far_ref, f32[16,128,128]{2,1,0:T(8,128)S(1)} %all-to-all-done.6.refs_0_), custom_call_target="tpu_custom_call" | custom-call | bytes 31457280 | tf_op jit(solution)/shard_map/mirror/pallas_call | solution.py:235
  186.1 7.0 %all-to-all-done.5.wide_ref.refs_0_ = f32[16,144,128]{2,1,0:T(8,128)S(1)} async-done(((f32[16,144,128]{2,1,0:T(8,128)}), f32[16,144,128]{2,1,0:T(8,128)S(1)}, u32[]{:S(2)}, u32[]{:S(2)}) %all-to-all-start.5) | async-done | bytes 1179680 | tf_op jit(solution)/shard_map/all_to_all | solution.py:487
  193.1 1.8 turn.3.refs_6_
  198.4 13.9 %all_to_all.40.gram_ref = f32[64,8,128]{2,1,0:T(8,128)S(1)} all-to-all(f32[64,8,128]{2,1,0:T(8,128)S(1)} %broadcast_in_dim.39), channel_id=1, replica_groups={{0,1,2,3,4,5,6,7,8,9,10,11,12,13,14,15,32,33,34,35,36,37,38,39,40,41,42..., dimensions={0} | all-to-all | bytes 524288 | tf_op jit(solution)/shard_map/all_to_all | solution.py:558
  212.3 3.0 %basis.1 = f32[2,32,256]{2,1,0:T(8,128)} custom-call(f32[128,128]{1,0:T(8,128)S(1)} %get-tuple-element.31.image_ref, f32[64,8,128]{2,1,0:T(8,128)S(1)} %all_to_all.40.gram_ref), custom_call_target="tpu_custom_call" | custom-call | tf_op jit(solution)/shard_map/basis/pallas_call | solution.py:469
  (90 shorter events, 42.6 us)
Async XLA Ops:
  20.1 11.0 %collective-permute-start = (f32[4,8,128]{2,1,0:T(8,128)}, f32[4,8,128]{2,1,0:T(8,128)S(1)}, u32[]{:S(2)}, u32[]{:S(2)}) collective-permute-start(f32[4,8,128]{2,1,0:T(8,128)} %get-tuple-element.22), channel_id=1, source_target_pairs={{0,16},{16,0},{32,48},{48,32},{64,80},{80,64},{96,112},{112,96},{1... | collective-permute-start | bytes 49160 | tf_op jit(solution)/shard_map/ppermute | solution.py:483
  24.0 15.1 %all-to-all-start = ((f32[16,8,128]{2,1,0:T(8,128)}), f32[16,8,128]{2,1,0:T(8,128)S(1)}, u32[]{:S(2)}, u32[]{:S(2)}) async-start(f32[16,8,128]{2,1,0:T(8,128)} %get-tuple-element.20), calls=%async_computation | async-start | bytes 131072 | tf_op jit(solution)/shard_map/all_to_all | solution.py:487
  31.8 4.1 %collective-permute-start.3 = (f32[1,8,128]{2,1,0:T(8,128)S(1)}, f32[1,8,128]{2,1,0:T(8,128)S(1)}, u32[]{:S(2)}, u32[]{:S(2)}) collective-permute-start(f32[1,8,128]{2,1,0:T(8,128)S(1)} %get-tuple-element.45), channel_id=1, source_target_pairs={{0,96},{16,112},{32,0},{48,16},{64,32},{80,48},{96,64},{112,80},{1... | collective-permute-start | bytes 12296 | tf_op jit(solution)/shard_map/ppermute | solution.py:479
  35.1 4.0 %collective-permute-start.2 = (f32[1,8,128]{2,1,0:T(8,128)S(1)}, f32[1,8,128]{2,1,0:T(8,128)S(1)}, u32[]{:S(2)}, u32[]{:S(2)}) collective-permute-start(f32[1,8,128]{2,1,0:T(8,128)S(1)} %get-tuple-element.46), channel_id=1, source_target_pairs={{0,64},{16,80},{32,96},{48,112},{64,0},{80,16},{96,32},{112,48},{1... | collective-permute-start | bytes 12296 | tf_op jit(solution)/shard_map/ppermute | solution.py:479
  35.1 4.0 %collective-permute-start.1 = (f32[1,8,128]{2,1,0:T(8,128)S(1)}, f32[1,8,128]{2,1,0:T(8,128)S(1)}, u32[]{:S(2)}, u32[]{:S(2)}) collective-permute-start(f32[1,8,128]{2,1,0:T(8,128)S(1)} %get-tuple-element.47), channel_id=1, source_target_pairs={{0,32},{16,48},{32,64},{48,80},{64,96},{80,112},{96,0},{112,16},{1... | collective-permute-start | bytes 12296 | tf_op jit(solution)/shard_map/ppermute | solution.py:479
  40.2 24.5 %all-to-all-start.2 = ((bf16[16,128,128]{2,1,0:T(8,128)(2,1)}), bf16[16,128,128]{2,1,0:T(8,128)(2,1)S(1)}, u32[]{:S(2)}, u32[]{:S(2)}) async-start(bf16[16,128,128]{2,1,0:T(8,128)(2,1)} %get-tuple-element.25), calls=%async_computation.2 | async-start | bytes 1048576 | tf_op jit(solution)/shard_map/all_to_all | solution.py:487
  46.8 2.8 %collective-permute-start.6 = (bf16[128,128]{1,0:T(8,128)(2,1)S(1)}, bf16[128,128]{1,0:T(8,128)(2,1)S(1)}, u32[]{:S(2)}, u32[]{:S(2)}) collective-permute-start(bf16[128,128]{1,0:T(8,128)(2,1)S(1)} %get-tuple-element.23), channel_id=1, source_target_pairs={{0,96},{16,112},{32,0},{48,16},{64,32},{80,48},{96,64},{112,80},{1... | collective-permute-start | bytes 98312 | tf_op jit(solution)/shard_map/ppermute | solution.py:479
  47.5 4.3 %collective-permute-start.5 = (bf16[128,128]{1,0:T(8,128)(2,1)S(1)}, bf16[128,128]{1,0:T(8,128)(2,1)S(1)}, u32[]{:S(2)}, u32[]{:S(2)}) collective-permute-start(bf16[128,128]{1,0:T(8,128)(2,1)S(1)} %get-tuple-element.23), channel_id=1, source_target_pairs={{0,64},{16,80},{32,96},{48,112},{64,0},{80,16},{96,32},{112,48},{1... | collective-permute-start | bytes 98312 | tf_op jit(solution)/shard_map/ppermute | solution.py:479
  48.5 4.0 %collective-permute-start.4 = (bf16[128,128]{1,0:T(8,128)(2,1)S(1)}, bf16[128,128]{1,0:T(8,128)(2,1)S(1)}, u32[]{:S(2)}, u32[]{:S(2)}) collective-permute-start(bf16[128,128]{1,0:T(8,128)(2,1)S(1)} %get-tuple-element.23), channel_id=1, source_target_pairs={{0,32},{16,48},{32,64},{48,80},{64,96},{80,112},{96,0},{112,16},{1... | collective-permute-start | bytes 98312 | tf_op jit(solution)/shard_map/ppermute | solution.py:479
  52.4 5.1 %collective-permute-start.7 = (bf16[4,128,128]{2,1,0:T(8,128)(2,1)S(1)}, bf16[4,128,128]{2,1,0:T(8,128)(2,1)S(1)}, u32[]{:S(2)}, u32[]{:S(2)}) collective-permute-start(bf16[4,128,128]{2,1,0:T(8,128)(2,1)S(1)} %pad_maximum_fusion.2.refs_0_), channel_id=1, source_target_pairs={{0,16},{16,0},{32,48},{48,32},{64,80},{80,64},{96,112},{112,96},{1... | collective-permute-start | bytes 393224 | tf_op jit(solution)/shard_map/ppermute | solution.py:483
  64.7 25.1 %all-to-all-start.1 = ((f32[16,128,128]{2,1,0:T(8,128)}), f32[16,128,128]{2,1,0:T(8,128)S(1)}, u32[]{:S(2)}, u32[]{:S(2)}) async-start(f32[16,128,128]{2,1,0:T(8,128)} %forward.3), calls=%async_computation.1 | async-start | bytes 2097152 | tf_op jit(solution)/shard_map/all_to_all | solution.py:487
  82.2 3.7 %collective-permute-start.11 = (f32[1,128,128]{2,1,0:T(8,128)S(1)}, f32[1,128,128]{2,1,0:T(8,128)S(1)}, u32[]{:S(2)}, u32[]{:S(2)}) collective-permute-start(f32[1,128,128]{2,1,0:T(8,128)S(1)} %get-tuple-element.41), channel_id=1, source_target_pairs={{0,96},{16,112},{32,0},{48,16},{64,32},{80,48},{96,64},{112,80},{1... | collective-permute-start | bytes 196616 | tf_op jit(solution)/shard_map/ppermute | solution.py:479
  83.6 4.7 %collective-permute-start.10 = (f32[1,128,128]{2,1,0:T(8,128)S(1)}, f32[1,128,128]{2,1,0:T(8,128)S(1)}, u32[]{:S(2)}, u32[]{:S(2)}) collective-permute-start(f32[1,128,128]{2,1,0:T(8,128)S(1)} %get-tuple-element.42), channel_id=1, source_target_pairs={{0,64},{16,80},{32,96},{48,112},{64,0},{80,16},{96,32},{112,48},{1... | collective-permute-start | bytes 196616 | tf_op jit(solution)/shard_map/ppermute | solution.py:479
  83.9 5.9 %collective-permute-start.9 = (f32[1,128,128]{2,1,0:T(8,128)S(1)}, f32[1,128,128]{2,1,0:T(8,128)S(1)}, u32[]{:S(2)}, u32[]{:S(2)}) collective-permute-start(f32[1,128,128]{2,1,0:T(8,128)S(1)} %get-tuple-element.43), channel_id=1, source_target_pairs={{0,32},{16,48},{32,64},{48,80},{64,96},{80,112},{96,0},{112,16},{1... | collective-permute-start | bytes 196616 | tf_op jit(solution)/shard_map/ppermute | solution.py:479
  91.0 24.4 %all-to-all-start.4 = ((f32[16,128,128]{2,1,0:T(8,128)}), f32[16,128,128]{2,1,0:T(8,128)S(1)}, u32[]{:S(2)}, u32[]{:S(2)}) async-start(f32[16,128,128]{2,1,0:T(8,128)} %get-tuple-element.28), calls=%async_computation.4 | async-start | bytes 2097152 | tf_op jit(solution)/shard_map/all_to_all | solution.py:487
  98.1 3.3 %collective-permute-start.14 = (f32[144,128]{1,0:T(8,128)S(1)}, f32[144,128]{1,0:T(8,128)S(1)}, u32[]{:S(2)}, u32[]{:S(2)}) collective-permute-start(f32[144,128]{1,0:T(8,128)S(1)} %get-tuple-element.27), channel_id=1, source_target_pairs={{0,96},{16,112},{32,0},{48,16},{64,32},{80,48},{96,64},{112,80},{1... | collective-permute-start | bytes 221192 | tf_op jit(solution)/shard_map/ppermute | solution.py:479
  98.2 4.8 %collective-permute-start.13 = (f32[144,128]{1,0:T(8,128)S(1)}, f32[144,128]{1,0:T(8,128)S(1)}, u32[]{:S(2)}, u32[]{:S(2)}) collective-permute-start(f32[144,128]{1,0:T(8,128)S(1)} %get-tuple-element.27), channel_id=1, source_target_pairs={{0,64},{16,80},{32,96},{48,112},{64,0},{80,16},{96,32},{112,48},{1... | collective-permute-start | bytes 221192 | tf_op jit(solution)/shard_map/ppermute | solution.py:479
  98.8 5.2 %collective-permute-start.12 = (f32[144,128]{1,0:T(8,128)S(1)}, f32[144,128]{1,0:T(8,128)S(1)}, u32[]{:S(2)}, u32[]{:S(2)}) collective-permute-start(f32[144,128]{1,0:T(8,128)S(1)} %get-tuple-element.27), channel_id=1, source_target_pairs={{0,32},{16,48},{32,64},{48,80},{64,96},{80,112},{96,0},{112,16},{1... | collective-permute-start | bytes 221192 | tf_op jit(solution)/shard_map/ppermute | solution.py:479
  104.1 4.2 %collective-permute-start.15 = (f32[4,144,128]{2,1,0:T(8,128)S(1)}, f32[4,144,128]{2,1,0:T(8,128)S(1)}, u32[]{:S(2)}, u32[]{:S(2)}) collective-permute-start(f32[4,144,128]{2,1,0:T(8,128)S(1)} %pad_maximum_fusion.refs_0_), channel_id=1, source_target_pairs={{0,16},{16,0},{32,48},{48,32},{64,80},{80,64},{96,112},{112,96},{1... | collective-permute-start | bytes 884744 | tf_op jit(solution)/shard_map/ppermute | solution.py:483
  115.5 26.6 %all-to-all-start.3 = ((f32[16,144,128]{2,1,0:T(8,128)}), f32[16,144,128]{2,1,0:T(8,128)S(1)}, u32[]{:S(2)}, u32[]{:S(2)}) async-start(f32[16,144,128]{2,1,0:T(8,128)} %forward.4), calls=%async_computation.3 | async-start | bytes 2359296 | tf_op jit(solution)/shard_map/all_to_all | solution.py:487
  133.0 10.9 %collective-permute-start.19 = (f32[1,128,128]{2,1,0:T(8,128)S(1)}, f32[1,128,128]{2,1,0:T(8,128)S(1)}, u32[]{:S(2)}, u32[]{:S(2)}) collective-permute-start(f32[1,128,128]{2,1,0:T(8,128)S(1)} %get-tuple-element.37), channel_id=1, source_target_pairs={{0,96},{16,112},{32,0},{48,16},{64,32},{80,48},{96,64},{112,80},{1... | collective-permute-start | bytes 196616 | tf_op jit(solution)/shard_map/ppermute | solution.py:479
  134.3 9.5 %collective-permute-start.18 = (f32[1,128,128]{2,1,0:T(8,128)S(1)}, f32[1,128,128]{2,1,0:T(8,128)S(1)}, u32[]{:S(2)}, u32[]{:S(2)}) collective-permute-start(f32[1,128,128]{2,1,0:T(8,128)S(1)} %get-tuple-element.38), channel_id=1, source_target_pairs={{0,64},{16,80},{32,96},{48,112},{64,0},{80,16},{96,32},{112,48},{1... | collective-permute-start | bytes 196616 | tf_op jit(solution)/shard_map/ppermute | solution.py:479
  134.7 9.2 %collective-permute-start.17 = (f32[1,128,128]{2,1,0:T(8,128)S(1)}, f32[1,128,128]{2,1,0:T(8,128)S(1)}, u32[]{:S(2)}, u32[]{:S(2)}) collective-permute-start(f32[1,128,128]{2,1,0:T(8,128)S(1)} %get-tuple-element.39), channel_id=1, source_target_pairs={{0,32},{16,48},{32,64},{48,80},{64,96},{80,112},{96,0},{112,16},{1... | collective-permute-start | bytes 196616 | tf_op jit(solution)/shard_map/ppermute | solution.py:479
  145.4 21.3 %all-to-all-start.6 = ((f32[16,128,128]{2,1,0:T(8,128)}), f32[16,128,128]{2,1,0:T(8,128)S(1)}, u32[]{:S(2)}, u32[]{:S(2)}) async-start(f32[16,128,128]{2,1,0:T(8,128)} %get-tuple-element.30), calls=%async_computation.6 | async-start | bytes 2097152 | tf_op jit(solution)/shard_map/all_to_all | solution.py:487
  149.2 3.3 %collective-permute-start.22 = (f32[144,128]{1,0:T(8,128)S(1)}, f32[144,128]{1,0:T(8,128)S(1)}, u32[]{:S(2)}, u32[]{:S(2)}) collective-permute-start(f32[144,128]{1,0:T(8,128)S(1)} %get-tuple-element.29), channel_id=1, source_target_pairs={{0,96},{16,112},{32,0},{48,16},{64,32},{80,48},{96,64},{112,80},{1... | collective-permute-start | bytes 221192 | tf_op jit(solution)/shard_map/ppermute | solution.py:479
  149.6 4.7 %collective-permute-start.21 = (f32[144,128]{1,0:T(8,128)S(1)}, f32[144,128]{1,0:T(8,128)S(1)}, u32[]{:S(2)}, u32[]{:S(2)}) collective-permute-start(f32[144,128]{1,0:T(8,128)S(1)} %get-tuple-element.29), channel_id=1, source_target_pairs={{0,64},{16,80},{32,96},{48,112},{64,0},{80,16},{96,32},{112,48},{1... | collective-permute-start | bytes 221192 | tf_op jit(solution)/shard_map/ppermute | solution.py:479
  150.2 5.2 %collective-permute-start.20 = (f32[144,128]{1,0:T(8,128)S(1)}, f32[144,128]{1,0:T(8,128)S(1)}, u32[]{:S(2)}, u32[]{:S(2)}) collective-permute-start(f32[144,128]{1,0:T(8,128)S(1)} %get-tuple-element.29), channel_id=1, source_target_pairs={{0,32},{16,48},{32,64},{48,80},{64,96},{80,112},{96,0},{112,16},{1... | collective-permute-start | bytes 221192 | tf_op jit(solution)/shard_map/ppermute | solution.py:479
  155.4 4.1 %collective-permute-start.23 = (f32[4,144,128]{2,1,0:T(8,128)S(1)}, f32[4,144,128]{2,1,0:T(8,128)S(1)}, u32[]{:S(2)}, u32[]{:S(2)}) collective-permute-start(f32[4,144,128]{2,1,0:T(8,128)S(1)} %pad_maximum_fusion.1.refs_0_), channel_id=1, source_target_pairs={{0,16},{16,0},{32,48},{48,32},{64,80},{80,64},{96,112},{112,96},{1... | collective-permute-start | bytes 884744 | tf_op jit(solution)/shard_map/ppermute | solution.py:483
  166.7 26.4 %all-to-all-start.5 = ((f32[16,144,128]{2,1,0:T(8,128)}), f32[16,144,128]{2,1,0:T(8,128)S(1)}, u32[]{:S(2)}, u32[]{:S(2)}) async-start(f32[16,144,128]{2,1,0:T(8,128)} %forward.5), calls=%async_computation.5 | async-start | bytes 2359296 | tf_op jit(solution)/shard_map/all_to_all | solution.py:487
  184.0 10.9 %collective-permute-start.27 = (f32[1,128,128]{2,1,0:T(8,128)S(1)}, f32[1,128,128]{2,1,0:T(8,128)S(1)}, u32[]{:S(2)}, u32[]{:S(2)}) collective-permute-start(f32[1,128,128]{2,1,0:T(8,128)S(1)} %get-tuple-element.33), channel_id=1, source_target_pairs={{0,96},{16,112},{32,0},{48,16},{64,32},{80,48},{96,64},{112,80},{1... | collective-permute-start | bytes 196616 | tf_op jit(solution)/shard_map/ppermute | solution.py:479
  185.4 9.5 %collective-permute-start.26 = (f32[1,128,128]{2,1,0:T(8,128)S(1)}, f32[1,128,128]{2,1,0:T(8,128)S(1)}, u32[]{:S(2)}, u32[]{:S(2)}) collective-permute-start(f32[1,128,128]{2,1,0:T(8,128)S(1)} %get-tuple-element.34), channel_id=1, source_target_pairs={{0,64},{16,80},{32,96},{48,112},{64,0},{80,16},{96,32},{112,48},{1... | collective-permute-start | bytes 196616 | tf_op jit(solution)/shard_map/ppermute | solution.py:479
  185.8 9.2 %collective-permute-start.25 = (f32[1,128,128]{2,1,0:T(8,128)S(1)}, f32[1,128,128]{2,1,0:T(8,128)S(1)}, u32[]{:S(2)}, u32[]{:S(2)}) collective-permute-start(f32[1,128,128]{2,1,0:T(8,128)S(1)} %get-tuple-element.35), channel_id=1, source_target_pairs={{0,32},{16,48},{32,64},{48,80},{64,96},{80,112},{96,0},{112,16},{1... | collective-permute-start | bytes 196616 | tf_op jit(solution)/shard_map/ppermute | solution.py:479
  (7 other events, 106.6 us)
